TPU v7x, 32 devices: a whole 2x2x4 slice. The times are simulated.
32 devices in a mesh: grp: 2 (over x), subj: 2 (over core), depth: 8 (over z, y).
Axes of the slice: x: 2, y: 2, z: 4, core: 2. Of those that a mesh axis runs over, the one named last changes fastest.
Arguments:
- template: bfloat16 [2, 4, 512, 4096], P('subj', None, 'depth'), may hold values from -6 to 6
- owner: int32 [4], replicated, may hold values from 0 to 1
- order: int32 [4, 4], P(('grp', 'subj')), parts along dimension 0, may hold values from 0 to 3, each once within a row
- subject: float32 [4, 4, 512, 4096], P(('grp', 'subj'), None, 'depth'), parts along dimension 0, may hold values from -6 to 6
- displacement: float32 [4, 3, 512, 4096], P(('grp', 'subj'), None, 'depth'), parts along dimension 0, may hold values from -3 to 3
Outputs:
- updated: float32 [4, 3, 512, 4096], P(('grp', 'subj'), None, 'depth'), parts along dimension 0
There are 2 independent parts, one for each index of `grp`. A program takes and returns all parts, laid end to end along the dimension named above; an argument that names none is the same for every part. Nothing has to cross between parts.
Inputs may be any that keep to these rules, and one draw needn't show every extreme that they name: owner[k] is the slot of template that holds stain k. Every row of order holds each stain once.
All inputs are finite; a program needn't handle non-finite values.
Results may differ from a plain program's by a relative error of at most 0.0003.
Values may be sent and summed in bfloat16 or wider, within the bound.
No kernel may reach another device: no remote copies, remote signals or barrier semaphores. Data moves between devices by JAX's collectives and lax.ppermute only.
A program may use at most 128 MiB of HBM per device.

v0:
```python
import jax
import jax.numpy as jnp
from jax import lax
from jax.sharding import PartitionSpec as P

GY = 64
SWEEPS = 4


step_size = 1.0
smooth_rate = 0.15
force_floor = 0.5


def from_root(block, axis, owner):
    block = jnp.where(lax.axis_index(axis) == owner, block, jnp.zeros_like(block))
    return lax.psum(block, axis)


def extended_2(block, sides, width):
    for axis, dim in sides:
        count = lax.axis_size(axis)
        forward = [(i, i + 1) for i in range(count - 1)]
        backward = [(target, source) for source, target in forward]
        low = lax.ppermute(
            lax.slice_in_dim(block, block.shape[dim] - width, None, axis=dim), axis, forward
        )
        high = lax.ppermute(lax.slice_in_dim(block, 0, width, axis=dim), axis, backward)
        block = jnp.concatenate([low, block, high], axis=dim)
    return block


def shift_cells(a, offset):
    zeros = jnp.zeros(a.shape[:-1] + (abs(offset),), a.dtype)
    if offset > 0:
        return jnp.concatenate([a[..., offset:], zeros], axis=-1)
    return jnp.concatenate([zeros, a[..., :offset]], axis=-1)


def lateral_parts(a):
    column = jnp.arange(a.shape[-1]) % GY
    x_plus = shift_cells(a, GY)
    x_minus = shift_cells(a, -GY)
    y_plus = jnp.where(column < GY - 1, shift_cells(a, 1), 0.0)
    y_minus = jnp.where(column > 0, shift_cells(a, -1), 0.0)
    return (x_plus, x_minus, y_plus, y_minus)


def gradients(padded):
    centre = padded[..., 1:-1, :]
    x_plus, x_minus, y_plus, y_minus = lateral_parts(centre)
    grad_x = (x_plus - x_minus) * 0.5
    grad_y = (y_plus - y_minus) * 0.5
    grad_z = (padded[..., 2:, :] - padded[..., :-2, :]) * 0.5
    return (grad_x, grad_y, grad_z, centre)


def sweep(padded):
    centre = padded[..., 1:-1, :]
    x_plus, x_minus, y_plus, y_minus = lateral_parts(centre)
    total = padded[..., 2:, :] + padded[..., :-2, :] + x_plus + x_minus + y_plus + y_minus
    return centre + smooth_rate * (total - 6.0 * centre)


def choose_stain(values, picked):
    return jnp.take_along_axis(values, picked[:, None, None, None], axis=1)[:, 0]


def fetch_fixed(source, owner):
    stains = source.shape[1]
    slabs = []
    for k in range(stains):
        slabs.append(from_root(source[0, k], "subj", owner[k]))
    return jnp.stack(slabs, 0).astype(jnp.float32)


def apply_force(padded, fixed, u, order):
    grad_x, grad_y, grad_z, centre = gradients(padded)
    for j in range(order.shape[1]):
        picked = order[:, j]
        gx = choose_stain(grad_x, picked)
        gy = choose_stain(grad_y, picked)
        gz = choose_stain(grad_z, picked)
        moving = choose_stain(centre, picked)
        target = jnp.take(fixed, picked, axis=0)
        diff = target - (moving + gx * u[:, 0] + gy * u[:, 1] + gz * u[:, 2])
        denom = gx * gx + gy * gy + gz * gz + diff * diff + force_floor
        u = u + step_size * diff[:, None] * jnp.stack([gx, gy, gz], 1) / denom[:, None]
    return u


def local(template, owner, order, subject, displacement):
    fixed = fetch_fixed(template, owner)
    padded = extended_2(subject, (("depth", 2),), 1)
    u = apply_force(padded, fixed, displacement, order)
    for i in range(SWEEPS):
        extended = extended_2(u, (("depth", 2),), 1)
        u = sweep(extended)
    return u


def solution(mesh):
    placed = (
        P("subj", None, "depth", None),
        P(),
        P(("grp", "subj"), None),
        P(("grp", "subj"), None, "depth", None),
        P(("grp", "subj"), None, "depth", None),
    )
    return jax.shard_map(
        local,
        mesh=mesh,
        in_specs=placed,
        out_specs=P(("grp", "subj"), None, "depth", None),
        check_vma=False,
    )
```

profile of v0, /device:TPU:12, one launch (start us, length us, event | category | flops | bytes accessed | tf_op | source)
XLA Modules:
  0.0 154.7 jit_solution(9540911621715314486)
XLA Ops:
  6.5 0.0 all-reduce.23.cloned.1.call-start
  6.5 1.3 fusion.75
  7.8 2.4 %collective-permute-start = (f32[1,4,1,4096]{3,2,1,0:T(1,128)S(1)}, f32[1,4,1,4096]{3,2,1,0:T(1,128)S(1)}, u32[]{:S(2)}, u32[]{:S(2)}) collective-permute-start(f32[1,4,1,4096]{3,2,1,0:T(1,128)S(1)} %get-tuple-element.53), channel_id=1, source_target_pairs={{1,0},{2,1},{3,2},{4,3},{5,4},{6,5},{7,6},{9,8},{10,9},{11,10},{12... | collective-permute-start | bytes 196616 | tf_op jit(solution)/shard_map/ppermute | solution.py:28
  10.3 4.3 %collective-permute-start.1 = (f32[1,4,1,4096]{3,2,1,0:T(1,128)S(1)}, f32[1,4,1,4096]{3,2,1,0:T(1,128)S(1)}, u32[]{:S(2)}, u32[]{:S(2)}) collective-permute-start(f32[1,4,1,4096]{3,2,1,0:T(1,128)S(1)} %get-tuple-element.54), channel_id=1, source_target_pairs={{0,1},{1,2},{2,3},{3,4},{4,5},{5,6},{6,7},{8,9},{9,10},{10,11},{11... | collective-permute-start | bytes 196616 | tf_op jit(solution)/shard_map/ppermute | solution.py:25
  14.6 1.5 fusion.91
  18.5 2.9 %select_bitcast_fusion.3 = (bf16[1,64,4096]{2,1,0:T(8,128)(2,1)}, bf16[1,64,4096]{2,1,0:T(8,128)(2,1)}, bf16[1,64,4096]{2,1,0:T(8,128)(2,1)}, bf16[1,64,4096]{2,1,0:T(8,128)(2,1)}) fusion(bf16[1,4,64,4096]{3,2,1,0:T(8,128)(2,1)} %param.9, pred[]{:T(512)S(6)} %eq.18, pred[]{:T(512)S(6)} %eq.19, pred[]{:T(512)S(6)} %eq.21, pred[]{:T(512)S(6)} %eq.20), kind=kLoop, calls=%fused_computation.114 | loop fusion | flops 1048576 | bytes 4194308 | tf_op jit(solution)/shard_map/stack | solution.py:74
  21.4 0.0 all-reduce.23.cloned.1.call-update
  21.5 0.0 copy-start
  21.5 5.2 %fusion.76 = (f32[1,4,64,4095]{3,2,1,0:T(8,128)S(1)}, f32[1,4,64,4095]{3,2,1,0:T(8,128)S(1)}) fusion(f32[1,4,64,4096]{3,2,1,0:T(8,128)} %param.12), kind=kLoop, calls=%fused_computation.123 | loop fusion | bytes 16773120 | tf_op jit(solution)/shard_map/slice | solution.py:36
  26.7 0.0 copy-done
  26.7 1.6 %fusion.77 = (f32[1,4,64,4032]{3,2,1,0:T(8,128)S(1)}, f32[1,4,64,4032]{3,2,1,0:T(8,128)S(1)}) fusion(f32[1,4,64,4096]{3,2,1,0:T(8,128)S(1)} %copy-done), kind=kLoop, calls=%fused_computation.124 | loop fusion | bytes 16515072 | tf_op jit(solution)/shard_map/slice | solution.py:36
  28.2 3.2 %subtract_multiply_fusion.1 = f32[1,4,64,4096]{3,2,1,0:T(8,128)} fusion(f32[1,4,64,4032]{3,2,1,0:T(8,128)S(1)} %get-tuple-element.58, f32[1,4,64,4032]{3,2,1,0:T(8,128)S(1)} %get-tuple-element.57), kind=kLoop, calls=%fused_computation.5 | loop fusion | flops 2097152 | bytes 12451840 | tf_op jit(solution)/shard_map/mul | solution.py:52
  31.4 3.1 %subtract_multiply_fusion = f32[1,4,64,4096]{3,2,1,0:T(8,128)} fusion(f32[1,4,64,4095]{3,2,1,0:T(8,128)S(1)} %get-tuple-element.56, f32[1,4,64,4095]{3,2,1,0:T(8,128)S(1)} %get-tuple-element.55, pred[4096]{0:T(1024)(128)(4,1)S(1)} %get-tuple-element.95, pred[4096]{0:T(1024)(128)(4,1)S(1)} %get-tuple-element.96), kind=kLoop, calls=%fused_computation.4 | loop fusion | flops 4194304 | bytes 12589056 | tf_op jit(solution)/shard_map/mul | solution.py:53
  34.5 0.7 fusion.90
  50.2 0.0 collective-permute-done
  50.2 0.0 collective-permute-done.1
  50.2 0.0 copy-start.2
  50.2 2.9 %fusion.1 = f32[1,4,64,4096]{3,2,1,0:T(8,128)} fusion(f32[1,4,64,4096]{3,2,1,0:T(8,128)S(1)} %copy-done, f32[1,4,1,4096]{3,2,1,0:T(1,128)S(1)} %collective-permute-done.1, f32[1,4,1,4096]{3,2,1,0:T(1,128)S(1)} %collective-permute-done), kind=kLoop, calls=%fused_computation.2 | loop fusion | flops 4194304 | bytes 8519680 | tf_op jit(solution)/shard_map/mul | solution.py:54
  53.2 2.0 %maximum_convert_fusion = f32[4,64,4096]{2,1,0:T(8,128)S(1)} fusion(bf16[1,64,4096]{2,1,0:T(8,128)(2,1)} %get-tuple-element.29, bf16[1,64,4096]{2,1,0:T(8,128)(2,1)} %get-tuple-element.30, bf16[1,64,4096]{2,1,0:T(8,128)(2,1)} %get-tuple-element.31, bf16[1,64,4096]{2,1,0:T(8,128)(2,1)} %get-tuple-element.32), kind=kLoop, calls=%fused_computation.58 | loop fusion | flops 4194304 | bytes 6291456 | tf_op jit(solution)/shard_map/convert_element_type | solution.py:74
  55.2 0.8 copy-done.1
  56.0 2.8 %fusion.64 = (f32[64,4096]{1,0:T(8,128)S(1)}, f32[1,64,4096]{2,1,0:T(8,128)S(1)}, f32[1,1,64,4096]{3,2,1,0:T(8,128)S(1)}, f32[1,1,64,4096]{3,2,1,0:T(8,128)S(1)}, f32[1,1,64,4096]{3,2,1,0:T(8,128)S(1)}) fusion(f32[1,3,64,4096]{3,2,1,0:T(8,128)S(1)} %copy-done.2, f32[1,4,64,4096]{3,2,1,0:T(8,128)S(1)} %copy-done.1, s32[]{:T(128)} %bitcast.13, pred[]{:T(512)} %bitcast.12, ...), kind=kLoop, calls=%fused_computation.94 | loop fusion | flops 5242880 | bytes 13631498 | tf_op jit(solution)/shard_map/div | solution.py:88
  58.8 0.0 copy-start.3
  58.8 0.0 copy-start.4
  58.8 2.2 %fusion.35 = f32[1,3,64,4096]{3,2,1,0:T(8,128)} fusion(f32[1,3,64,4096]{3,2,1,0:T(8,128)S(1)} %copy-done.2, f32[1,1,64,4096]{3,2,1,0:T(8,128)S(1)} %get-tuple-element.52, f32[1,1,64,4096]{3,2,1,0:T(8,128)S(1)} %get-tuple-element.51, f32[1,1,64,4096]{3,2,1,0:T(8,128)S(1)} %get-tuple-element.50, f32[64,4096]{1,0:T(8,128)S(1)} %get-tuple-element.48, ...), kind=kLoop, calls=%fused_computation.48 | loop fusion | flops 3932160 | bytes 11534336 | tf_op jit(solution)/shard_map/add | solution.py:88
  61.1 1.1 copy-done.3
  62.1 1.3 copy-done.4
  63.4 4.4 %fusion.62 = (f32[64,4096]{1,0:T(8,128)S(1)}, f32[1,64,4096]{2,1,0:T(8,128)S(1)}, f32[1,1,64,4096]{3,2,1,0:T(8,128)S(1)}, f32[1,1,64,4096]{3,2,1,0:T(8,128)}, f32[1,1,64,4096]{3,2,1,0:T(8,128)}) fusion(f32[1,3,64,4096]{3,2,1,0:T(8,128)} %fusion.35, f32[1,4,64,4096]{3,2,1,0:T(8,128)S(1)} %copy-done.1, s32[]{:T(128)} %bitcast.23, pred[]{:T(512)} %bitcast.22, ...), kind=kLoop, calls=%fused_computation.91 | loop fusion | flops 5242880 | bytes 13631498 | tf_op jit(solution)/shard_map/div | solution.py:88
  67.8 4.4 %fusion.37 = f32[1,3,64,4096]{3,2,1,0:T(8,128)} fusion(f32[1,1,64,4096]{3,2,1,0:T(8,128)} %get-tuple-element.47, f32[1,1,64,4096]{3,2,1,0:T(8,128)} %get-tuple-element.46, f32[1,1,64,4096]{3,2,1,0:T(8,128)S(1)} %get-tuple-element.45, f32[64,4096]{1,0:T(8,128)S(1)} %get-tuple-element.43, f32[64,4096]{1,0:T(8,128)S(1)} %bitcast.94, ...), kind=kLoop, calls=%fused_computation.51 | loop fusion | flops 7864320 | bytes 16777216 | tf_op jit(solution)/shard_map/add | solution.py:88
  72.2 5.1 %fusion.60 = (f32[64,4096]{1,0:T(8,128)}, f32[1,64,4096]{2,1,0:T(8,128)}, f32[1,1,64,4096]{3,2,1,0:T(8,128)}, f32[1,1,64,4096]{3,2,1,0:T(8,128)}, f32[1,1,64,4096]{3,2,1,0:T(8,128)}) fusion(f32[1,3,64,4096]{3,2,1,0:T(8,128)} %fusion.37, f32[1,4,64,4096]{3,2,1,0:T(8,128)S(1)} %copy-done.1, s32[]{:T(128)} %bitcast.33, pred[]{:T(512)} %bitcast.32, ...), kind=kLoop, calls=%fused_computation.88 | loop fusion | flops 5242880 | bytes 13631498 | tf_op jit(solution)/shard_map/div | solution.py:88
  77.3 5.1 %fusion.39 = f32[1,3,64,4096]{3,2,1,0:T(8,128)} fusion(f32[1,1,64,4096]{3,2,1,0:T(8,128)} %get-tuple-element.42, f32[1,1,64,4096]{3,2,1,0:T(8,128)} %get-tuple-element.41, f32[1,1,64,4096]{3,2,1,0:T(8,128)} %get-tuple-element.40, f32[64,4096]{1,0:T(8,128)} %get-tuple-element.38, f32[64,4096]{1,0:T(8,128)} %bitcast.97, f32[64,4096]{1,0:T(8,128)S(1)} %get-tuple-element.43, ...), kind=kLoop, calls=%fused_computation.54 | loop fusion | flops 11796480 | bytes 22020096 | tf_op jit(solution)/shard_map/add | solution.py:88
  82.4 5.1 %fusion.58 = (f32[64,4096]{1,0:T(8,128)}, f32[1,64,4096]{2,1,0:T(8,128)}, f32[1,1,64,4096]{3,2,1,0:T(8,128)}, f32[1,1,64,4096]{3,2,1,0:T(8,128)}, f32[1,1,64,4096]{3,2,1,0:T(8,128)}) fusion(f32[1,3,64,4096]{3,2,1,0:T(8,128)} %fusion.39, f32[1,4,64,4096]{3,2,1,0:T(8,128)S(1)} %copy-done.1, s32[]{:T(128)} %bitcast.43, pred[]{:T(512)} %bitcast.42, ...), kind=kLoop, calls=%fused_computation.85 | loop fusion | flops 5242880 | bytes 13631498 | tf_op jit(solution)/shard_map/div | solution.py:88
  87.5 6.4 %fusion.41 = f32[1,3,64,4096]{3,2,1,0:T(8,128)S(1)} fusion(f32[1,1,64,4096]{3,2,1,0:T(8,128)} %get-tuple-element.37, f32[1,1,64,4096]{3,2,1,0:T(8,128)} %get-tuple-element.36, f32[1,1,64,4096]{3,2,1,0:T(8,128)} %get-tuple-element.35, f32[64,4096]{1,0:T(8,128)} %get-tuple-element.33, f32[64,4096]{1,0:T(8,128)} %bitcast.99, f32[64,4096]{1,0:T(8,128)} %get-tuple-element.38, ...), kind=kLoop, calls=%fused_computation.57 | loop fusion | flops 15728640 | bytes 27262976 | tf_op jit(solution)/shard_map/add | solution.py:88
  94.0 0.1 fusion.89
  94.1 1.1 fusion.88
  95.2 1.9 %collective-permute-start.2 = (f32[1,3,1,4096]{3,2,1,0:T(1,128)S(1)}, f32[1,3,1,4096]{3,2,1,0:T(1,128)S(1)}, u32[]{:S(2)}, u32[]{:S(2)}) collective-permute-start(f32[1,3,1,4096]{3,2,1,0:T(1,128)S(1)} %get-tuple-element.81), channel_id=1, source_target_pairs={{1,0},{2,1},{3,2},{4,3},{5,4},{6,5},{7,6},{9,8},{10,9},{11,10},{12... | collective-permute-start | bytes 147464 | tf_op jit(solution)/shard_map/ppermute | solution.py:28
  97.1 4.8 %collective-permute-start.3 = (f32[1,3,1,4096]{3,2,1,0:T(1,128)S(1)}, f32[1,3,1,4096]{3,2,1,0:T(1,128)S(1)}, u32[]{:S(2)}, u32[]{:S(2)}) collective-permute-start(f32[1,3,1,4096]{3,2,1,0:T(1,128)S(1)} %get-tuple-element.82), channel_id=1, source_target_pairs={{0,1},{1,2},{2,3},{3,4},{4,5},{5,6},{6,7},{8,9},{9,10},{10,11},{11... | collective-permute-start | bytes 147464 | tf_op jit(solution)/shard_map/ppermute | solution.py:25
  101.9 1.1 fusion.87
  103.1 0.0 collective-permute-done.2
  103.1 0.6 collective-permute-done.3
  103.7 2.9 %fusion.33 = f32[1,3,64,4096]{3,2,1,0:T(8,128)S(1)} fusion(f32[1,3,64,4096]{3,2,1,0:T(8,128)S(1)} %fusion.41, f32[1,3,1,4096]{3,2,1,0:T(1,128)S(1)} %collective-permute-done.3, f32[1,3,1,4096]{3,2,1,0:T(1,128)S(1)} %collective-permute-done.2, f32[1,3,64,4095]{3,2,1,0:T(8,128)S(1)} %get-tuple-element.80, f32[1,3,64,4095]{3,2,1,0:T(8,128)S(1)} %get-tuple-element.79, ...), kind=kLoop, calls=%fused_computation.44 | loop fusion | flops 10223616 | bytes 18881024 | tf_op jit(solution)/shard_map/add | solution.py:62
  106.6 0.1 fusion.86
  106.7 1.1 fusion.85
  107.8 4.1 %collective-permute-start.4 = (f32[1,3,1,4096]{3,2,1,0:T(1,128)S(1)}, f32[1,3,1,4096]{3,2,1,0:T(1,128)S(1)}, u32[]{:S(2)}, u32[]{:S(2)}) collective-permute-start(f32[1,3,1,4096]{3,2,1,0:T(1,128)S(1)} %get-tuple-element.75), channel_id=1, source_target_pairs={{1,0},{2,1},{3,2},{4,3},{5,4},{6,5},{7,6},{9,8},{10,9},{11,10},{12... | collective-permute-start | bytes 147464 | tf_op jit(solution)/shard_map/ppermute | solution.py:28
  111.9 2.9 %collective-permute-start.5 = (f32[1,3,1,4096]{3,2,1,0:T(1,128)S(1)}, f32[1,3,1,4096]{3,2,1,0:T(1,128)S(1)}, u32[]{:S(2)}, u32[]{:S(2)}) collective-permute-start(f32[1,3,1,4096]{3,2,1,0:T(1,128)S(1)} %get-tuple-element.76), channel_id=1, source_target_pairs={{0,1},{1,2},{2,3},{3,4},{4,5},{5,6},{6,7},{8,9},{9,10},{10,11},{11... | collective-permute-start | bytes 147464 | tf_op jit(solution)/shard_map/ppermute | solution.py:25
  114.9 1.1 fusion.84
  116.0 0.0 collective-permute-done.4
  116.1 1.9 %collective-permute-done.5 = f32[1,3,1,4096]{3,2,1,0:T(1,128)S(1)} collective-permute-done((f32[1,3,1,4096]{3,2,1,0:T(1,128)S(1)}, f32[1,3,1,4096]{3,2,1,0:T(1,128)S(1)}, u32[]{:S(2)}, u32[]{:S(2)}) %collective-permute-start.5) | collective-permute-done | bytes 49184 | tf_op jit(solution)/shard_map/ppermute | solution.py:25
  117.9 2.9 %fusion.25 = f32[1,3,64,4096]{3,2,1,0:T(8,128)S(1)} fusion(f32[1,3,64,4096]{3,2,1,0:T(8,128)S(1)} %fusion.33, f32[1,3,1,4096]{3,2,1,0:T(1,128)S(1)} %collective-permute-done.5, f32[1,3,1,4096]{3,2,1,0:T(1,128)S(1)} %collective-permute-done.4, f32[1,3,64,4095]{3,2,1,0:T(8,128)S(1)} %get-tuple-element.74, f32[1,3,64,4095]{3,2,1,0:T(8,128)S(1)} %get-tuple-element.73, ...), kind=kLoop, calls=%fused_computation.34 | loop fusion | flops 10223616 | bytes 18881024 | tf_op jit(solution)/shard_map/add | solution.py:62
  120.8 0.1 fusion.83
  120.9 1.1 fusion.82
  122.1 2.8 %collective-permute-start.6 = (f32[1,3,1,4096]{3,2,1,0:T(1,128)S(1)}, f32[1,3,1,4096]{3,2,1,0:T(1,128)S(1)}, u32[]{:S(2)}, u32[]{:S(2)}) collective-permute-start(f32[1,3,1,4096]{3,2,1,0:T(1,128)S(1)} %get-tuple-element.69), channel_id=1, source_target_pairs={{1,0},{2,1},{3,2},{4,3},{5,4},{6,5},{7,6},{9,8},{10,9},{11,10},{12... | collective-permute-start | bytes 147464 | tf_op jit(solution)/shard_map/ppermute | solution.py:28
  124.9 3.9 %collective-permute-start.7 = (f32[1,3,1,4096]{3,2,1,0:T(1,128)S(1)}, f32[1,3,1,4096]{3,2,1,0:T(1,128)S(1)}, u32[]{:S(2)}, u32[]{:S(2)}) collective-permute-start(f32[1,3,1,4096]{3,2,1,0:T(1,128)S(1)} %get-tuple-element.70), channel_id=1, source_target_pairs={{0,1},{1,2},{2,3},{3,4},{4,5},{5,6},{6,7},{8,9},{9,10},{10,11},{11... | collective-permute-start | bytes 147464 | tf_op jit(solution)/shard_map/ppermute | solution.py:25
  128.8 1.1 fusion.81
  130.0 0.0 collective-permute-done.6
  130.0 0.9 collective-permute-done.7
  130.9 2.9 %fusion.17 = f32[1,3,64,4096]{3,2,1,0:T(8,128)S(1)} fusion(f32[1,3,64,4096]{3,2,1,0:T(8,128)S(1)} %fusion.25, f32[1,3,1,4096]{3,2,1,0:T(1,128)S(1)} %collective-permute-done.7, f32[1,3,1,4096]{3,2,1,0:T(1,128)S(1)} %collective-permute-done.6, f32[1,3,64,4095]{3,2,1,0:T(8,128)S(1)} %get-tuple-element.68, f32[1,3,64,4095]{3,2,1,0:T(8,128)S(1)} %get-tuple-element.67, ...), kind=kLoop, calls=%fused_computation.24 | loop fusion | flops 10223616 | bytes 18881024 | tf_op jit(solution)/shard_map/add | solution.py:62
  133.8 0.1 fusion.80
  133.8 1.1 fusion.79
  135.0 2.8 %collective-permute-start.8 = (f32[1,3,1,4096]{3,2,1,0:T(1,128)S(1)}, f32[1,3,1,4096]{3,2,1,0:T(1,128)S(1)}, u32[]{:S(2)}, u32[]{:S(2)}) collective-permute-start(f32[1,3,1,4096]{3,2,1,0:T(1,128)S(1)} %get-tuple-element.63), channel_id=1, source_target_pairs={{1,0},{2,1},{3,2},{4,3},{5,4},{6,5},{7,6},{9,8},{10,9},{11,10},{12... | collective-permute-start | bytes 147464 | tf_op jit(solution)/shard_map/ppermute | solution.py:28
  137.8 3.9 %collective-permute-start.9 = (f32[1,3,1,4096]{3,2,1,0:T(1,128)S(1)}, f32[1,3,1,4096]{3,2,1,0:T(1,128)S(1)}, u32[]{:S(2)}, u32[]{:S(2)}) collective-permute-start(f32[1,3,1,4096]{3,2,1,0:T(1,128)S(1)} %get-tuple-element.64), channel_id=1, source_target_pairs={{0,1},{1,2},{2,3},{3,4},{4,5},{5,6},{6,7},{8,9},{9,10},{10,11},{11... | collective-permute-start | bytes 147464 | tf_op jit(solution)/shard_map/ppermute | solution.py:25
  141.8 1.1 fusion.78
  142.9 0.0 collective-permute-done.8
  142.9 0.9 collective-permute-done.9
  143.8 4.0 %fusion.9 = f32[1,3,64,4096]{3,2,1,0:T(8,128)} fusion(f32[1,3,64,4096]{3,2,1,0:T(8,128)S(1)} %fusion.17, f32[1,3,1,4096]{3,2,1,0:T(1,128)S(1)} %collective-permute-done.9, f32[1,3,1,4096]{3,2,1,0:T(1,128)S(1)} %collective-permute-done.8, f32[1,3,64,4095]{3,2,1,0:T(8,128)S(1)} %get-tuple-element.62, f32[1,3,64,4095]{3,2,1,0:T(8,128)S(1)} %get-tuple-element.61, ...), kind=kLoop, calls=%fused_computation.14 | loop fusion | flops 10223616 | bytes 18881024 | tf_op jit(solution)/shard_map/add | solution.py:62
  (12 shorter events, 0.0 us)
Async XLA Ops:
  6.5 46.6 %all-reduce.23.cloned.1.call-start = ((), (), s32[]{:S(2)}) async-start(), calls=%async_computation | async-start | bytes 4194304 | tf_op jit(solution)/shard_map/psum | solution.py:17
  7.8 42.3 %collective-permute-start = (f32[1,4,1,4096]{3,2,1,0:T(1,128)S(1)}, f32[1,4,1,4096]{3,2,1,0:T(1,128)S(1)}, u32[]{:S(2)}, u32[]{:S(2)}) collective-permute-start(f32[1,4,1,4096]{3,2,1,0:T(1,128)S(1)} %get-tuple-element.53), channel_id=1, source_target_pairs={{1,0},{2,1},{3,2},{4,3},{5,4},{6,5},{7,6},{9,8},{10,9},{11,10},{12... | collective-permute-start | bytes 196616 | tf_op jit(solution)/shard_map/ppermute | solution.py:28
  10.3 39.9 %collective-permute-start.1 = (f32[1,4,1,4096]{3,2,1,0:T(1,128)S(1)}, f32[1,4,1,4096]{3,2,1,0:T(1,128)S(1)}, u32[]{:S(2)}, u32[]{:S(2)}) collective-permute-start(f32[1,4,1,4096]{3,2,1,0:T(1,128)S(1)} %get-tuple-element.54), channel_id=1, source_target_pairs={{0,1},{1,2},{2,3},{3,4},{4,5},{5,6},{6,7},{8,9},{9,10},{10,11},{11... | collective-permute-start | bytes 196616 | tf_op jit(solution)/shard_map/ppermute | solution.py:25
  21.5 5.2 %copy-start = (f32[1,4,64,4096]{3,2,1,0:T(8,128)S(1)}, f32[1,4,64,4096]{3,2,1,0:T(8,128)}, u32[]{:S(2)}) copy-start(f32[1,4,64,4096]{3,2,1,0:T(8,128)} %param.12) | copy-start | bytes 12582916
  31.4 3.1 %copy-start.8 = (s32[1,4]{1,0:T(1,128)S(1)}, s32[1,4]{1,0:T(1,128)}, u32[]{:S(2)}) copy-start(s32[1,4]{1,0:T(1,128)} %param.11) | copy-start | bytes 52
  50.2 5.0 %copy-start.2 = (f32[1,3,64,4096]{3,2,1,0:T(8,128)S(1)}, f32[1,3,64,4096]{3,2,1,0:T(8,128)}, u32[]{:S(2)}) copy-start(f32[1,3,64,4096]{3,2,1,0:T(8,128)} %param.13) | copy-start | bytes 9437188
  53.2 2.8 %copy-start.1 = (f32[1,4,64,4096]{3,2,1,0:T(8,128)S(1)}, f32[1,4,64,4096]{3,2,1,0:T(8,128)}, u32[]{:S(2)}) copy-start(f32[1,4,64,4096]{3,2,1,0:T(8,128)} %param.12) | copy-start | bytes 12582916
  58.8 3.3 %copy-start.3 = (f32[1,4,64,4096]{3,2,1,0:T(8,128)S(1)}, f32[1,4,64,4096]{3,2,1,0:T(8,128)}, u32[]{:S(2)}) copy-start(f32[1,4,64,4096]{3,2,1,0:T(8,128)} %subtract_multiply_fusion.1) | copy-start | bytes 12582916
  58.8 4.6 %copy-start.4 = (f32[1,4,64,4096]{3,2,1,0:T(8,128)S(1)}, f32[1,4,64,4096]{3,2,1,0:T(8,128)}, u32[]{:S(2)}) copy-start(f32[1,4,64,4096]{3,2,1,0:T(8,128)} %fusion.1) | copy-start | bytes 12582916
  67.8 9.5 %copy-start.5 = (f32[64,4096]{1,0:T(8,128)}, f32[64,4096]{1,0:T(8,128)S(1)}, u32[]{:S(2)}) copy-start(f32[64,4096]{1,0:T(8,128)S(1)} %get-tuple-element.43) | copy-start | bytes 3145732
  67.8 9.5 %copy-start.6 = (f32[1,64,4096]{2,1,0:T(8,128)}, f32[1,64,4096]{2,1,0:T(8,128)S(1)}, u32[]{:S(2)}) copy-start(f32[1,64,4096]{2,1,0:T(8,128)S(1)} %get-tuple-element.44) | copy-start | bytes 3145732
  67.8 9.5 %copy-start.7 = (f32[1,1,64,4096]{3,2,1,0:T(8,128)}, f32[1,1,64,4096]{3,2,1,0:T(8,128)S(1)}, u32[]{:S(2)}) copy-start(f32[1,1,64,4096]{3,2,1,0:T(8,128)S(1)} %get-tuple-element.45) | copy-start | bytes 3145732
  95.2 7.9 %collective-permute-start.2 = (f32[1,3,1,4096]{3,2,1,0:T(1,128)S(1)}, f32[1,3,1,4096]{3,2,1,0:T(1,128)S(1)}, u32[]{:S(2)}, u32[]{:S(2)}) collective-permute-start(f32[1,3,1,4096]{3,2,1,0:T(1,128)S(1)} %get-tuple-element.81), channel_id=1, source_target_pairs={{1,0},{2,1},{3,2},{4,3},{5,4},{6,5},{7,6},{9,8},{10,9},{11,10},{12... | collective-permute-start | bytes 147464 | tf_op jit(solution)/shard_map/ppermute | solution.py:28
  97.1 6.6 %collective-permute-start.3 = (f32[1,3,1,4096]{3,2,1,0:T(1,128)S(1)}, f32[1,3,1,4096]{3,2,1,0:T(1,128)S(1)}, u32[]{:S(2)}, u32[]{:S(2)}) collective-permute-start(f32[1,3,1,4096]{3,2,1,0:T(1,128)S(1)} %get-tuple-element.82), channel_id=1, source_target_pairs={{0,1},{1,2},{2,3},{3,4},{4,5},{5,6},{6,7},{8,9},{9,10},{10,11},{11... | collective-permute-start | bytes 147464 | tf_op jit(solution)/shard_map/ppermute | solution.py:25
  107.8 8.2 %collective-permute-start.4 = (f32[1,3,1,4096]{3,2,1,0:T(1,128)S(1)}, f32[1,3,1,4096]{3,2,1,0:T(1,128)S(1)}, u32[]{:S(2)}, u32[]{:S(2)}) collective-permute-start(f32[1,3,1,4096]{3,2,1,0:T(1,128)S(1)} %get-tuple-element.75), channel_id=1, source_target_pairs={{1,0},{2,1},{3,2},{4,3},{5,4},{6,5},{7,6},{9,8},{10,9},{11,10},{12... | collective-permute-start | bytes 147464 | tf_op jit(solution)/shard_map/ppermute | solution.py:28
  111.9 6.0 %collective-permute-start.5 = (f32[1,3,1,4096]{3,2,1,0:T(1,128)S(1)}, f32[1,3,1,4096]{3,2,1,0:T(1,128)S(1)}, u32[]{:S(2)}, u32[]{:S(2)}) collective-permute-start(f32[1,3,1,4096]{3,2,1,0:T(1,128)S(1)} %get-tuple-element.76), channel_id=1, source_target_pairs={{0,1},{1,2},{2,3},{3,4},{4,5},{5,6},{6,7},{8,9},{9,10},{10,11},{11... | collective-permute-start | bytes 147464 | tf_op jit(solution)/shard_map/ppermute | solution.py:25
  122.1 7.9 %collective-permute-start.6 = (f32[1,3,1,4096]{3,2,1,0:T(1,128)S(1)}, f32[1,3,1,4096]{3,2,1,0:T(1,128)S(1)}, u32[]{:S(2)}, u32[]{:S(2)}) collective-permute-start(f32[1,3,1,4096]{3,2,1,0:T(1,128)S(1)} %get-tuple-element.69), channel_id=1, source_target_pairs={{1,0},{2,1},{3,2},{4,3},{5,4},{6,5},{7,6},{9,8},{10,9},{11,10},{12... | collective-permute-start | bytes 147464 | tf_op jit(solution)/shard_map/ppermute | solution.py:28
  124.9 6.0 %collective-permute-start.7 = (f32[1,3,1,4096]{3,2,1,0:T(1,128)S(1)}, f32[1,3,1,4096]{3,2,1,0:T(1,128)S(1)}, u32[]{:S(2)}, u32[]{:S(2)}) collective-permute-start(f32[1,3,1,4096]{3,2,1,0:T(1,128)S(1)} %get-tuple-element.70), channel_id=1, source_target_pairs={{0,1},{1,2},{2,3},{3,4},{4,5},{5,6},{6,7},{8,9},{9,10},{10,11},{11... | collective-permute-start | bytes 147464 | tf_op jit(solution)/shard_map/ppermute | solution.py:25
  135.0 7.9 %collective-permute-start.8 = (f32[1,3,1,4096]{3,2,1,0:T(1,128)S(1)}, f32[1,3,1,4096]{3,2,1,0:T(1,128)S(1)}, u32[]{:S(2)}, u32[]{:S(2)}) collective-permute-start(f32[1,3,1,4096]{3,2,1,0:T(1,128)S(1)} %get-tuple-element.63), channel_id=1, source_target_pairs={{1,0},{2,1},{3,2},{4,3},{5,4},{6,5},{7,6},{9,8},{10,9},{11,10},{12... | collective-permute-start | bytes 147464 | tf_op jit(solution)/shard_map/ppermute | solution.py:28
  137.8 6.0 %collective-permute-start.9 = (f32[1,3,1,4096]{3,2,1,0:T(1,128)S(1)}, f32[1,3,1,4096]{3,2,1,0:T(1,128)S(1)}, u32[]{:S(2)}, u32[]{:S(2)}) collective-permute-start(f32[1,3,1,4096]{3,2,1,0:T(1,128)S(1)} %get-tuple-element.64), channel_id=1, source_target_pairs={{0,1},{1,2},{2,3},{3,4},{4,5},{5,6},{6,7},{8,9},{9,10},{10,11},{11... | collective-permute-start | bytes 147464 | tf_op jit(solution)/shard_map/ppermute | solution.py:25
Sparse Core Ops, SparseCore 0:
  21.6 21.7 all-reduce.22
where the time goes:
time: 157 us; the launch traced here: 155 us
  other arithmetic  62.5 us (40%)
  starting transfers between devices  34 us (22%)
  between operations  31.2 us (20%)
  local copies, waits for them, and re-layouts  22.7 us (14%)
  waiting for transfers between devices  4.26 us (3%)
    ppermute x5, starting transfers between devices, extended_2(): lax.ppermute(lax.slice_in_dim(block, block.shape[dim] - width, None, axis...  19.9 us
    add x4, other arithmetic, apply_force(): u + step_size * diff[:, None] * jnp.stack([gx, gy, gz], 1) / denom[:, None]  18.2 us
    div x4, other arithmetic, apply_force(): step_size * diff[:, None] * jnp.stack([gx, gy, gz], 1) / denom[:, None]  17.4 us
    slice x10, local copies, waits for them, and re-layouts, shift_cells(): return jnp.concatenate([a[..., offset:], zeros], axis=-1)  15.8 us
    ppermute x5, starting transfers between devices, extended_2(): lax.ppermute(lax.slice_in_dim(block, 0, width, axis=dim), axis, backward)  14.1 us
    add x4, other arithmetic, sweep(): return centre + smooth_rate * (total - 6.0 * centre)  12.7 us
    ppermute x5, waiting for transfers between devices, extended_2(): lax.ppermute(lax.slice_in_dim(block, block.shape[dim] - width, None, axis...  4.23 us
    mul x1, other arithmetic, gradients(): grad_x = (x_plus - x_minus) * 0.5  3.18 us
  transfers between devices with their start and end apart: 11, of which 4 were waited for; matrix products, arithmetic and copies ran while one was open for 17% of the time, Pallas kernels for 0%

commit v1 on v0

v1 whole, which is shorter than its diff:
```python
import functools

import jax
import jax.numpy as jnp
from jax import lax
from jax.experimental import pallas as pl
from jax.experimental.pallas import tpu as pltpu
from jax.sharding import PartitionSpec as P

GY = 64
SWEEPS = 4
LANES = 128
RATE = 0.15
F32 = jnp.float32
BF16 = jnp.bfloat16
EDGE = 16

ANY = pl.BlockSpec(memory_space=pl.ANY)
VMEM = pl.BlockSpec(memory_space=pltpu.VMEM)
SMEM = pl.BlockSpec(memory_space=pltpu.SMEM)


def params():
    return pltpu.CompilerParams(vmem_limit_bytes=48 << 20)


def pair_swaps(count):
    def swaps(first):
        return [p for i in range(first, count - 1, 2) for p in ((i, i + 1), (i + 1, i))]

    return swaps(0), swaps(1)


def lateral_matrix(difference):
    row = lax.broadcasted_iota(jnp.int32, (2 * LANES, 2 * LANES), 0) & (LANES - 1)
    col = lax.broadcasted_iota(jnp.int32, (2 * LANES, 2 * LANES), 1)
    right = col >= LANES
    col = col & (LANES - 1)
    swap = jnp.where((row ^ col) == GY, 1.0, 0.0)
    same = (row & GY) == (col & GY)
    plus = jnp.where((row == col + 1) & same, 1.0, 0.0)
    minus = jnp.where((row == col - 1) & same, 1.0, 0.0)
    left = plus - minus if difference else plus + minus + swap
    return jnp.where(right, swap, left).astype(BF16)


def lateral(x, matrix):
    high = x.astype(BF16)
    low = (x - high.astype(F32)).astype(BF16)
    return jnp.dot(jnp.concatenate([high, low], 1), matrix, preferred_element_type=F32)


def low_half(rows):
    return lax.broadcasted_iota(jnp.int32, (rows, LANES), 1) < GY


def force_stain(s_ref, k, j, regions, f_ref, u_ref, r_ref, y_ref, matrix):
    tiles = s_ref.shape[1]
    parts = [s_ref[k, :, s0 : s0 + n, :] for s0, _, _, n in regions]
    x = parts[0] if len(parts) == 1 else jnp.concatenate(parts, 1)
    total = x.shape[1]
    p = lateral(x.reshape(tiles * total, LANES), matrix)
    y_ref[...] = p[:, :LANES].reshape(tiles, total, LANES)
    r_ref[1 : tiles + 1] = p[:, LANES:].reshape(tiles, total, LANES)
    lo = low_half(16)
    for s0, f0, u0, n in regions:
        for z in range(0, n, 16):
            rows = slice(f0 + z, f0 + z + 16)
            r_now = r_ref[1, rows, :]
            before = jnp.where(lo, r_ref[0, rows, :], r_now)
            for c in range(tiles):
                r_next = r_ref[c + 2, rows, :]
                after = jnp.where(lo, r_now, r_next)
                gx = after - before
                before, r_now = after, r_next
                gy = y_ref[c, rows, :]
                s = s0 + z
                gz = s_ref[k, c, s + 1 : s + 17, :] - s_ref[k, c, s - 1 : s + 15, :]
                fixed = f_ref[j, rows, c * LANES : (c + 1) * LANES].astype(F32)
                at = slice(u0 + z, u0 + z + 16)
                ux, uy, uz = u_ref[0, c, at, :], u_ref[1, c, at, :], u_ref[2, c, at, :]
                moved = (gx * ux + gy * uy) + gz * uz
                twice = (fixed - s_ref[k, c, s : s + 16, :]) * 2.0 - moved
                denom = (gx * gx + gy * gy) + (gz * gz + (twice * twice + 2.0))
                w = twice / denom
                u_ref[0, c, at, :] = ux + w * gx
                u_ref[1, c, at, :] = uy + w * gy
                u_ref[2, c, at, :] = uz + w * gz


def sweep(src, store, q, z0, rows, r_ref, matrix):
    tiles = src.shape[1]
    x = src[q, :, z0 : z0 + rows, :].reshape(tiles * rows, LANES)
    p = lateral(x, matrix)
    r_ref[1 : tiles + 1] = p[:, LANES:].reshape(tiles, rows, LANES)
    inside = p[:, :LANES].reshape(tiles, rows, LANES)
    lo = low_half(rows)
    for c in range(tiles):
        depth = src[q, c, z0 - 1 : z0 - 1 + rows, :] + src[q, c, z0 + 1 : z0 + 1 + rows, :]
        across = jnp.where(lo, r_ref[c, :, :], r_ref[c + 2, :, :])
        store(c, src[q, c, z0 : z0 + rows, :] * (1.0 / RATE - 6.0) + depth + (inside[c] + across))


def fetch_template(own, recv, owner, k, j, f_ref, pieces, sems, base):
    mine = owner[k] == lax.axis_index("subj")
    for i, (src, dst, n) in enumerate(pieces):

        def copy(ref, i=i, src=src, dst=dst, n=n):
            return pltpu.make_async_copy(
                ref.at[0, k, pl.ds(src, n), :], f_ref.at[j, pl.ds(dst, n), :], sems.at[base + i]
            )

        @pl.when(mine)
        def _():
            copy(own).start()

        @pl.when(jnp.logical_not(mine))
        def _():
            copy(recv).start()


def wait_template(own, k, j, f_ref, pieces, sems, base):
    for i, (src, dst, n) in enumerate(pieces):
        pltpu.make_async_copy(
            own.at[0, k, pl.ds(src, n), :], f_ref.at[j, pl.ds(dst, n), :], sems.at[base + i]
        ).wait()


def edge_kernel(depth, order, owner, even_recv, odd_recv, subject, own, recv, moved, u_ref, even_send, odd_send,
                s_ref, f_ref, r_ref, y_ref, s_sem, f_sem, u_sem):
    stains, tiles = s_ref.shape[:2]
    last = depth // 8
    even = (lax.axis_index("depth") % 2) == 0
    s_copies = []
    for j in range(stains):
        for i, t in enumerate((0, 1, 2, last - 3, last - 2, last - 1)):
            s_copies.append(
                pltpu.make_async_copy(
                    subject.at[order[0, j], t], s_ref.at[order[0, j], :, 8 + 8 * i : 16 + 8 * i, :], s_sem.at[j, i]
                )
            )
    u_copies = [
        pltpu.make_async_copy(moved.at[:, t], u_ref.at[:, :, 8 * i : 8 * i + 8, :], u_sem.at[i])
        for i, t in enumerate((0, 1, last - 2, last - 1))
    ]
    pieces = ((0, 0, EDGE), (depth - EDGE, EDGE, EDGE))
    for j in range(stains):
        for copy in s_copies[6 * j : 6 * j + 6]:
            copy.start()
        fetch_template(own, recv, owner, order[0, j], j, f_ref, pieces, f_sem, 2 * j)
        if j == 0:
            for copy in u_copies:
                copy.start()
    r_ref[0] = jnp.zeros(r_ref.shape[1:], F32)
    r_ref[tiles + 1] = jnp.zeros(r_ref.shape[1:], F32)
    matrix = lateral_matrix(True)
    for c in range(tiles):
        at = slice(c * LANES, (c + 1) * LANES)
        a, b = even_recv[:, at], odd_recv[:, at]
        low, high = jnp.where(even, b, a), jnp.where(even, a, b)
        for k in range(stains):
            s_ref[k, c, 7:8, :] = low[k : k + 1]
            s_ref[k, c, 56:57, :] = high[k : k + 1]
    regions = ((8, 0, 0, EDGE), (40, EDGE, EDGE, EDGE))
    for j in range(stains):
        for copy in s_copies[6 * j : 6 * j + 6]:
            copy.wait()
        wait_template(own, order[0, j], j, f_ref, pieces, f_sem, 2 * j)
        if j == 0:
            for copy in u_copies:
                copy.wait()
        force_stain(s_ref, order[0, j], j, regions, f_ref, u_ref, r_ref, y_ref, matrix)
    n = SWEEPS
    for q in range(3):
        for c in range(tiles):
            at = slice(c * LANES, (c + 1) * LANES)
            low, high = u_ref[q, c, 0:n, :], u_ref[q, c, 2 * EDGE - n : 2 * EDGE, :]
            even_send[q, :, at] = jnp.where(even, high, low)
            odd_send[q, :, at] = jnp.where(even, low, high)


def inner_kernel(depth, order, owner, subject, own, recv, moved, edge, out,
                 s_ref, f_ref, r_ref, y_ref, a_ref, b_ref, rs_ref, o_ref, s_sem, f_sem, u_sem, o_sem):
    stains, tiles = s_ref.shape[:2]
    last = depth // 8
    first = EDGE // 8
    count = last - 2 * first
    rows = depth - 2 * EDGE
    s_copies = []
    for j in range(stains):
        k = order[0, j]
        for i in range(count + 2):
            s_copies.append(
                pltpu.make_async_copy(
                    subject.at[k, first - 1 + i], s_ref.at[k, :, 8 * i : 8 * i + 8, :], s_sem.at[j, i]
                )
            )
    per = count + 2
    u_copies = [
        pltpu.make_async_copy(
            moved.at[:, first + i], a_ref.at[:, :, 8 + EDGE + 8 * i : 16 + EDGE + 8 * i, :], u_sem.at[i]
        )
        for i in range(count)
    ]
    e_copies = [
        pltpu.make_async_copy(edge.at[:, :, 0:EDGE, :], a_ref.at[:, :, 8 : 8 + EDGE, :], u_sem.at[count]),
        pltpu.make_async_copy(
            edge.at[:, :, EDGE : 2 * EDGE, :], a_ref.at[:, :, 8 + depth - EDGE : 8 + depth, :], u_sem.at[count + 1]
        ),
    ]
    pieces = ((EDGE, 0, rows),)
    for j in range(stains):
        for copy in s_copies[per * j : per * j + per]:
            copy.start()
        fetch_template(own, recv, owner, order[0, j], j, f_ref, pieces, f_sem, j)
        if j == 0:
            for copy in u_copies:
                copy.start()
    for copy in e_copies:
        copy.start()
    for ref in (r_ref, rs_ref):
        ref[0] = jnp.zeros(ref.shape[1:], F32)
        ref[tiles + 1] = jnp.zeros(ref.shape[1:], F32)
    for ref in (a_ref, b_ref):
        ref[:, :, 0:8, :] = jnp.zeros((3, tiles, 8, LANES), F32)
        ref[:, :, 8 + depth : 16 + depth, :] = jnp.zeros((3, tiles, 8, LANES), F32)
    matrix = lateral_matrix(True)
    for j in range(stains):
        k = order[0, j]
        for copy in s_copies[per * j : per * j + per]:
            copy.wait()
        wait_template(own, k, j, f_ref, pieces, f_sem, j)
        if j == 0:
            for copy in u_copies:
                copy.wait()
        force_stain(s_ref, k, j, ((8, 0, 8 + EDGE, rows),), f_ref, a_ref, r_ref, y_ref, matrix)
    for copy in e_copies:
        copy.wait()
    matrix = lateral_matrix(False)
    src, dst = a_ref, b_ref
    for i in range(SWEEPS):
        final = i == SWEEPS - 1

        def one(q, _, src=src, dst=dst, final=final):
            def store(c, value):
                if final:
                    o_ref[q, :, c * LANES : (c + 1) * LANES] = value * RATE**SWEEPS
                else:
                    dst[q, c, 8 : 8 + depth, :] = value

            sweep(src, store, q, 8, depth, rs_ref, matrix)
            if final:
                pltpu.make_async_copy(o_ref.at[q], out.at[0, q], o_sem.at[q]).start()
            return 0

        lax.fori_loop(0, 3, one, 0)
        src, dst = dst, src
    for q in range(3):
        pltpu.make_async_copy(o_ref.at[q], out.at[0, q], o_sem.at[q]).wait()


def seam_kernel(depth, edge, even_recv, odd_recv, before, out, a_ref, b_ref, r_ref, o_ref, sem):
    tiles = edge.shape[1]
    at_depth = lax.axis_index("depth")
    even = (at_depth % 2) == 0
    has_low = at_depth > 0
    has_high = at_depth < lax.axis_size("depth") - 1
    ends = (0, depth - 8)
    ins = [
        pltpu.make_async_copy(before.at[0, :, z : z + 8, :], o_ref.at[i], sem.at[i]) for i, z in enumerate(ends)
    ]
    outs = [pltpu.make_async_copy(o_ref.at[i], out.at[0, :, z : z + 8, :], sem.at[i]) for i, z in enumerate(ends)]
    a_copies = [
        pltpu.make_async_copy(edge.at[:, :, 2 * EDGE - 8 : 2 * EDGE, :], a_ref.at[:, :, 8:16, :], sem.at[2]),
        pltpu.make_async_copy(edge.at[:, :, 0:8, :], a_ref.at[:, :, 24:32, :], sem.at[3]),
    ]
    for copy in a_copies + ins:
        copy.start()
    r_ref[0] = jnp.zeros(r_ref.shape[1:], F32)
    r_ref[tiles + 1] = jnp.zeros(r_ref.shape[1:], F32)
    for ref in (a_ref, b_ref):
        for z in (0, 32):
            ref[:, :, z : z + 8, :] = jnp.zeros((3, tiles, 8, LANES), F32)
    n = SWEEPS
    for q in range(3):
        for c in range(tiles):
            at = slice(c * LANES, (c + 1) * LANES)
            x, y = even_recv[q, :, at], odd_recv[q, :, at]
            a_ref[q, c, 16 : 16 + n, :] = jnp.where(even, x, y)
            a_ref[q, c, 20 : 20 + n, :] = jnp.where(even, y, x)
    row = lax.broadcasted_iota(jnp.int32, (24, LANES), 0)
    keep = jnp.where((row >= 8) & (row < 12), jnp.where(has_high, 1.0, 0.0), 1.0)
    keep = jnp.where((row >= 12) & (row < 16), jnp.where(has_low, 1.0, 0.0), keep)
    top = lax.broadcasted_iota(jnp.int32, (8, LANES), 0) < 4
    matrix = lateral_matrix(False)
    for copy in a_copies:
        copy.wait()
    src, dst = a_ref, b_ref
    for i in range(SWEEPS):
        final = i == SWEEPS - 1
        if final:
            for copy in ins:
                copy.wait()

        def one(q, _, src=src, dst=dst, final=final):
            def store(c, value):
                at = slice(c * LANES, (c + 1) * LANES)
                if final:
                    value = value * RATE**SWEEPS
                    o_ref[0, q, :, at] = jnp.where(top, value[16:24], o_ref[0, q, :, at])
                    o_ref[1, q, :, at] = jnp.where(top, o_ref[1, q, :, at], value[0:8])
                else:
                    dst[q, c, 8:32, :] = value * keep

            sweep(src, store, q, 8, 24, r_ref, matrix)
            return 0

        lax.fori_loop(0, 3, one, 0)
        src, dst = dst, src
    for copy in outs:
        copy.start()
    for copy in outs:
        copy.wait()


def local(template, owner, order, subject, displacement):
    stains, depth, cells = subject.shape[1:]
    tiles = cells // LANES
    count = lax.axis_size("depth")
    even_pairs, odd_pairs = pair_swaps(count)
    even = (lax.axis_index("depth") % 2) == 0

    recv = lax.ppermute(template, "subj", [(0, 1), (1, 0)])
    first, final = subject[0, :, 0, :], subject[0, :, depth - 1, :]
    even_recv = lax.ppermute(jnp.where(even, final, first), "depth", even_pairs)
    odd_recv = lax.ppermute(jnp.where(even, first, final), "depth", odd_pairs)

    def tiled(a):
        return a.reshape(a.shape[1], depth // 8, 8, tiles, LANES).transpose(0, 1, 3, 2, 4)

    subject5, moved5 = tiled(subject), tiled(displacement)
    sds = jax.ShapeDtypeStruct
    dma = pltpu.SemaphoreType.DMA
    edge, even_send, odd_send = pl.pallas_call(
        functools.partial(edge_kernel, depth),
        out_shape=(
            sds((3, tiles, 2 * EDGE, LANES), F32),
            sds((3, SWEEPS, cells), F32),
            sds((3, SWEEPS, cells), F32),
        ),
        in_specs=[SMEM, SMEM, VMEM, VMEM, ANY, ANY, ANY, ANY],
        out_specs=(VMEM, VMEM, VMEM),
        scratch_shapes=[
            pltpu.VMEM((stains, tiles, 64, LANES), F32),
            pltpu.VMEM((stains, 2 * EDGE, cells), BF16),
            pltpu.VMEM((tiles + 2, 2 * EDGE, LANES), F32),
            pltpu.VMEM((tiles, 2 * EDGE, LANES), F32),
            dma((stains, 6)),
            dma((2 * stains,)),
            dma((4,)),
        ],
        compiler_params=params(),
        cost_estimate=pl.CostEstimate(flops=10**8, bytes_accessed=8 << 20, transcendentals=0),
        name="edge_force",
    )(order, owner, even_recv, odd_recv, subject5, template, recv, moved5)

    u_even = lax.ppermute(even_send, "depth", even_pairs)
    u_odd = lax.ppermute(odd_send, "depth", odd_pairs)

    inner = depth - 2 * EDGE
    inside = pl.pallas_call(
        functools.partial(inner_kernel, depth),
        out_shape=sds(displacement.shape, F32),
        in_specs=[SMEM, SMEM, ANY, ANY, ANY, ANY, ANY],
        out_specs=ANY,
        scratch_shapes=[
            pltpu.VMEM((stains, tiles, inner + 16, LANES), F32),
            pltpu.VMEM((stains, inner, cells), BF16),
            pltpu.VMEM((tiles + 2, inner, LANES), F32),
            pltpu.VMEM((tiles, inner, LANES), F32),
            pltpu.VMEM((3, tiles, depth + 16, LANES), F32),
            pltpu.VMEM((3, tiles, depth + 16, LANES), F32),
            pltpu.VMEM((tiles + 2, depth, LANES), F32),
            pltpu.VMEM((3, depth, cells), F32),
            dma((stains, inner // 8 + 2)),
            dma((stains,)),
            dma((inner // 8 + 2,)),
            dma((3,)),
        ],
        compiler_params=params(),
        cost_estimate=pl.CostEstimate(flops=10**9, bytes_accessed=40 << 20, transcendentals=0),
        name="inner_force_and_sweeps",
    )(order, owner, subject5, template, recv, moved5, edge)

    return pl.pallas_call(
        functools.partial(seam_kernel, depth),
        out_shape=sds(displacement.shape, F32),
        in_specs=[ANY, VMEM, VMEM, ANY],
        out_specs=ANY,
        scratch_shapes=[
            pltpu.VMEM((3, tiles, 40, LANES), F32),
            pltpu.VMEM((3, tiles, 40, LANES), F32),
            pltpu.VMEM((tiles + 2, 24, LANES), F32),
            pltpu.VMEM((2, 3, 8, cells), F32),
            dma((4,)),
        ],
        input_output_aliases={3: 0},
        compiler_params=params(),
        name="seam_sweeps",
    )(edge, u_even, u_odd, inside)


def solution(mesh):
    placed = (
        P("subj", None, "depth", None),
        P(),
        P(("grp", "subj"), None),
        P(("grp", "subj"), None, "depth", None),
        P(("grp", "subj"), None, "depth", None),
    )
    return jax.shard_map(
        local,
        mesh=mesh,
        in_specs=placed,
        out_specs=P(("grp", "subj"), None, "depth", None),
        check_vma=False,
    )
```

time: 157 us -> 44.1 us (0.28); the launches traced: 155 us -> 43.9 us
  other arithmetic: 62.5 us -> 0.09 us
  between operations: 31.2 us -> 0.08 us
  starting transfers between devices: 34 us -> 8.89 us
  Pallas kernels: 0 us -> 22.9 us
  local copies, waits for them, and re-layouts: 22.7 us -> 7.1 us
    add x8 -> x0, other arithmetic: 30.9 us -> none  [the longest x4 18.2 us: apply_force(): u + step_size * diff[:, None] * jnp.stack([gx, gy, gz], 1) / denom[:, None]]
    ppermute x10 -> x5, starting transfers between devices: 34 us -> 8.89 us  [the longest x1 4.43 us: local(): u_odd = lax.ppermute(odd_send, 'depth', odd_pairs)]
    pallas_call x0 -> x3, Pallas kernels: none -> 22.9 us  [the longest x1 12.6 us: local(): pl.pallas_call(functools.partial(inner_kernel, depth), out_shape=sds(disp...]
    slice x17 -> x1, local copies, waits for them, and re-layouts: 19.5 us -> 1.29 us  [local(): first, final = (subject[0, :, 0, :], subject[0, :, depth - 1, :])]
    div x4 -> x0, other arithmetic: 17.4 us -> none  [apply_force(): step_size * diff[:, None] * jnp.stack([gx, gy, gz], 1) / denom[:, None]]
    mul x3 -> x0, other arithmetic: 9.24 us -> none  [the longest x1 3.18 us: gradients(): grad_x = (x_plus - x_minus) * 0.5]
    another operation x1 -> x0, other arithmetic: 2.89 us -> none  [fetch_fixed(): return jnp.stack(slabs, 0).astype(jnp.float32)]
    unnamed x18 -> x12, local copies, waits for them, and re-layouts: 3.17 us -> 5.81 us
  transfers between devices with their start and end apart: 11 -> 5, of which waited for: 4 -> 2; matrix products, arithmetic and copies ran while one was open for 17% -> 3% of each run, Pallas kernels for 0% -> 29%
where the time goes in v1:
time: 44.1 us; the launch traced here: 43.9 us
  Pallas kernels  22.9 us (52%)
  starting transfers between devices  8.89 us (20%)
  local copies, waits for them, and re-layouts  7.1 us (16%)
  waiting for transfers between devices  4.81 us (11%)
    pallas_call x1, Pallas kernels, local(): pl.pallas_call(functools.partial(inner_kernel, depth), out_shape=sds(disp...  12.6 us
    unnamed x12, local copies, waits for them, and re-layouts  5.81 us
    pallas_call x1, Pallas kernels, local(): pl.pallas_call(functools.partial(edge_kernel, depth), out_shape=(sds((3,...  5.52 us
    pallas_call x1, Pallas kernels, local(): pl.pallas_call(functools.partial(seam_kernel, depth), out_shape=sds(displ...  4.72 us
    ppermute x1, starting transfers between devices, local(): u_odd = lax.ppermute(odd_send, 'depth', odd_pairs)  4.43 us
    ppermute x1, waiting for transfers between devices, local(): odd_recv = lax.ppermute(jnp.where(even, first, final), 'depth', odd_pairs)  3.51 us
    ppermute x1, starting transfers between devices, local(): odd_recv = lax.ppermute(jnp.where(even, first, final), 'depth', odd_pairs)  3.43 us
    ppermute x1, waiting for transfers between devices, local(): even_recv = lax.ppermute(jnp.where(even, final, first), 'depth', even_pairs)  1.3 us
  transfers between devices with their start and end apart: 5, of which 2 were waited for; matrix products, arithmetic and copies ran while one was open for 3% of the time, Pallas kernels for 29%

profile of v1, /device:TPU:12, one launch (start us, length us, event | category | flops | bytes accessed | tf_op | source)
XLA Modules:
  0.0 43.9 jit_solution(8901739802535434390)
XLA Ops:
  0.0 0.0 collective-permute-start.2
  0.0 1.3 %fusion = (f32[1,4,1,4096]{3,2,1,0:T(1,128)S(1)}, f32[1,4,1,4096]{3,2,1,0:T(1,128)S(1)}) fusion(f32[1,4,64,4096]{3,2,1,0:T(8,128)} %param.8), kind=kLoop, calls=%fused_computation.2 | loop fusion | bytes 262144 | tf_op jit(solution)/shard_map/slice | solution.py:334
  1.3 0.1 select_bitcast_fusion
  1.4 3.4 %collective-permute-start.1 = (f32[4,4096]{1,0:T(4,128)S(1)}, f32[4,4096]{1,0:T(4,128)S(1)}, u32[]{:S(2)}, u32[]{:S(2)}) collective-permute-start(f32[4,4096]{1,0:T(4,128)S(1)} %get-tuple-element.13), channel_id=1, source_target_pairs={{1,2},{2,1},{3,4},{4,3},{5,6},{6,5},{9,10},{10,9},{11,12},{12,11},... | collective-permute-start | bytes 196616 | tf_op jit(solution)/shard_map/ppermute | solution.py:336
  4.8 0.5 %collective-permute-start = (f32[4,4096]{1,0:T(4,128)S(1)}, f32[4,4096]{1,0:T(4,128)S(1)}, u32[]{:S(2)}, u32[]{:S(2)}) collective-permute-start(f32[4,4096]{1,0:T(4,128)S(1)} %get-tuple-element.14), channel_id=1, source_target_pairs={{0,1},{1,0},{2,3},{3,2},{4,5},{5,4},{6,7},{7,6},{8,9},{9,8},{10,11... | collective-permute-start | bytes 196616 | tf_op jit(solution)/shard_map/ppermute | solution.py:335
  5.3 3.5 %collective-permute-done.1.odd_recv = f32[4,4096]{1,0:T(4,128)S(1)} collective-permute-done((f32[4,4096]{1,0:T(4,128)S(1)}, f32[4,4096]{1,0:T(4,128)S(1)}, u32[]{:S(2)}, u32[]{:S(2)}) %collective-permute-start.1) | collective-permute-done | bytes 65568 | tf_op jit(solution)/shard_map/ppermute | solution.py:336
  8.8 1.3 %collective-permute-done.even_recv = f32[4,4096]{1,0:T(4,128)S(1)} collective-permute-done((f32[4,4096]{1,0:T(4,128)S(1)}, f32[4,4096]{1,0:T(4,128)S(1)}, u32[]{:S(2)}, u32[]{:S(2)}) %collective-permute-start) | collective-permute-done | bytes 65568 | tf_op jit(solution)/shard_map/ppermute | solution.py:335
  10.1 0.0 collective-permute-done.2.recv
  10.1 0.0 copy-start.2
  10.1 1.3 %copy-done.2 = bf16[1,4,64,4096]{3,2,1,0:T(8,128)(2,1)} copy-done((bf16[1,4,64,4096]{3,2,1,0:T(8,128)(2,1)}, bf16[1,4,64,4096]{3,2,1,0:T(8,128)(2,1)S(1)}, u32[]{:S(2)}) %copy-start.2) | copy-done | bytes 2097176
  11.4 0.0 copy-start
  11.4 1.6 %copy-done = bf16[1,4,64,4096]{3,2,1,0:T(8,128)(2,1)S(1)} copy-done((bf16[1,4,64,4096]{3,2,1,0:T(8,128)(2,1)S(1)}, bf16[1,4,64,4096]{3,2,1,0:T(8,128)(2,1)}, u32[]{:S(2)}) %copy-start) | copy-done | bytes 2097176
  13.0 0.0 copy-start.4
  13.0 0.7 %copy-done.4 = s32[1,4]{1,0:T(1,128)S(1)} copy-done((s32[1,4]{1,0:T(1,128)S(1)}, s32[1,4]{1,0:T(1,128)}, u32[]{:S(2)}) %copy-start.4) | copy-done | bytes 40
  13.7 0.0 copy-start.5
  13.7 0.7 %copy-done.5 = s32[4]{0:T(128)S(1)} copy-done((s32[4]{0:T(128)S(1)}, s32[4]{0:T(128)}, u32[]{:S(2)}) %copy-start.5) | copy-done | bytes 40
  14.3 0.0 copy-start.1
  14.3 5.5 %edge_force.1 = (f32[3,32,32,128]{3,2,1,0:T(8,128)S(1)}, f32[3,4,4096]{2,1,0:T(4,128)S(1)}, f32[3,4,4096]{2,1,0:T(4,128)S(1)}) custom-call(s32[1,4]{1,0:T(1,128)S(1)} %copy-done.4, s32[4]{0:T(128)S(1)} %copy-done.5, f32[4,4096]{1,0:T(4,128)S(1)} %collective-permute-done.even_recv, f32[4,4096]{1,0:T(4,128)S(1)} %collective-permute-done.1.odd_recv, ...), custom_call_target="tpu_custom_call" | custom-call | flops 100000000 | bytes 8388608 | tf_op jit(solution)/shard_map/edge_force/pallas_call | solution.py:344
  19.9 0.6 %collective-permute-start.3 = (f32[3,4,4096]{2,1,0:T(4,128)S(1)}, f32[3,4,4096]{2,1,0:T(4,128)S(1)}, u32[]{:S(2)}, u32[]{:S(2)}) collective-permute-start(f32[3,4,4096]{2,1,0:T(4,128)S(1)} %get-tuple-element.9), channel_id=1, source_target_pairs={{0,1},{1,0},{2,3},{3,2},{4,5},{5,4},{6,7},{7,6},{8,9},{9,8},{10,11... | collective-permute-start | bytes 589832 | tf_op jit(solution)/shard_map/ppermute | solution.py:367
  20.4 4.4 %collective-permute-start.4 = (f32[3,4,4096]{2,1,0:T(4,128)S(1)}, f32[3,4,4096]{2,1,0:T(4,128)S(1)}, u32[]{:S(2)}, u32[]{:S(2)}) collective-permute-start(f32[3,4,4096]{2,1,0:T(4,128)S(1)} %get-tuple-element.10), channel_id=1, source_target_pairs={{1,2},{2,1},{3,4},{4,3},{5,6},{6,5},{9,10},{10,9},{11,12},{12,11},... | collective-permute-start | bytes 589832 | tf_op jit(solution)/shard_map/ppermute | solution.py:368
  24.9 0.0 copy-done.1
  24.9 0.0 copy-start.3
  24.9 1.6 %copy-done.3 = bf16[1,4,64,4096]{3,2,1,0:T(8,128)(2,1)S(1)} copy-done((bf16[1,4,64,4096]{3,2,1,0:T(8,128)(2,1)S(1)}, bf16[1,4,64,4096]{3,2,1,0:T(8,128)(2,1)}, u32[]{:S(2)}) %copy-start.3) | copy-done | bytes 2097176
  26.5 12.6 %inner_force_and_sweeps.1.before = f32[1,3,64,4096]{3,2,1,0:T(8,128)} custom-call(s32[1,4]{1,0:T(1,128)S(1)} %copy-done.4, s32[4]{0:T(128)S(1)} %copy-done.5, f32[4,8,32,8,128]{4,3,2,1,0:T(8,128)} %bitcast.11, bf16[1,4,64,4096]{3,2,1,0:T(8,128)(2,1)S(1)} %copy-done.1, bf16[1,4,64,4096]{3,2,1,0:T(8,128)(2,1)S(1)} %copy-done.3, ...), custom_call_target="tpu_custom_call" | custom-call | flops 1000000000 | bytes 41943040 | tf_op jit(solution)/shard_map/inner_force_and_sweeps/pallas_call | solution.py:371
  39.1 0.0 collective-permute-done.3.even_recv
  39.1 0.0 collective-permute-done.4.odd_recv
  39.1 4.7 %seam_sweeps.1 = f32[1,3,64,4096]{3,2,1,0:T(8,128)} custom-call(f32[3,32,32,128]{3,2,1,0:T(8,128)S(1)} %get-tuple-element.8.edge, f32[3,4,4096]{2,1,0:T(4,128)S(1)} %collective-permute-done.3.even_recv, f32[3,4,4096]{2,1,0:T(4,128)S(1)} %collective-permute-done.4.odd_recv, ...), custom_call_target="tpu_custom_call", output_to_operand_aliasing={{}: (3, {})} | custom-call | tf_op jit(solution)/shard_map/seam_sweeps/pallas_call | solution.py:395
Async XLA Ops:
  0.0 10.1 %collective-permute-start.2 = (bf16[1,4,64,4096]{3,2,1,0:T(8,128)(2,1)}, bf16[1,4,64,4096]{3,2,1,0:T(8,128)(2,1)S(1)}, u32[]{:S(2)}, u32[]{:S(2)}) collective-permute-start(bf16[1,4,64,4096]{3,2,1,0:T(8,128)(2,1)} %own.3), channel_id=1, source_target_pairs={{0,8},{8,0},{1,9},{9,1},{2,10},{10,2},{3,11},{11,3},{4,12},{12,4},... | collective-permute-start | bytes 6291464 | tf_op jit(solution)/shard_map/ppermute | solution.py:333
  1.4 7.4 %collective-permute-start.1 = (f32[4,4096]{1,0:T(4,128)S(1)}, f32[4,4096]{1,0:T(4,128)S(1)}, u32[]{:S(2)}, u32[]{:S(2)}) collective-permute-start(f32[4,4096]{1,0:T(4,128)S(1)} %get-tuple-element.13), channel_id=1, source_target_pairs={{1,2},{2,1},{3,4},{4,3},{5,6},{6,5},{9,10},{10,9},{11,12},{12,11},... | collective-permute-start | bytes 196616 | tf_op jit(solution)/shard_map/ppermute | solution.py:336
  4.8 5.3 %collective-permute-start = (f32[4,4096]{1,0:T(4,128)S(1)}, f32[4,4096]{1,0:T(4,128)S(1)}, u32[]{:S(2)}, u32[]{:S(2)}) collective-permute-start(f32[4,4096]{1,0:T(4,128)S(1)} %get-tuple-element.14), channel_id=1, source_target_pairs={{0,1},{1,0},{2,3},{3,2},{4,5},{5,4},{6,7},{7,6},{8,9},{9,8},{10,11... | collective-permute-start | bytes 196616 | tf_op jit(solution)/shard_map/ppermute | solution.py:335
  10.1 1.3 %copy-start.2 = (bf16[1,4,64,4096]{3,2,1,0:T(8,128)(2,1)}, bf16[1,4,64,4096]{3,2,1,0:T(8,128)(2,1)S(1)}, u32[]{:S(2)}) copy-start(bf16[1,4,64,4096]{3,2,1,0:T(8,128)(2,1)S(1)} %collective-permute-done.2.recv) | copy-start | bytes 6291460
  11.4 1.6 %copy-start = (bf16[1,4,64,4096]{3,2,1,0:T(8,128)(2,1)S(1)}, bf16[1,4,64,4096]{3,2,1,0:T(8,128)(2,1)}, u32[]{:S(2)}) copy-start(bf16[1,4,64,4096]{3,2,1,0:T(8,128)(2,1)} %own.3) | copy-start | bytes 6291460
  13.0 0.7 %copy-start.4 = (s32[1,4]{1,0:T(1,128)S(1)}, s32[1,4]{1,0:T(1,128)}, u32[]{:S(2)}) copy-start(s32[1,4]{1,0:T(1,128)} %order.3) | copy-start | bytes 52
  13.7 0.7 %copy-start.5 = (s32[4]{0:T(128)S(1)}, s32[4]{0:T(128)}, u32[]{:S(2)}) copy-start(s32[4]{0:T(128)} %owner.3) | copy-start | bytes 52
  14.3 10.5 %copy-start.1 = (bf16[1,4,64,4096]{3,2,1,0:T(8,128)(2,1)S(1)}, bf16[1,4,64,4096]{3,2,1,0:T(8,128)(2,1)}, u32[]{:S(2)}) copy-start(bf16[1,4,64,4096]{3,2,1,0:T(8,128)(2,1)} %own.3) | copy-start | bytes 6291460
  19.9 19.3 %collective-permute-start.3 = (f32[3,4,4096]{2,1,0:T(4,128)S(1)}, f32[3,4,4096]{2,1,0:T(4,128)S(1)}, u32[]{:S(2)}, u32[]{:S(2)}) collective-permute-start(f32[3,4,4096]{2,1,0:T(4,128)S(1)} %get-tuple-element.9), channel_id=1, source_target_pairs={{0,1},{1,0},{2,3},{3,2},{4,5},{5,4},{6,7},{7,6},{8,9},{9,8},{10,11... | collective-permute-start | bytes 589832 | tf_op jit(solution)/shard_map/ppermute | solution.py:367
  20.4 18.7 %collective-permute-start.4 = (f32[3,4,4096]{2,1,0:T(4,128)S(1)}, f32[3,4,4096]{2,1,0:T(4,128)S(1)}, u32[]{:S(2)}, u32[]{:S(2)}) collective-permute-start(f32[3,4,4096]{2,1,0:T(4,128)S(1)} %get-tuple-element.10), channel_id=1, source_target_pairs={{1,2},{2,1},{3,4},{4,3},{5,6},{6,5},{9,10},{10,9},{11,12},{12,11},... | collective-permute-start | bytes 589832 | tf_op jit(solution)/shard_map/ppermute | solution.py:368
  24.9 1.6 %copy-start.3 = (bf16[1,4,64,4096]{3,2,1,0:T(8,128)(2,1)S(1)}, bf16[1,4,64,4096]{3,2,1,0:T(8,128)(2,1)}, u32[]{:S(2)}) copy-start(bf16[1,4,64,4096]{3,2,1,0:T(8,128)(2,1)} %copy-done.2) | copy-start | bytes 6291460

commit v2 on v1

v2 whole, which is shorter than its diff:
```python
import functools

import jax
import jax.numpy as jnp
from jax import lax
from jax.experimental import pallas as pl
from jax.experimental.pallas import tpu as pltpu
from jax.sharding import PartitionSpec as P

GY = 64
SWEEPS = 4
LANES = 128
RATE = 0.15
F32 = jnp.float32
BF16 = jnp.bfloat16

ANY = pl.BlockSpec(memory_space=pl.ANY)
HBM = pl.BlockSpec(memory_space=pltpu.HBM)
VMEM = pl.BlockSpec(memory_space=pltpu.VMEM)


def params(mib):
    return pltpu.CompilerParams(vmem_limit_bytes=mib << 20)


def pair_swaps(count):
    def swaps(first):
        return [p for i in range(first, count - 1, 2) for p in ((i, i + 1), (i + 1, i))]

    return swaps(0), swaps(1)


def lateral_matrix(difference):
    row = lax.broadcasted_iota(jnp.int32, (2 * LANES, 2 * LANES), 0) & (LANES - 1)
    col = lax.broadcasted_iota(jnp.int32, (2 * LANES, 2 * LANES), 1)
    right = col >= LANES
    col = col & (LANES - 1)
    swap = jnp.where((row ^ col) == GY, 1.0, 0.0)
    same = (row & GY) == (col & GY)
    plus = jnp.where((row == col + 1) & same, 1.0, 0.0)
    minus = jnp.where((row == col - 1) & same, 1.0, 0.0)
    left = plus - minus if difference else plus + minus + swap
    return jnp.where(right, swap, left).astype(BF16)


def lateral(x, matrix):
    high = x.astype(BF16)
    low = (x - high.astype(F32)).astype(BF16)
    return jnp.dot(jnp.concatenate([high, low], 1), matrix, preferred_element_type=F32)


def low_half(rows):
    return lax.broadcasted_iota(jnp.int32, (rows, LANES), 1) < GY


def pieces_of(start, rows):
    done = start
    while done < start + rows:
        block = done // 16 * 16
        stop = min(block + 16, start + rows)
        yield block, done - block, stop - done
        done = stop


def force_stain(s_ref, k, regions, f_ref, u_ref, r_ref, y_ref, matrix):
    tiles = s_ref.shape[1]
    parts = [s_ref[k, :, s0 : s0 + n, :] for s0, _, _, n in regions]
    x = parts[0] if len(parts) == 1 else jnp.concatenate(parts, 1)
    total = x.shape[1]
    p = lateral(x.reshape(tiles * total, LANES), matrix)
    y_ref[...] = p[:, :LANES].reshape(tiles, total, LANES)
    r_ref[1 : tiles + 1] = p[:, LANES:].reshape(tiles, total, LANES)
    base = 0
    for s0, f0, u0, n in regions:
        for block, skip, count in pieces_of(f0, n):
            z = block + skip - f0
            rows = slice(base + z, base + z + count)
            at = slice(u0 + z, u0 + z + count)
            s = s0 + z
            lo = low_half(count)
            r_now = r_ref[1, rows, :]
            before = jnp.where(lo, r_ref[0, rows, :], r_now)
            for c in range(tiles):
                r_next = r_ref[c + 2, rows, :]
                after = jnp.where(lo, r_now, r_next)
                gx = after - before
                before, r_now = after, r_next
                gy = y_ref[c, rows, :]
                gz = s_ref[k, c, s + 1 : s + 1 + count, :] - s_ref[k, c, s - 1 : s - 1 + count, :]
                fixed = f_ref[k, block : block + 16, c * LANES : (c + 1) * LANES].astype(F32)
                fixed = fixed[skip : skip + count]
                ux, uy, uz = u_ref[0, c, at, :], u_ref[1, c, at, :], u_ref[2, c, at, :]
                moved = (gx * ux + gy * uy) + gz * uz
                twice = (fixed - s_ref[k, c, s : s + count, :]) * 2.0 - moved
                denom = (gx * gx + gy * gy) + (gz * gz + (twice * twice + 2.0))
                w = twice * inverse(denom)
                u_ref[0, c, at, :] = ux + w * gx
                u_ref[1, c, at, :] = uy + w * gy
                u_ref[2, c, at, :] = uz + w * gz
        base += n


def inverse(x):
    r = pl.reciprocal(x, approx=True)
    return r * (2.0 - x * r)


def sweep(src, store, q, z0, rows, r_ref, matrix):
    tiles = src.shape[1]
    x = src[q, :, z0 : z0 + rows, :].reshape(tiles * rows, LANES)
    p = lateral(x, matrix)
    r_ref[q, 1 : tiles + 1] = p[:, LANES:].reshape(tiles, rows, LANES)
    inside = p[:, :LANES].reshape(tiles, rows, LANES)
    lo = low_half(rows)
    for c in range(tiles):
        depth = src[q, c, z0 - 1 : z0 - 1 + rows, :] + src[q, c, z0 + 1 : z0 + 1 + rows, :]
        across = jnp.where(lo, r_ref[q, c, :, :], r_ref[q, c + 2, :, :])
        store(c, src[q, c, z0 : z0 + rows, :] * (1.0 / RATE - 6.0) + depth + (inside[c] + across))


def clear_rim(ref, axis):
    shape = list(ref.shape)
    shape[axis] = 1
    at = [slice(None)] * len(shape)
    for i in (0, ref.shape[axis] - 1):
        at[axis] = slice(i, i + 1)
        ref[tuple(at)] = jnp.zeros(shape, F32)


class Template:
    def __init__(self, own, recv, owner, f_ref, sems, pieces):
        self.own, self.recv, self.owner, self.f_ref, self.sems, self.pieces = own, recv, owner, f_ref, sems, pieces

    def copy(self, ref, k, i):
        src, dst, n = self.pieces[i]
        return pltpu.make_async_copy(
            ref.at[0, k, pl.ds(src, n), :], self.f_ref.at[k, pl.ds(dst, n), :], self.sems.at[k, i]
        )

    def start(self, k):
        mine = self.owner[k] == lax.axis_index("subj")

        @pl.when(mine)
        def _():
            for i in range(len(self.pieces)):
                self.copy(self.own, k, i).start()

        @pl.when(jnp.logical_not(mine))
        def _():
            for i in range(len(self.pieces)):
                self.copy(self.recv, k, i).start()

    def wait(self, k):
        for i in range(len(self.pieces)):
            self.copy(self.own, k, i).wait()


def force_steps(order_hbm, owner_hbm, subject, own, recv, moved, order, owner, s_ref, f_ref, r_ref, y_ref,
                u_ref, o_sem, s_sem, f_sem, u_sem, planes, pieces, u_planes, regions, halo=None):
    stains = s_ref.shape[0]
    small = [
        pltpu.make_async_copy(order_hbm, order, o_sem.at[0]),
        pltpu.make_async_copy(owner_hbm, owner, o_sem.at[1]),
    ]
    for copy in small:
        copy.start()

    def s_copies(k):
        return [
            pltpu.make_async_copy(subject.at[k, t], s_ref.at[k, :, z : z + 8, :], s_sem.at[k, i])
            for i, (t, z) in enumerate(planes)
        ]

    for copy in small:
        copy.wait()
    template = Template(own, recv, owner, f_ref, f_sem, pieces)
    u_copies = [
        pltpu.make_async_copy(moved.at[:, t], u_ref.at[:, :, z : z + 8, :], u_sem.at[i])
        for i, (t, z) in enumerate(u_planes)
    ]
    for j in range(stains):
        k = order[0, j]
        for copy in s_copies(k):
            copy.start()
        template.start(k)
        if j == 0:
            for copy in u_copies:
                copy.start()
    clear_rim(r_ref, 0)
    matrix = lateral_matrix(True)
    if halo is not None:
        halo()
    for j in range(stains):
        k = order[0, j]
        for copy in s_copies(k):
            copy.wait()
        template.wait(k)
        if j == 0:
            for copy in u_copies:
                copy.wait()
        force_stain(s_ref, k, regions, f_ref, u_ref, r_ref, y_ref, matrix)


def inner_kernel(depth, order_hbm, owner_hbm, subject, own, recv, moved, u_ref, *scratch):
    last = depth // 8
    planes = [(t, 8 * t) for t in range(last)]
    u_planes = [(t, 8 * t - 8) for t in range(1, last - 1)]
    order, owner, s_ref, f_ref, r_ref, y_ref, o_sem, s_sem, f_sem, u_sem = scratch
    force_steps(order_hbm, owner_hbm, subject, own, recv, moved, order, owner, s_ref, f_ref, r_ref, y_ref,
                u_ref, o_sem, s_sem, f_sem, u_sem, planes, ((0, 0, depth),), u_planes, ((8, 8, 0, depth - 16),))


def edge_kernel(depth, order_hbm, owner_hbm, even_recv, odd_recv, subject, own, recv, moved, middle, u_ref, even_send,
                odd_send, *scratch):
    order, owner, s_ref, f_ref, r_ref, y_ref, o_sem, s_sem, f_sem, u_sem = scratch
    stains, tiles = s_ref.shape[:2]
    last = depth // 8
    even = (lax.axis_index("depth") % 2) == 0

    def halo():
        for c in range(tiles):
            at = slice(c * LANES, (c + 1) * LANES)
            a, b = even_recv[:, at], odd_recv[:, at]
            low, high = jnp.where(even, b, a), jnp.where(even, a, b)
            for k in range(stains):
                s_ref[k, c, 7:8, :] = low[k : k + 1]
                s_ref[k, c, 40:41, :] = high[k : k + 1]

    planes = [(0, 8), (1, 16), (last - 2, 24), (last - 1, 32)]
    pieces = ((0, 0, 16), (depth - 16, 16, 16))
    force_steps(order_hbm, owner_hbm, subject, own, recv, moved, order, owner, s_ref, f_ref, r_ref, y_ref,
                u_ref, o_sem, s_sem, f_sem, u_sem, planes, pieces, [(0, 0), (last - 1, 8)],
                ((8, 0, 0, 8), (32, 24, 8, 8)), halo)
    n = SWEEPS
    for q in range(3):
        for c in range(tiles):
            at = slice(c * LANES, (c + 1) * LANES)
            low, high = u_ref[q, c, 0:n, :], u_ref[q, c, 16 - n : 16, :]
            even_send[q, :, at] = jnp.where(even, high, low)
            odd_send[q, :, at] = jnp.where(even, low, high)


def sweep_kernel(depth, middle, edge, out, a_ref, b_ref, r_ref, o_ref, sem, o_sem):
    tiles = a_ref.shape[1]

    def ins(q):
        return [
            pltpu.make_async_copy(middle.at[q], a_ref.at[q, :, 16:depth, :], sem.at[q, 0]),
            pltpu.make_async_copy(edge.at[q, :, 0:8, :], a_ref.at[q, :, 8:16, :], sem.at[q, 1]),
            pltpu.make_async_copy(edge.at[q, :, 8:16, :], a_ref.at[q, :, depth : depth + 8, :], sem.at[q, 2]),
        ]

    for q in range(3):
        for copy in ins(q):
            copy.start()
    clear_rim(r_ref, 1)
    for ref in (a_ref, b_ref):
        for z in (0, depth + 8):
            ref[:, :, z : z + 8, :] = jnp.zeros((3, tiles, 8, LANES), F32)
    matrix = lateral_matrix(False)
    src, dst = a_ref, b_ref
    for i in range(SWEEPS):
        final = i == SWEEPS - 1
        for q in range(3):

            def store(c, value, q=q, dst=dst, final=final):
                if final:
                    o_ref[q, :, c * LANES : (c + 1) * LANES] = value * RATE**SWEEPS
                else:
                    dst[q, c, 8 : 8 + depth, :] = value

            if i == 0:
                for copy in ins(q):
                    copy.wait()
            sweep(src, store, q, 8, depth, r_ref, matrix)
            if final:
                pltpu.make_async_copy(o_ref.at[q], out.at[0, q], o_sem.at[q]).start()
        src, dst = dst, src
    for q in range(3):
        pltpu.make_async_copy(o_ref.at[q], out.at[0, q], o_sem.at[q]).wait()


def seam_kernel(depth, edge, even_recv, odd_recv, before, out, a_ref, b_ref, r_ref, o_ref, sem):
    tiles = edge.shape[1]
    at_depth = lax.axis_index("depth")
    even = (at_depth % 2) == 0
    has_low = at_depth > 0
    has_high = at_depth < lax.axis_size("depth") - 1
    ends = (0, depth - 8)
    ins = [
        pltpu.make_async_copy(before.at[0, :, z : z + 8, :], o_ref.at[i], sem.at[i]) for i, z in enumerate(ends)
    ]
    outs = [pltpu.make_async_copy(o_ref.at[i], out.at[0, :, z : z + 8, :], sem.at[i]) for i, z in enumerate(ends)]
    a_copies = [
        pltpu.make_async_copy(edge.at[:, :, 8:16, :], a_ref.at[:, :, 8:16, :], sem.at[2]),
        pltpu.make_async_copy(edge.at[:, :, 0:8, :], a_ref.at[:, :, 24:32, :], sem.at[3]),
    ]
    for copy in a_copies + ins:
        copy.start()
    clear_rim(r_ref, 1)
    for ref in (a_ref, b_ref):
        for z in (0, 32):
            ref[:, :, z : z + 8, :] = jnp.zeros((3, tiles, 8, LANES), F32)
    n = SWEEPS
    for q in range(3):
        for c in range(tiles):
            at = slice(c * LANES, (c + 1) * LANES)
            x, y = even_recv[q, :, at], odd_recv[q, :, at]
            a_ref[q, c, 16 : 16 + n, :] = jnp.where(even, x, y)
            a_ref[q, c, 20 : 20 + n, :] = jnp.where(even, y, x)
    row = lax.broadcasted_iota(jnp.int32, (24, LANES), 0)
    keep = jnp.where((row >= 8) & (row < 12), jnp.where(has_high, 1.0, 0.0), 1.0)
    keep = jnp.where((row >= 12) & (row < 16), jnp.where(has_low, 1.0, 0.0), keep)
    top = lax.broadcasted_iota(jnp.int32, (8, LANES), 0) < 4
    matrix = lateral_matrix(False)
    for copy in a_copies:
        copy.wait()
    src, dst = a_ref, b_ref
    for i in range(SWEEPS):
        final = i == SWEEPS - 1
        if final:
            for copy in ins:
                copy.wait()
        for q in range(3):

            def store(c, value, q=q, dst=dst, final=final):
                at = slice(c * LANES, (c + 1) * LANES)
                if final:
                    value = value * RATE**SWEEPS
                    o_ref[0, q, :, at] = jnp.where(top, value[16:24], o_ref[0, q, :, at])
                    o_ref[1, q, :, at] = jnp.where(top, o_ref[1, q, :, at], value[0:8])
                else:
                    dst[q, c, 8:32, :] = value * keep

            sweep(src, store, q, 8, 24, r_ref, matrix)
        src, dst = dst, src
    for copy in outs:
        copy.start()
    for copy in outs:
        copy.wait()


def local(template, owner, order, subject, displacement):
    stains, depth, cells = subject.shape[1:]
    tiles = cells // LANES
    count = lax.axis_size("depth")
    even_pairs, odd_pairs = pair_swaps(count)
    even = (lax.axis_index("depth") % 2) == 0

    recv = lax.ppermute(template, "subj", [(0, 1), (1, 0)])
    first, final = subject[0, :, 0, :], subject[0, :, depth - 1, :]
    even_recv = lax.ppermute(jnp.where(even, final, first), "depth", even_pairs)
    odd_recv = lax.ppermute(jnp.where(even, first, final), "depth", odd_pairs)

    def tiled(a):
        return a.reshape(a.shape[1], depth // 8, 8, tiles, LANES).transpose(0, 1, 3, 2, 4)

    subject5, moved5 = tiled(subject), tiled(displacement)
    sds = jax.ShapeDtypeStruct
    dma = pltpu.SemaphoreType.DMA

    def force_scratch(s_planes, f_planes, planes, s_parts, f_parts, u_parts):
        return [
            pltpu.SMEM(order.shape, jnp.int32),
            pltpu.SMEM(owner.shape, jnp.int32),
            pltpu.VMEM((stains, tiles, s_planes, LANES), F32),
            pltpu.VMEM((stains, f_planes, cells), BF16),
            pltpu.VMEM((tiles + 2, planes, LANES), F32),
            pltpu.VMEM((tiles, planes, LANES), F32),
            dma((2,)),
            dma((stains, s_parts)),
            dma((stains, f_parts)),
            dma((u_parts,)),
        ]

    tall = depth // 8
    middle = pl.pallas_call(
        functools.partial(inner_kernel, depth),
        out_shape=sds((3, tiles, depth - 16, LANES), F32),
        in_specs=[HBM] * 6,
        out_specs=VMEM,
        scratch_shapes=force_scratch(depth, depth, depth - 16, tall, 1, tall - 2),
        compiler_params=params(64),
        cost_estimate=pl.CostEstimate(flops=4 * 10**8, bytes_accessed=10 << 20, transcendentals=0),
        name="inner_force",
    )(order, owner, subject5, template, recv, moved5)

    edge, even_send, odd_send = pl.pallas_call(
        functools.partial(edge_kernel, depth),
        out_shape=(
            sds((3, tiles, 16, LANES), F32),
            sds((3, SWEEPS, cells), F32),
            sds((3, SWEEPS, cells), F32),
        ),
        in_specs=[HBM, HBM, VMEM, VMEM, HBM, HBM, HBM, HBM, ANY],
        out_specs=(VMEM, VMEM, VMEM),
        scratch_shapes=force_scratch(48, 32, 16, 4, 2, 2),
        compiler_params=params(64),
        cost_estimate=pl.CostEstimate(flops=10**8, bytes_accessed=8 << 20, transcendentals=0),
        name="edge_force",
    )(order, owner, even_recv, odd_recv, subject5, template, recv, moved5, middle)

    u_even = lax.ppermute(even_send, "depth", even_pairs)
    u_odd = lax.ppermute(odd_send, "depth", odd_pairs)

    inside = pl.pallas_call(
        functools.partial(sweep_kernel, depth),
        out_shape=sds(displacement.shape, F32),
        in_specs=[ANY, ANY],
        out_specs=ANY,
        scratch_shapes=[
            pltpu.VMEM((3, tiles, depth + 16, LANES), F32),
            pltpu.VMEM((3, tiles, depth + 16, LANES), F32),
            pltpu.VMEM((3, tiles + 2, depth, LANES), F32),
            pltpu.VMEM((3, depth, cells), F32),
            dma((3, 3)),
            dma((3,)),
        ],
        compiler_params=params(64),
        cost_estimate=pl.CostEstimate(flops=10**9, bytes_accessed=40 << 20, transcendentals=0),
        name="sweeps",
    )(middle, edge)

    return pl.pallas_call(
        functools.partial(seam_kernel, depth),
        out_shape=sds(displacement.shape, F32),
        in_specs=[ANY, VMEM, VMEM, ANY],
        out_specs=ANY,
        scratch_shapes=[
            pltpu.VMEM((3, tiles, 40, LANES), F32),
            pltpu.VMEM((3, tiles, 40, LANES), F32),
            pltpu.VMEM((3, tiles + 2, 24, LANES), F32),
            pltpu.VMEM((2, 3, 8, cells), F32),
            dma((4,)),
        ],
        input_output_aliases={3: 0},
        compiler_params=params(64),
        name="seam_sweeps",
    )(edge, u_even, u_odd, inside)


def solution(mesh):
    placed = (
        P("subj", None, "depth", None),
        P(),
        P(("grp", "subj"), None),
        P(("grp", "subj"), None, "depth", None),
        P(("grp", "subj"), None, "depth", None),
    )
    return jax.shard_map(
        local,
        mesh=mesh,
        in_specs=placed,
        out_specs=P(("grp", "subj"), None, "depth", None),
        check_vma=False,
    )
```

time: 44.1 us -> 39.2 us (0.89)
  local copies, waits for them, and re-layouts: 7.1 us -> 1.29 us
  waiting for transfers between devices: 4.81 us -> 0.01 us
  Pallas kernels: 22.9 us -> 27.5 us
  other arithmetic: 0.09 us -> 0.73 us
    unnamed x12 -> x0, local copies, waits for them, and re-layouts: 5.81 us -> none
    pallas_call x1 -> x2, Pallas kernels: 12.6 us -> 16.5 us  [the longest x1 8.76 us: local(): pl.pallas_call(functools.partial(inner_kernel, depth), out_shape=sds((3,...]
    ppermute x1, waiting for transfers between devices: 3.51 us -> 0.01 us  [local(): odd_recv = lax.ppermute(jnp.where(even, first, final), 'depth', odd_pairs)]
    ppermute x1, waiting for transfers between devices: 1.3 us -> 0.01 us  [local(): even_recv = lax.ppermute(jnp.where(even, final, first), 'depth', even_pairs)]
    ppermute x1, starting transfers between devices: 0.57 us -> 1.7 us  [local(): u_even = lax.ppermute(even_send, 'depth', even_pairs)]
    ppermute x1, starting transfers between devices: 4.43 us -> 3.48 us  [local(): u_odd = lax.ppermute(odd_send, 'depth', odd_pairs)]
    select_n x1, other arithmetic: 0.09 us -> 0.73 us  [local(): odd_recv = lax.ppermute(jnp.where(even, first, final), 'depth', odd_pairs)]
    pallas_call x1, Pallas kernels: 5.52 us -> 6.12 us  [local(): pl.pallas_call(functools.partial(edge_kernel, depth), out_shape=(sds((3,...]
  transfers between devices with their start and end apart: 5 -> 5, of which waited for: 2 -> 0; matrix products, arithmetic and copies ran while one was open for 3% -> 5% of each run, Pallas kernels for 29% -> 42%
where the time goes in v2:
time: 39.2 us; the launch traced here: 38.9 us
  Pallas kernels  27.5 us (70%)
  starting transfers between devices  9.06 us (23%)
  local copies, waits for them, and re-layouts  1.29 us (3%)
  other arithmetic  0.73 us (2%)
    pallas_call x1, Pallas kernels, local(): pl.pallas_call(functools.partial(inner_kernel, depth), out_shape=sds((3,...  8.76 us
    pallas_call x1, Pallas kernels, local(): pl.pallas_call(functools.partial(sweep_kernel, depth), out_shape=sds(disp...  7.69 us
    pallas_call x1, Pallas kernels, local(): pl.pallas_call(functools.partial(edge_kernel, depth), out_shape=(sds((3,...  6.12 us
    pallas_call x1, Pallas kernels, local(): pl.pallas_call(functools.partial(seam_kernel, depth), out_shape=sds(displ...  4.97 us
    ppermute x1, starting transfers between devices, local(): u_odd = lax.ppermute(odd_send, 'depth', odd_pairs)  3.48 us
    ppermute x1, starting transfers between devices, local(): odd_recv = lax.ppermute(jnp.where(even, first, final), 'depth', odd_pairs)  3.42 us
    ppermute x1, starting transfers between devices, local(): u_even = lax.ppermute(even_send, 'depth', even_pairs)  1.7 us
    slice x1, local copies, waits for them, and re-layouts, local(): first, final = (subject[0, :, 0, :], subject[0, :, depth - 1, :])  1.29 us
  transfers between devices with their start and end apart: 5, of which 0 were waited for; matrix products, arithmetic and copies ran while one was open for 5% of the time, Pallas kernels for 42%

profile of v2, /device:TPU:12, one launch (start us, length us, event | category | flops | bytes accessed | tf_op | source)
XLA Modules:
  0.0 38.9 jit_solution(15552780269961844666)
XLA Ops:
  0.0 0.0 collective-permute-start.2
  0.0 1.3 %fusion = (f32[1,4,1,4096]{3,2,1,0:T(1,128)S(1)}, f32[1,4,1,4096]{3,2,1,0:T(1,128)S(1)}) fusion(f32[1,4,64,4096]{3,2,1,0:T(8,128)} %param.8), kind=kLoop, calls=%fused_computation.2 | loop fusion | bytes 262144 | tf_op jit(solution)/shard_map/slice | solution.py:351
  1.3 0.7 %select_bitcast_fusion = (f32[4,4096]{1,0:T(4,128)}, f32[4,4096]{1,0:T(4,128)}) fusion(f32[1,4,1,4096]{3,2,1,0:T(1,128)S(1)} %get-tuple-element.12, f32[1,4,1,4096]{3,2,1,0:T(1,128)S(1)} %get-tuple-element.11, pred[]{:T(512)S(6)} %eq.5), kind=kLoop, calls=%fused_computation | loop fusion | flops 32768 | bytes 262145 | tf_op jit(solution)/shard_map/jit(_where)/select_n | solution.py:353
  2.0 3.4 %collective-permute-start.1 = (f32[4,4096]{1,0:T(4,128)}, f32[4,4096]{1,0:T(4,128)}, u32[]{:S(2)}, u32[]{:S(2)}) collective-permute-start(f32[4,4096]{1,0:T(4,128)} %get-tuple-element.13), channel_id=1, source_target_pairs={{1,2},{2,1},{3,4},{4,3},{5,6},{6,5},{9,10},{10,9},{11,12},{12,11},... | collective-permute-start | bytes 196616 | tf_op jit(solution)/shard_map/ppermute | solution.py:353
  5.5 0.5 %collective-permute-start = (f32[4,4096]{1,0:T(4,128)}, f32[4,4096]{1,0:T(4,128)}, u32[]{:S(2)}, u32[]{:S(2)}) collective-permute-start(f32[4,4096]{1,0:T(4,128)} %get-tuple-element.14), channel_id=1, source_target_pairs={{0,1},{1,0},{2,3},{3,2},{4,5},{5,4},{6,7},{7,6},{8,9},{9,8},{10,11... | collective-permute-start | bytes 196616 | tf_op jit(solution)/shard_map/ppermute | solution.py:352
  5.9 0.0 collective-permute-done.2.recv
  5.9 8.8 %inner_force.1.middle = f32[3,32,48,128]{3,2,1,0:T(8,128)} custom-call(s32[1,4]{1,0:T(1,128)} %order_hbm.3, s32[4]{0:T(128)} %owner_hbm.3, f32[4,8,32,8,128]{4,3,2,1,0:T(8,128)} %bitcast.10, bf16[1,4,64,4096]{3,2,1,0:T(8,128)(2,1)} %own.3, bf16[1,4,64,4096]{3,2,1,0:T(8,128)(2,1)} %collective-permute-done.2.recv, f32[3,8,32,8,128]{4,3,2,1,0:T(8,128)} %bitcast.12), custom_call_target="tpu_custom_call" | custom-call | flops 400000000 | bytes 10485760 | tf_op jit(solution)/shard_map/inner_force/pallas_call | solution.py:377
  14.7 0.0 collective-permute-done.1.odd_recv
  14.7 0.0 collective-permute-done.even_recv
  14.7 6.1 %edge_force.1 = (f32[3,32,16,128]{3,2,1,0:T(8,128)}, f32[3,4,4096]{2,1,0:T(4,128)}, f32[3,4,4096]{2,1,0:T(4,128)}) custom-call(s32[1,4]{1,0:T(1,128)} %order_hbm.3, s32[4]{0:T(128)} %owner_hbm.3, f32[4,4096]{1,0:T(4,128)} %collective-permute-done.even_recv, f32[4,4096]{1,0:T(4,128)} %collective-permute-done.1.odd_recv, f32[4,8,32,8,128]{4,3,2,1,0:T(8,128)} %bitcast.11, ...), custom_call_target="tpu_custom_call" | custom-call | flops 100000000 | bytes 8388608 | tf_op jit(solution)/shard_map/edge_force/pallas_call | solution.py:388
  20.8 1.7 %collective-permute-start.3 = (f32[3,4,4096]{2,1,0:T(4,128)}, f32[3,4,4096]{2,1,0:T(4,128)}, u32[]{:S(2)}, u32[]{:S(2)}) collective-permute-start(f32[3,4,4096]{2,1,0:T(4,128)} %get-tuple-element.9), channel_id=1, source_target_pairs={{0,1},{1,0},{2,3},{3,2},{4,5},{5,4},{6,7},{7,6},{8,9},{9,8},{10,11... | collective-permute-start | bytes 589832 | tf_op jit(solution)/shard_map/ppermute | solution.py:403
  22.5 3.5 %collective-permute-start.4 = (f32[3,4,4096]{2,1,0:T(4,128)}, f32[3,4,4096]{2,1,0:T(4,128)}, u32[]{:S(2)}, u32[]{:S(2)}) collective-permute-start(f32[3,4,4096]{2,1,0:T(4,128)} %get-tuple-element.10), channel_id=1, source_target_pairs={{1,2},{2,1},{3,4},{4,3},{5,6},{6,5},{9,10},{10,9},{11,12},{12,11},... | collective-permute-start | bytes 589832 | tf_op jit(solution)/shard_map/ppermute | solution.py:404
  26.0 7.7 %sweeps.1.before = f32[1,3,64,4096]{3,2,1,0:T(8,128)} custom-call(f32[3,32,48,128]{3,2,1,0:T(8,128)} %inner_force.1.middle, f32[3,32,16,128]{3,2,1,0:T(8,128)} %get-tuple-element.8.edge), custom_call_target="tpu_custom_call" | custom-call | flops 1000000000 | bytes 41943040 | tf_op jit(solution)/shard_map/sweeps/pallas_call | solution.py:406
  33.7 0.0 collective-permute-done.3.even_recv
  33.7 0.0 collective-permute-done.4.odd_recv
  33.7 5.0 %seam_sweeps.1 = f32[1,3,64,4096]{3,2,1,0:T(8,128)} custom-call(f32[3,32,16,128]{3,2,1,0:T(8,128)} %get-tuple-element.8.edge, f32[3,4,4096]{2,1,0:T(4,128)} %collective-permute-done.3.even_recv, f32[3,4,4096]{2,1,0:T(4,128)} %collective-permute-done.4.odd_recv, f32[1,3,64,4096]{3,2,1,0:T(8,128)} %sweeps.1.before), custom_call_target="tpu_custom_call", output_to_operand_aliasing={{}: (3, {})} | custom-call | tf_op jit(solution)/shard_map/seam_sweeps/pallas_call | solution.py:424
Async XLA Ops:
  0.0 5.9 %collective-permute-start.2 = (bf16[1,4,64,4096]{3,2,1,0:T(8,128)(2,1)}, bf16[1,4,64,4096]{3,2,1,0:T(8,128)(2,1)}, u32[]{:S(2)}, u32[]{:S(2)}) collective-permute-start(bf16[1,4,64,4096]{3,2,1,0:T(8,128)(2,1)} %own.3), channel_id=1, source_target_pairs={{0,8},{8,0},{1,9},{9,1},{2,10},{10,2},{3,11},{11,3},{4,12},{12,4},... | collective-permute-start | bytes 6291464 | tf_op jit(solution)/shard_map/ppermute | solution.py:350
  2.0 12.7 %collective-permute-start.1 = (f32[4,4096]{1,0:T(4,128)}, f32[4,4096]{1,0:T(4,128)}, u32[]{:S(2)}, u32[]{:S(2)}) collective-permute-start(f32[4,4096]{1,0:T(4,128)} %get-tuple-element.13), channel_id=1, source_target_pairs={{1,2},{2,1},{3,4},{4,3},{5,6},{6,5},{9,10},{10,9},{11,12},{12,11},... | collective-permute-start | bytes 196616 | tf_op jit(solution)/shard_map/ppermute | solution.py:353
  5.5 9.2 %collective-permute-start = (f32[4,4096]{1,0:T(4,128)}, f32[4,4096]{1,0:T(4,128)}, u32[]{:S(2)}, u32[]{:S(2)}) collective-permute-start(f32[4,4096]{1,0:T(4,128)} %get-tuple-element.14), channel_id=1, source_target_pairs={{0,1},{1,0},{2,3},{3,2},{4,5},{5,4},{6,7},{7,6},{8,9},{9,8},{10,11... | collective-permute-start | bytes 196616 | tf_op jit(solution)/shard_map/ppermute | solution.py:352
  20.8 12.9 %collective-permute-start.3 = (f32[3,4,4096]{2,1,0:T(4,128)}, f32[3,4,4096]{2,1,0:T(4,128)}, u32[]{:S(2)}, u32[]{:S(2)}) collective-permute-start(f32[3,4,4096]{2,1,0:T(4,128)} %get-tuple-element.9), channel_id=1, source_target_pairs={{0,1},{1,0},{2,3},{3,2},{4,5},{5,4},{6,7},{7,6},{8,9},{9,8},{10,11... | collective-permute-start | bytes 589832 | tf_op jit(solution)/shard_map/ppermute | solution.py:403
  22.5 11.2 %collective-permute-start.4 = (f32[3,4,4096]{2,1,0:T(4,128)}, f32[3,4,4096]{2,1,0:T(4,128)}, u32[]{:S(2)}, u32[]{:S(2)}) collective-permute-start(f32[3,4,4096]{2,1,0:T(4,128)} %get-tuple-element.10), channel_id=1, source_target_pairs={{1,2},{2,1},{3,4},{4,3},{5,6},{6,5},{9,10},{10,9},{11,12},{12,11},... | collective-permute-start | bytes 589832 | tf_op jit(solution)/shard_map/ppermute | solution.py:404

commit v3 on v2

v3 whole, which is shorter than its diff:
```python
import functools

import jax
import jax.numpy as jnp
from jax import lax
from jax.experimental import pallas as pl
from jax.experimental.pallas import tpu as pltpu
from jax.sharding import PartitionSpec as P

GY = 64
SWEEPS = 4
LANES = 128
RATE = 0.15
F32 = jnp.float32
BF16 = jnp.bfloat16
LIMIT = 48
LOAD = 46

ANY = pl.BlockSpec(memory_space=pl.ANY)
HBM = pl.BlockSpec(memory_space=pltpu.HBM)
VMEM = pl.BlockSpec(memory_space=pltpu.VMEM)


def params(mib):
    return pltpu.CompilerParams(vmem_limit_bytes=mib << 20)


def pair_swaps(count):
    def swaps(first):
        return [p for i in range(first, count - 1, 2) for p in ((i, i + 1), (i + 1, i))]

    return swaps(0), swaps(1)


def lateral_matrix(difference):
    row = lax.broadcasted_iota(jnp.int32, (2 * LANES, 2 * LANES), 0) & (LANES - 1)
    col = lax.broadcasted_iota(jnp.int32, (2 * LANES, 2 * LANES), 1)
    right = col >= LANES
    col = col & (LANES - 1)
    swap = jnp.where((row ^ col) == GY, 1.0, 0.0)
    same = (row & GY) == (col & GY)
    plus = jnp.where((row == col + 1) & same, 1.0, 0.0)
    minus = jnp.where((row == col - 1) & same, 1.0, 0.0)
    left = plus - minus if difference else plus + minus + swap
    return jnp.where(right, swap, left).astype(BF16)


def lateral(x, matrix):
    high = x.astype(BF16)
    low = (x - high.astype(F32)).astype(BF16)
    return jnp.dot(jnp.concatenate([high, low], 1), matrix, preferred_element_type=F32)


def low_half(rows):
    return lax.broadcasted_iota(jnp.int32, (rows, LANES), 1) < GY


def pieces_of(start, rows):
    done = start
    while done < start + rows:
        block = done // 16 * 16
        stop = min(block + 16, start + rows)
        yield block, done - block, stop - done
        done = stop


def force_stain(s_ref, k, regions, f_ref, u_ref, r_ref, y_ref, matrix):
    tiles = s_ref.shape[1]
    parts = [s_ref[k, :, s0 : s0 + n, :] for s0, _, _, n in regions]
    x = parts[0] if len(parts) == 1 else jnp.concatenate(parts, 1)
    total = x.shape[1]
    p = lateral(x.reshape(tiles * total, LANES), matrix)
    y_ref[...] = p[:, :LANES].reshape(tiles, total, LANES)
    r_ref[1 : tiles + 1] = p[:, LANES:].reshape(tiles, total, LANES)
    base = 0
    for s0, f0, u0, n in regions:
        for block, skip, count in pieces_of(f0, n):
            z = block + skip - f0
            rows = slice(base + z, base + z + count)
            at = slice(u0 + z, u0 + z + count)
            s = s0 + z
            lo = low_half(count)
            r_now = r_ref[1, rows, :]
            before = jnp.where(lo, r_ref[0, rows, :], r_now)
            for c in range(tiles):
                r_next = r_ref[c + 2, rows, :]
                after = jnp.where(lo, r_now, r_next)
                gx = after - before
                before, r_now = after, r_next
                gy = y_ref[c, rows, :]
                gz = s_ref[k, c, s + 1 : s + 1 + count, :] - s_ref[k, c, s - 1 : s - 1 + count, :]
                fixed = f_ref[k, block : block + 16, c * LANES : (c + 1) * LANES].astype(F32)
                fixed = fixed[skip : skip + count]
                ux, uy, uz = u_ref[0, c, at, :], u_ref[1, c, at, :], u_ref[2, c, at, :]
                moved = (gx * ux + gy * uy) + gz * uz
                twice = (fixed - s_ref[k, c, s : s + count, :]) * 2.0 - moved
                denom = (gx * gx + gy * gy) + (gz * gz + (twice * twice + 2.0))
                w = twice * inverse(denom)
                u_ref[0, c, at, :] = ux + w * gx
                u_ref[1, c, at, :] = uy + w * gy
                u_ref[2, c, at, :] = uz + w * gz
        base += n


def inverse(x):
    r = pl.reciprocal(x, approx=True)
    return r * (2.0 - x * r)


def sweep(src, store, q, z0, rows, r_ref, matrix):
    tiles = src.shape[1]
    x = src[q, :, z0 : z0 + rows, :].reshape(tiles * rows, LANES)
    p = lateral(x, matrix)
    r_ref[q, 1 : tiles + 1] = p[:, LANES:].reshape(tiles, rows, LANES)
    inside = p[:, :LANES].reshape(tiles, rows, LANES)
    lo = low_half(rows)
    for c in range(tiles):
        depth = src[q, c, z0 - 1 : z0 - 1 + rows, :] + src[q, c, z0 + 1 : z0 + 1 + rows, :]
        across = jnp.where(lo, r_ref[q, c, :, :], r_ref[q, c + 2, :, :])
        store(c, src[q, c, z0 : z0 + rows, :] * (1.0 / RATE - 6.0) + depth + (inside[c] + across))


def clear_rim(ref, axis):
    shape = list(ref.shape)
    shape[axis] = 1
    at = [slice(None)] * len(shape)
    for i in (0, ref.shape[axis] - 1):
        at[axis] = slice(i, i + 1)
        ref[tuple(at)] = jnp.zeros(shape, F32)


def load_kernel(depth, subject, moved, own, s_ref, u_ref, own_ref, even_send, odd_send, s_sem, u_sem, o_sem):
    stains, tiles = s_ref.shape[:2]
    tall = depth // 8
    even = (lax.axis_index("depth") % 2) == 0

    def s_copy(t):
        return pltpu.make_async_copy(subject.at[:, t], s_ref.at[:, :, 8 + 8 * t : 16 + 8 * t, :], s_sem.at[t])

    def u_copy(t):
        return pltpu.make_async_copy(moved.at[:, t], u_ref.at[:, :, 8 + 8 * t : 16 + 8 * t, :], u_sem.at[t])

    order = (0, tall - 1) + tuple(range(1, tall - 1))
    for t in order:
        s_copy(t).start()
    for t in range(tall):
        u_copy(t).start()
    template = pltpu.make_async_copy(own.at[0], own_ref, o_sem)
    template.start()
    for z in (0, depth + 8):
        u_ref[:, :, z : z + 8, :] = jnp.zeros((3, tiles, 8, LANES), F32)
    for t in order[:2]:
        s_copy(t).wait()
    for k in range(stains):
        for c in range(tiles):
            at = slice(c * LANES, (c + 1) * LANES)
            low, high = s_ref[k, c, 8:9, :], s_ref[k, c, depth + 7 : depth + 8, :]
            even_send[k : k + 1, at] = jnp.where(even, high, low)
            odd_send[k : k + 1, at] = jnp.where(even, low, high)
    for t in order[2:]:
        s_copy(t).wait()
    for t in range(tall):
        u_copy(t).wait()
    template.wait()


def inner_kernel(depth, order_hbm, owner_hbm, s_ref, u_in, own, recv, f_ref, u_ref, order, owner, r_ref,
                 y_ref, o_sem, f_sem):
    stains = s_ref.shape[0]
    small = [
        pltpu.make_async_copy(order_hbm, order, o_sem.at[0]),
        pltpu.make_async_copy(owner_hbm, owner, o_sem.at[1]),
    ]
    for copy in small:
        copy.start()
    clear_rim(r_ref, 0)
    matrix = lateral_matrix(True)
    for copy in small:
        copy.wait()

    def f_copy(source, k):
        return pltpu.make_async_copy(source, f_ref.at[k], f_sem.at[k])

    for j in range(stains):
        k = order[0, j]
        mine = owner[k] == lax.axis_index("subj")

        @pl.when(mine)
        def _():
            f_copy(own.at[k], k).start()

        @pl.when(jnp.logical_not(mine))
        def _():
            f_copy(recv.at[0, k], k).start()

    for j in range(stains):
        k = order[0, j]
        f_copy(own.at[k], k).wait()
        force_stain(s_ref, k, ((16, 8, 16, depth - 16),), f_ref, u_ref, r_ref, y_ref, matrix)


def edge_kernel(depth, order_hbm, even_recv, odd_recv, s_in, f_ref, u_in, s_ref, u_ref, even_send, odd_send,
                order, r_ref, y_ref, o_sem):
    stains, tiles = s_ref.shape[:2]
    copy = pltpu.make_async_copy(order_hbm, order, o_sem)
    copy.start()
    even = (lax.axis_index("depth") % 2) == 0
    clear_rim(r_ref, 0)
    matrix = lateral_matrix(True)
    for c in range(tiles):
        at = slice(c * LANES, (c + 1) * LANES)
        a, b = even_recv[:, at], odd_recv[:, at]
        low, high = jnp.where(even, b, a), jnp.where(even, a, b)
        for k in range(stains):
            s_ref[k, c, 7:8, :] = low[k : k + 1]
            s_ref[k, c, depth + 8 : depth + 9, :] = high[k : k + 1]
    copy.wait()
    for j in range(stains):
        regions = ((8, 0, 8, 8), (depth, depth - 8, depth, 8))
        force_stain(s_ref, order[0, j], regions, f_ref, u_ref, r_ref, y_ref, matrix)
    n = SWEEPS
    for q in range(3):
        for c in range(tiles):
            at = slice(c * LANES, (c + 1) * LANES)
            low, high = u_ref[q, c, 8 : 8 + n, :], u_ref[q, c, 8 + depth - n : 8 + depth, :]
            even_send[q, :, at] = jnp.where(even, high, low)
            odd_send[q, :, at] = jnp.where(even, low, high)


def sweep_kernel(depth, u_ref, out, a_ref, b_ref, r_ref, o_ref, o_sem):
    tiles = a_ref.shape[1]
    clear_rim(r_ref, 1)
    for ref in (a_ref, b_ref):
        for z in (0, depth + 8):
            ref[:, :, z : z + 8, :] = jnp.zeros((3, tiles, 8, LANES), F32)
    matrix = lateral_matrix(False)
    src, dst = u_ref, a_ref
    for i in range(SWEEPS):
        final = i == SWEEPS - 1
        for q in range(3):

            def store(c, value, q=q, dst=dst, final=final):
                if final:
                    o_ref[q, :, c * LANES : (c + 1) * LANES] = value * RATE**SWEEPS
                else:
                    dst[q, c, 8 : 8 + depth, :] = value

            sweep(src, store, q, 8, depth, r_ref, matrix)
            if final:
                pltpu.make_async_copy(o_ref.at[q], out.at[0, q], o_sem.at[q]).start()
        src, dst = dst, (b_ref if dst is a_ref else a_ref)
    for q in range(3):
        pltpu.make_async_copy(o_ref.at[q], out.at[0, q], o_sem.at[q]).wait()


def seam_kernel(depth, u_ref, even_recv, odd_recv, before, out, a_ref, b_ref, r_ref, o_ref, sem):
    tiles = u_ref.shape[1]
    at_depth = lax.axis_index("depth")
    even = (at_depth % 2) == 0
    has_low = at_depth > 0
    has_high = at_depth < lax.axis_size("depth") - 1
    ends = (0, depth - 8)
    ins = [
        pltpu.make_async_copy(before.at[0, :, z : z + 8, :], o_ref.at[i], sem.at[i]) for i, z in enumerate(ends)
    ]
    outs = [
        pltpu.make_async_copy(o_ref.at[i, q], out.at[0, q, z : z + 8, :], sem.at[2 + 2 * q + i])
        for q in range(3)
        for i, z in enumerate(ends)
    ]
    for copy in ins:
        copy.start()
    clear_rim(r_ref, 1)
    n = SWEEPS
    for q in range(3):
        for ref in (a_ref, b_ref):
            for z in (0, 32):
                ref[q, :, z : z + 8, :] = jnp.zeros((tiles, 8, LANES), F32)
        a_ref[q, :, 8:16, :] = u_ref[q, :, depth : depth + 8, :]
        a_ref[q, :, 24:32, :] = u_ref[q, :, 8:16, :]
        for c in range(tiles):
            at = slice(c * LANES, (c + 1) * LANES)
            x, y = even_recv[q, :, at], odd_recv[q, :, at]
            a_ref[q, c, 16 : 16 + n, :] = jnp.where(even, x, y)
            a_ref[q, c, 20 : 20 + n, :] = jnp.where(even, y, x)
    row = lax.broadcasted_iota(jnp.int32, (24, LANES), 0)
    keep = jnp.where((row >= 8) & (row < 12), jnp.where(has_high, 1.0, 0.0), 1.0)
    keep = jnp.where((row >= 12) & (row < 16), jnp.where(has_low, 1.0, 0.0), keep)
    top = lax.broadcasted_iota(jnp.int32, (8, LANES), 0) < 4
    matrix = lateral_matrix(False)
    src, dst = a_ref, b_ref
    for i in range(SWEEPS):
        final = i == SWEEPS - 1
        if final:
            for copy in ins:
                copy.wait()
        for q in range(3):

            def store(c, value, q=q, dst=dst, final=final):
                at = slice(c * LANES, (c + 1) * LANES)
                if final:
                    value = value * RATE**SWEEPS
                    o_ref[0, q, :, at] = jnp.where(top, value[16:24], o_ref[0, q, :, at])
                    o_ref[1, q, :, at] = jnp.where(top, o_ref[1, q, :, at], value[0:8])
                else:
                    dst[q, c, 8:32, :] = value * keep

            sweep(src, store, q, 8, 24, r_ref, matrix)
            if final:
                for copy in outs[2 * q : 2 * q + 2]:
                    copy.start()
        src, dst = dst, src
    for copy in outs:
        copy.wait()


def local(template, owner, order, subject, displacement):
    stains, depth, cells = subject.shape[1:]
    tiles = cells // LANES
    count = lax.axis_size("depth")
    even_pairs, odd_pairs = pair_swaps(count)

    recv = lax.ppermute(template, "subj", [(0, 1), (1, 0)])

    def tiled(a):
        return a.reshape(a.shape[1], depth // 8, 8, tiles, LANES).transpose(0, 1, 3, 2, 4)

    subject5, moved5 = tiled(subject), tiled(displacement)
    sds = jax.ShapeDtypeStruct
    dma = pltpu.SemaphoreType.DMA

    tall = depth // 8
    s_type = pltpu.VMEM((stains, tiles, depth + 16, LANES), F32)
    f_type = pltpu.VMEM((stains, depth, cells), BF16)
    u_type = pltpu.VMEM((3, tiles, depth + 16, LANES), F32)
    send_type = pltpu.VMEM((3, SWEEPS, cells), F32)

    def force_scratch(planes):
        return [pltpu.VMEM((tiles + 2, planes, LANES), F32), pltpu.VMEM((tiles, planes, LANES), F32)]

    plane_type = pltpu.VMEM((stains, cells), F32)
    s, u, own, even_send, odd_send = pl.pallas_call(
        functools.partial(load_kernel, depth),
        out_shape=(s_type, u_type, f_type, plane_type, plane_type),
        in_specs=[HBM] * 3,
        out_specs=(VMEM,) * 5,
        scratch_shapes=[dma((tall,)), dma((tall,)), dma],
        compiler_params=params(LOAD),
        name="load",
    )(subject5, moved5, template)

    even_recv = lax.ppermute(even_send, "depth", even_pairs)
    odd_recv = lax.ppermute(odd_send, "depth", odd_pairs)

    f, u = pl.pallas_call(
        functools.partial(inner_kernel, depth),
        out_shape=(f_type, u_type),
        in_specs=[HBM, HBM, VMEM, VMEM, VMEM, ANY],
        out_specs=(VMEM, VMEM),
        scratch_shapes=[pltpu.SMEM(order.shape, jnp.int32), pltpu.SMEM(owner.shape, jnp.int32)]
        + force_scratch(depth - 16)
        + [dma((2,)), dma((stains,))],
        input_output_aliases={3: 1},
        compiler_params=params(20),
        cost_estimate=pl.CostEstimate(flops=4 * 10**8, bytes_accessed=10 << 20, transcendentals=0),
        name="inner_force",
    )(order, owner, s, u, own, recv)

    s, u, even_send, odd_send = pl.pallas_call(
        functools.partial(edge_kernel, depth),
        out_shape=(s_type, u_type, send_type, send_type),
        in_specs=[HBM, VMEM, VMEM, VMEM, VMEM, VMEM],
        out_specs=(VMEM, VMEM, VMEM, VMEM),
        scratch_shapes=[pltpu.SMEM(order.shape, jnp.int32)] + force_scratch(16) + [dma],
        input_output_aliases={3: 0, 5: 1},
        compiler_params=params(20),
        cost_estimate=pl.CostEstimate(flops=10**8, bytes_accessed=8 << 20, transcendentals=0),
        name="edge_force",
    )(order, even_recv, odd_recv, s, f, u)

    u_even = lax.ppermute(even_send, "depth", even_pairs)
    u_odd = lax.ppermute(odd_send, "depth", odd_pairs)

    inside = pl.pallas_call(
        functools.partial(sweep_kernel, depth),
        out_shape=sds(displacement.shape, F32),
        in_specs=[VMEM],
        out_specs=ANY,
        scratch_shapes=[
            pltpu.VMEM((3, tiles, depth + 16, LANES), F32),
            pltpu.VMEM((3, tiles, depth + 16, LANES), F32),
            pltpu.VMEM((3, tiles + 2, depth, LANES), F32),
            pltpu.VMEM((3, depth, cells), F32),
            dma((3,)),
        ],
        compiler_params=params(LIMIT),
        cost_estimate=pl.CostEstimate(flops=10**9, bytes_accessed=40 << 20, transcendentals=0),
        name="sweeps",
    )(u)

    return pl.pallas_call(
        functools.partial(seam_kernel, depth),
        out_shape=sds(displacement.shape, F32),
        in_specs=[VMEM, VMEM, VMEM, ANY],
        out_specs=ANY,
        scratch_shapes=[
            pltpu.VMEM((3, tiles, 40, LANES), F32),
            pltpu.VMEM((3, tiles, 40, LANES), F32),
            pltpu.VMEM((3, tiles + 2, 24, LANES), F32),
            pltpu.VMEM((2, 3, 8, cells), F32),
            dma((8,)),
        ],
        input_output_aliases={3: 0},
        compiler_params=params(LIMIT),
        name="seam_sweeps",
    )(u, u_even, u_odd, inside)


def solution(mesh):
    placed = (
        P("subj", None, "depth", None),
        P(),
        P(("grp", "subj"), None),
        P(("grp", "subj"), None, "depth", None),
        P(("grp", "subj"), None, "depth", None),
    )
    return jax.shard_map(
        local,
        mesh=mesh,
        in_specs=placed,
        out_specs=P(("grp", "subj"), None, "depth", None),
        check_vma=False,
    )
```

time: 39.2 us -> 31.1 us (0.79)
  Pallas kernels: 27.5 us -> 20 us
  local copies, waits for them, and re-layouts: 1.29 us -> 0.01 us
  starting transfers between devices: 9.06 us -> 10.2 us
  other arithmetic: 0.73 us -> 0 us
    pallas_call x2 -> x3, Pallas kernels: 14.9 us -> 10.9 us  [the longest x1 4.94 us: local(): pl.pallas_call(functools.partial(inner_kernel, depth), out_shape=(f_type,...]
    pallas_call x1, Pallas kernels: 7.69 us -> 5.85 us  [local(): pl.pallas_call(functools.partial(sweep_kernel, depth), out_shape=sds(disp...]
    pallas_call x1, Pallas kernels: 4.97 us -> 3.27 us  [local(): pl.pallas_call(functools.partial(seam_kernel, depth), out_shape=sds(displ...]
    ppermute x1, starting transfers between devices: 1.7 us -> 0.07 us  [local(): u_even = lax.ppermute(even_send, 'depth', even_pairs)]
    ppermute x1, starting transfers between devices: 3.48 us -> 5.1 us  [local(): u_odd = lax.ppermute(odd_send, 'depth', odd_pairs)]
    slice x1 -> x0, local copies, waits for them, and re-layouts: 1.29 us -> none  [local(): first, final = (subject[0, :, 0, :], subject[0, :, depth - 1, :])]
    ppermute x2, starting transfers between devices: 3.87 us -> 5 us  [the longest x1 4.43 us: local(): odd_recv = lax.ppermute(odd_send, 'depth', odd_pairs)]
    select_n x1 -> x0, other arithmetic: 0.73 us -> none  [local(): odd_recv = lax.ppermute(jnp.where(even, first, final), 'depth', odd_pairs)]
  transfers between devices with their start and end apart: 5 -> 5, of which waited for: 0 -> 0; matrix products, arithmetic and copies ran while one was open for 5% -> 0% of each run, Pallas kernels for 42% -> 48%
where the time goes in v3:
time: 31.1 us; the launch traced here: 30.5 us
  Pallas kernels  20 us (64%)
  starting transfers between devices  10.2 us (33%)
    pallas_call x1, Pallas kernels, local(): pl.pallas_call(functools.partial(sweep_kernel, depth), out_shape=sds(disp...  5.85 us
    ppermute x1, starting transfers between devices, local(): u_odd = lax.ppermute(odd_send, 'depth', odd_pairs)  5.1 us
    pallas_call x1, Pallas kernels, local(): pl.pallas_call(functools.partial(inner_kernel, depth), out_shape=(f_type,...  4.94 us
    ppermute x1, starting transfers between devices, local(): odd_recv = lax.ppermute(odd_send, 'depth', odd_pairs)  4.43 us
    pallas_call x1, Pallas kernels, local(): pl.pallas_call(functools.partial(load_kernel, depth), out_shape=(s_type,...  3.99 us
    pallas_call x1, Pallas kernels, local(): pl.pallas_call(functools.partial(seam_kernel, depth), out_shape=sds(displ...  3.27 us
    pallas_call x1, Pallas kernels, local(): pl.pallas_call(functools.partial(edge_kernel, depth), out_shape=(s_type,...  1.97 us
  transfers between devices with their start and end apart: 5, of which 0 were waited for; matrix products, arithmetic and copies ran while one was open for 0% of the time, Pallas kernels for 48%

profile of v3, /device:TPU:12, one launch (start us, length us, event | category | flops | bytes accessed | tf_op | source)
XLA Modules:
  0.0 30.5 jit_solution(3808439132372610019)
XLA Ops:
  0.0 0.0 collective-permute-start.2
  0.0 0.0 copy-start
  0.0 0.0 copy-start.1
  0.0 4.0 %load.1 = (f32[4,32,80,128]{3,2,1,0:T(8,128)S(1)}, f32[3,32,80,128]{3,2,1,0:T(8,128)S(1)}, bf16[4,64,4096]{2,1,0:T(8,128)(2,1)S(1)}, f32[4,4096]{1,0:T(4,128)S(1)}, f32[4,4096]{1,0:T(4,128)S(1)}) custom-call(f32[4,8,32,8,128]{4,3,2,1,0:T(8,128)} %bitcast.6, f32[3,8,32,8,128]{4,3,2,1,0:T(8,128)} %bitcast.7, bf16[1,4,64,4096]{3,2,1,0:T(8,128)(2,1)} %own.1), custom_call_target="tpu_custom_call" | custom-call | tf_op jit(solution)/shard_map/load/pallas_call | solution.py:342
  4.0 0.6 %collective-permute-start = (f32[4,4096]{1,0:T(4,128)S(1)}, f32[4,4096]{1,0:T(4,128)S(1)}, u32[]{:S(2)}, u32[]{:S(2)}) collective-permute-start(f32[4,4096]{1,0:T(4,128)S(1)} %get-tuple-element.15), channel_id=1, source_target_pairs={{0,1},{1,0},{2,3},{3,2},{4,5},{5,4},{6,7},{7,6},{8,9},{9,8},{10,11... | collective-permute-start | bytes 196616 | tf_op jit(solution)/shard_map/ppermute | solution.py:352
  4.6 4.4 %collective-permute-start.1 = (f32[4,4096]{1,0:T(4,128)S(1)}, f32[4,4096]{1,0:T(4,128)S(1)}, u32[]{:S(2)}, u32[]{:S(2)}) collective-permute-start(f32[4,4096]{1,0:T(4,128)S(1)} %get-tuple-element.16), channel_id=1, source_target_pairs={{1,2},{2,1},{3,4},{4,3},{5,6},{6,5},{9,10},{10,9},{11,12},{12,11},... | collective-permute-start | bytes 196616 | tf_op jit(solution)/shard_map/ppermute | solution.py:353
  9.0 0.0 collective-permute-done.2.recv
  9.0 0.0 copy-done
  9.0 0.0 copy-done.1
  9.0 4.9 %inner_force.1 = (bf16[4,64,4096]{2,1,0:T(8,128)(2,1)S(1)}, f32[3,32,80,128]{3,2,1,0:T(8,128)S(1)}) custom-call(s32[1,4]{1,0:T(1,128)S(1)} %copy-done, s32[4]{0:T(128)S(1)} %copy-done.1, f32[4,32,80,128]{3,2,1,0:T(8,128)S(1)} %get-tuple-element.17.s_ref.s_in, f32[3,32,80,128]{3,2,1,0:T(8,128)S(1)} %get-tuple-element.18.u_in, ...), custom_call_target="tpu_custom_call", output_to_operand_aliasing={{1}: (3, {})} | custom-call | flops 400000000 | bytes 10485760 | tf_op jit(solution)/shard_map/inner_force/pallas_call | solution.py:355
  14.0 0.0 collective-permute-done.even_recv
  14.0 0.0 collective-permute-done.1.odd_recv
  14.0 2.0 %edge_force.1 = (f32[4,32,80,128]{3,2,1,0:T(8,128)S(1)}, f32[3,32,80,128]{3,2,1,0:T(8,128)S(1)}, f32[3,4,4096]{2,1,0:T(4,128)S(1)}, f32[3,4,4096]{2,1,0:T(4,128)S(1)}) custom-call(s32[1,4]{1,0:T(1,128)S(1)} %copy-done, f32[4,4096]{1,0:T(4,128)S(1)} %collective-permute-done.even_recv, ...), custom_call_target="tpu_custom_call", output_to_operand_aliasing={{0}: (3, {}), {1}: (5, {})} | custom-call | flops 100000000 | bytes 8388608 | tf_op jit(solution)/shard_map/edge_force/pallas_call | solution.py:369
  16.0 0.1 collective-permute-start.3
  16.1 5.1 %collective-permute-start.4 = (f32[3,4,4096]{2,1,0:T(4,128)S(1)}, f32[3,4,4096]{2,1,0:T(4,128)S(1)}, u32[]{:S(2)}, u32[]{:S(2)}) collective-permute-start(f32[3,4,4096]{2,1,0:T(4,128)S(1)} %get-tuple-element.24), channel_id=1, source_target_pairs={{1,2},{2,1},{3,4},{4,3},{5,6},{6,5},{9,10},{10,9},{11,12},{12,11},... | collective-permute-start | bytes 589832 | tf_op jit(solution)/shard_map/ppermute | solution.py:382
  21.2 5.9 %sweeps.1.before = f32[1,3,64,4096]{3,2,1,0:T(8,128)} custom-call(f32[3,32,80,128]{3,2,1,0:T(8,128)S(1)} %get-tuple-element.22.u_ref), custom_call_target="tpu_custom_call" | custom-call | flops 1000000000 | bytes 41943040 | tf_op jit(solution)/shard_map/sweeps/pallas_call | solution.py:384
  27.0 0.0 collective-permute-done.3.even_recv
  27.1 0.0 collective-permute-done.4.odd_recv
  27.1 3.3 %seam_sweeps.1 = f32[1,3,64,4096]{3,2,1,0:T(8,128)} custom-call(f32[3,32,80,128]{3,2,1,0:T(8,128)S(1)} %get-tuple-element.22.u_ref, f32[3,4,4096]{2,1,0:T(4,128)S(1)} %collective-permute-done.3.even_recv, f32[3,4,4096]{2,1,0:T(4,128)S(1)} %collective-permute-done.4.odd_recv, f32[1,3,64,4096]{3,2,1,0:T(8,128)} %sweeps.1.before), custom_call_target="tpu_custom_call", output_to_operand_aliasing={{}: (3, {})} | custom-call | tf_op jit(solution)/shard_map/seam_sweeps/pallas_call | solution.py:401
Async XLA Ops:
  0.0 9.0 %collective-permute-start.2 = (bf16[1,4,64,4096]{3,2,1,0:T(8,128)(2,1)}, bf16[1,4,64,4096]{3,2,1,0:T(8,128)(2,1)S(1)}, u32[]{:S(2)}, u32[]{:S(2)}) collective-permute-start(bf16[1,4,64,4096]{3,2,1,0:T(8,128)(2,1)} %own.1), channel_id=1, source_target_pairs={{0,8},{8,0},{1,9},{9,1},{2,10},{10,2},{3,11},{11,3},{4,12},{12,4},... | collective-permute-start | bytes 6291464 | tf_op jit(solution)/shard_map/ppermute | solution.py:323
  0.0 9.0 %copy-start = (s32[1,4]{1,0:T(1,128)S(1)}, s32[1,4]{1,0:T(1,128)}, u32[]{:S(2)}) copy-start(s32[1,4]{1,0:T(1,128)} %order_hbm.3) | copy-start | bytes 52
  0.0 9.0 %copy-start.1 = (s32[4]{0:T(128)S(1)}, s32[4]{0:T(128)}, u32[]{:S(2)}) copy-start(s32[4]{0:T(128)} %owner_hbm.1) | copy-start | bytes 52
  4.0 10.0 %collective-permute-start = (f32[4,4096]{1,0:T(4,128)S(1)}, f32[4,4096]{1,0:T(4,128)S(1)}, u32[]{:S(2)}, u32[]{:S(2)}) collective-permute-start(f32[4,4096]{1,0:T(4,128)S(1)} %get-tuple-element.15), channel_id=1, source_target_pairs={{0,1},{1,0},{2,3},{3,2},{4,5},{5,4},{6,7},{7,6},{8,9},{9,8},{10,11... | collective-permute-start | bytes 196616 | tf_op jit(solution)/shard_map/ppermute | solution.py:352
  4.6 9.4 %collective-permute-start.1 = (f32[4,4096]{1,0:T(4,128)S(1)}, f32[4,4096]{1,0:T(4,128)S(1)}, u32[]{:S(2)}, u32[]{:S(2)}) collective-permute-start(f32[4,4096]{1,0:T(4,128)S(1)} %get-tuple-element.16), channel_id=1, source_target_pairs={{1,2},{2,1},{3,4},{4,3},{5,6},{6,5},{9,10},{10,9},{11,12},{12,11},... | collective-permute-start | bytes 196616 | tf_op jit(solution)/shard_map/ppermute | solution.py:353
  16.0 11.1 %collective-permute-start.3 = (f32[3,4,4096]{2,1,0:T(4,128)S(1)}, f32[3,4,4096]{2,1,0:T(4,128)S(1)}, u32[]{:S(2)}, u32[]{:S(2)}) collective-permute-start(f32[3,4,4096]{2,1,0:T(4,128)S(1)} %get-tuple-element.23), channel_id=1, source_target_pairs={{0,1},{1,0},{2,3},{3,2},{4,5},{5,4},{6,7},{7,6},{8,9},{9,8},{10,11... | collective-permute-start | bytes 589832 | tf_op jit(solution)/shard_map/ppermute | solution.py:381
  16.1 11.0 %collective-permute-start.4 = (f32[3,4,4096]{2,1,0:T(4,128)S(1)}, f32[3,4,4096]{2,1,0:T(4,128)S(1)}, u32[]{:S(2)}, u32[]{:S(2)}) collective-permute-start(f32[3,4,4096]{2,1,0:T(4,128)S(1)} %get-tuple-element.24), channel_id=1, source_target_pairs={{1,2},{2,1},{3,4},{4,3},{5,6},{6,5},{9,10},{10,9},{11,12},{12,11},... | collective-permute-start | bytes 589832 | tf_op jit(solution)/shard_map/ppermute | solution.py:382

commit v4 on v3

--- a/solution.py
+++ b/solution.py
@@ -64,7 +64,7 @@
         done = stop
 
 
-def force_stain(s_ref, k, regions, f_ref, u_ref, r_ref, y_ref, matrix):
+def force_stain(s_ref, k, mine, regions, own, recv, u_ref, r_ref, y_ref, matrix):
     tiles = s_ref.shape[1]
     parts = [s_ref[k, :, s0 : s0 + n, :] for s0, _, _, n in regions]
     x = parts[0] if len(parts) == 1 else jnp.concatenate(parts, 1)
@@ -89,7 +89,8 @@
                 before, r_now = after, r_next
                 gy = y_ref[c, rows, :]
                 gz = s_ref[k, c, s + 1 : s + 1 + count, :] - s_ref[k, c, s - 1 : s - 1 + count, :]
-                fixed = f_ref[k, block : block + 16, c * LANES : (c + 1) * LANES].astype(F32)
+                place = (k, slice(block, block + 16), slice(c * LANES, (c + 1) * LANES))
+                fixed = jnp.where(mine, own[place], recv[(0,) + place]).astype(F32)
                 fixed = fixed[skip : skip + count]
                 ux, uy, uz = u_ref[0, c, at, :], u_ref[1, c, at, :], u_ref[2, c, at, :]
                 moved = (gx * ux + gy * uy) + gz * uz
@@ -129,7 +130,7 @@
         ref[tuple(at)] = jnp.zeros(shape, F32)
 
 
-def load_kernel(depth, subject, moved, own, s_ref, u_ref, own_ref, even_send, odd_send, s_sem, u_sem, o_sem):
+def load_kernel(depth, subject, moved, s_ref, u_ref, even_send, odd_send, s_sem, u_sem):
     stains, tiles = s_ref.shape[:2]
     tall = depth // 8
     even = (lax.axis_index("depth") % 2) == 0
@@ -145,10 +146,6 @@
         s_copy(t).start()
     for t in range(tall):
         u_copy(t).start()
-    template = pltpu.make_async_copy(own.at[0], own_ref, o_sem)
-    template.start()
-    for z in (0, depth + 8):
-        u_ref[:, :, z : z + 8, :] = jnp.zeros((3, tiles, 8, LANES), F32)
     for t in order[:2]:
         s_copy(t).wait()
     for k in range(stains):
@@ -161,49 +158,34 @@
         s_copy(t).wait()
     for t in range(tall):
         u_copy(t).wait()
-    template.wait()
-
-
-def inner_kernel(depth, order_hbm, owner_hbm, s_ref, u_in, own, recv, f_ref, u_ref, order, owner, r_ref,
-                 y_ref, o_sem, f_sem):
-    stains = s_ref.shape[0]
-    small = [
+
+
+def inner_kernel(depth, order_hbm, owner_hbm, s_ref, u_in, own, recv, u_ref, order, owner, r_ref, y_ref, o_sem):
+    copies = [
         pltpu.make_async_copy(order_hbm, order, o_sem.at[0]),
         pltpu.make_async_copy(owner_hbm, owner, o_sem.at[1]),
     ]
-    for copy in small:
+    for copy in copies:
         copy.start()
     clear_rim(r_ref, 0)
     matrix = lateral_matrix(True)
-    for copy in small:
+    for copy in copies:
         copy.wait()
-
-    def f_copy(source, k):
-        return pltpu.make_async_copy(source, f_ref.at[k], f_sem.at[k])
-
-    for j in range(stains):
+    for j in range(s_ref.shape[0]):
         k = order[0, j]
         mine = owner[k] == lax.axis_index("subj")
-
-        @pl.when(mine)
-        def _():
-            f_copy(own.at[k], k).start()
-
-        @pl.when(jnp.logical_not(mine))
-        def _():
-            f_copy(recv.at[0, k], k).start()
-
-    for j in range(stains):
-        k = order[0, j]
-        f_copy(own.at[k], k).wait()
-        force_stain(s_ref, k, ((16, 8, 16, depth - 16),), f_ref, u_ref, r_ref, y_ref, matrix)
-
-
-def edge_kernel(depth, order_hbm, even_recv, odd_recv, s_in, f_ref, u_in, s_ref, u_ref, even_send, odd_send,
-                order, r_ref, y_ref, o_sem):
+        force_stain(s_ref, k, mine, ((16, 8, 16, depth - 16),), own, recv, u_ref, r_ref, y_ref, matrix)
+
+
+def edge_kernel(depth, order_hbm, owner_hbm, even_recv, odd_recv, own, recv, s_in, u_in, s_ref, u_ref, even_send,
+                odd_send, order, owner, r_ref, y_ref, o_sem):
     stains, tiles = s_ref.shape[:2]
-    copy = pltpu.make_async_copy(order_hbm, order, o_sem)
-    copy.start()
+    copies = [
+        pltpu.make_async_copy(order_hbm, order, o_sem.at[0]),
+        pltpu.make_async_copy(owner_hbm, owner, o_sem.at[1]),
+    ]
+    for copy in copies:
+        copy.start()
     even = (lax.axis_index("depth") % 2) == 0
     clear_rim(r_ref, 0)
     matrix = lateral_matrix(True)
@@ -214,10 +196,13 @@
         for k in range(stains):
             s_ref[k, c, 7:8, :] = low[k : k + 1]
             s_ref[k, c, depth + 8 : depth + 9, :] = high[k : k + 1]
-    copy.wait()
+    for copy in copies:
+        copy.wait()
     for j in range(stains):
+        k = order[0, j]
+        mine = owner[k] == lax.axis_index("subj")
         regions = ((8, 0, 8, 8), (depth, depth - 8, depth, 8))
-        force_stain(s_ref, order[0, j], regions, f_ref, u_ref, r_ref, y_ref, matrix)
+        force_stain(s_ref, k, mine, regions, own, recv, u_ref, r_ref, y_ref, matrix)
     n = SWEEPS
     for q in range(3):
         for c in range(tiles):
@@ -228,11 +213,7 @@
 
 
 def sweep_kernel(depth, u_ref, out, a_ref, b_ref, r_ref, o_ref, o_sem):
-    tiles = a_ref.shape[1]
     clear_rim(r_ref, 1)
-    for ref in (a_ref, b_ref):
-        for z in (0, depth + 8):
-            ref[:, :, z : z + 8, :] = jnp.zeros((3, tiles, 8, LANES), F32)
     matrix = lateral_matrix(False)
     src, dst = u_ref, a_ref
     for i in range(SWEEPS):
@@ -273,9 +254,6 @@
     clear_rim(r_ref, 1)
     n = SWEEPS
     for q in range(3):
-        for ref in (a_ref, b_ref):
-            for z in (0, 32):
-                ref[q, :, z : z + 8, :] = jnp.zeros((tiles, 8, LANES), F32)
         a_ref[q, :, 8:16, :] = u_ref[q, :, depth : depth + 8, :]
         a_ref[q, :, 24:32, :] = u_ref[q, :, 8:16, :]
         for c in range(tiles):
@@ -283,9 +261,8 @@
             x, y = even_recv[q, :, at], odd_recv[q, :, at]
             a_ref[q, c, 16 : 16 + n, :] = jnp.where(even, x, y)
             a_ref[q, c, 20 : 20 + n, :] = jnp.where(even, y, x)
-    row = lax.broadcasted_iota(jnp.int32, (24, LANES), 0)
-    keep = jnp.where((row >= 8) & (row < 12), jnp.where(has_high, 1.0, 0.0), 1.0)
-    keep = jnp.where((row >= 12) & (row < 16), jnp.where(has_low, 1.0, 0.0), keep)
+    row = lax.broadcasted_iota(jnp.int32, (8, LANES), 0)
+    keep = jnp.where(row < n, jnp.where(has_high, 1.0, 0.0), jnp.where(has_low, 1.0, 0.0))
     top = lax.broadcasted_iota(jnp.int32, (8, LANES), 0) < 4
     matrix = lateral_matrix(False)
     src, dst = a_ref, b_ref
@@ -303,7 +280,9 @@
                     o_ref[0, q, :, at] = jnp.where(top, value[16:24], o_ref[0, q, :, at])
                     o_ref[1, q, :, at] = jnp.where(top, o_ref[1, q, :, at], value[0:8])
                 else:
-                    dst[q, c, 8:32, :] = value * keep
+                    dst[q, c, 8:16, :] = value[0:8]
+                    dst[q, c, 16:24, :] = value[8:16] * keep
+                    dst[q, c, 24:32, :] = value[16:24]
 
             sweep(src, store, q, 8, 24, r_ref, matrix)
             if final:
@@ -331,7 +310,6 @@
 
     tall = depth // 8
     s_type = pltpu.VMEM((stains, tiles, depth + 16, LANES), F32)
-    f_type = pltpu.VMEM((stains, depth, cells), BF16)
     u_type = pltpu.VMEM((3, tiles, depth + 16, LANES), F32)
     send_type = pltpu.VMEM((3, SWEEPS, cells), F32)
 
@@ -339,28 +317,28 @@
         return [pltpu.VMEM((tiles + 2, planes, LANES), F32), pltpu.VMEM((tiles, planes, LANES), F32)]
 
     plane_type = pltpu.VMEM((stains, cells), F32)
-    s, u, own, even_send, odd_send = pl.pallas_call(
+    s, u, even_send, odd_send = pl.pallas_call(
         functools.partial(load_kernel, depth),
-        out_shape=(s_type, u_type, f_type, plane_type, plane_type),
-        in_specs=[HBM] * 3,
-        out_specs=(VMEM,) * 5,
-        scratch_shapes=[dma((tall,)), dma((tall,)), dma],
+        out_shape=(s_type, u_type, plane_type, plane_type),
+        in_specs=[HBM, HBM],
+        out_specs=(VMEM,) * 4,
+        scratch_shapes=[dma((tall,)), dma((tall,))],
         compiler_params=params(LOAD),
         name="load",
-    )(subject5, moved5, template)
+    )(subject5, moved5)
 
     even_recv = lax.ppermute(even_send, "depth", even_pairs)
     odd_recv = lax.ppermute(odd_send, "depth", odd_pairs)
 
-    f, u = pl.pallas_call(
+    scalars = [pltpu.SMEM(order.shape, jnp.int32), pltpu.SMEM(owner.shape, jnp.int32)]
+    own = template[0]
+    u = pl.pallas_call(
         functools.partial(inner_kernel, depth),
-        out_shape=(f_type, u_type),
-        in_specs=[HBM, HBM, VMEM, VMEM, VMEM, ANY],
-        out_specs=(VMEM, VMEM),
-        scratch_shapes=[pltpu.SMEM(order.shape, jnp.int32), pltpu.SMEM(owner.shape, jnp.int32)]
-        + force_scratch(depth - 16)
-        + [dma((2,)), dma((stains,))],
-        input_output_aliases={3: 1},
+        out_shape=u_type,
+        in_specs=[HBM, HBM, VMEM, VMEM, VMEM, VMEM],
+        out_specs=VMEM,
+        scratch_shapes=scalars + force_scratch(depth - 16) + [dma((2,))],
+        input_output_aliases={3: 0},
         compiler_params=params(20),
         cost_estimate=pl.CostEstimate(flops=4 * 10**8, bytes_accessed=10 << 20, transcendentals=0),
         name="inner_force",
@@ -369,14 +347,14 @@
     s, u, even_send, odd_send = pl.pallas_call(
         functools.partial(edge_kernel, depth),
         out_shape=(s_type, u_type, send_type, send_type),
-        in_specs=[HBM, VMEM, VMEM, VMEM, VMEM, VMEM],
+        in_specs=[HBM, HBM] + [VMEM] * 6,
         out_specs=(VMEM, VMEM, VMEM, VMEM),
-        scratch_shapes=[pltpu.SMEM(order.shape, jnp.int32)] + force_scratch(16) + [dma],
-        input_output_aliases={3: 0, 5: 1},
+        scratch_shapes=scalars + force_scratch(16) + [dma((2,))],
+        input_output_aliases={6: 0, 7: 1},
         compiler_params=params(20),
         cost_estimate=pl.CostEstimate(flops=10**8, bytes_accessed=8 << 20, transcendentals=0),
         name="edge_force",
-    )(order, even_recv, odd_recv, s, f, u)
+    )(order, owner, even_recv, odd_recv, own, recv, s, u)
 
     u_even = lax.ppermute(even_send, "depth", even_pairs)
     u_odd = lax.ppermute(odd_send, "depth", odd_pairs)

time: 31.1 us -> 29.8 us (0.958)
  Pallas kernels: 20 us -> 18.7 us
    pallas_call x1, Pallas kernels: 3.99 us -> 3.35 us  [local(): pl.pallas_call(functools.partial(load_kernel, depth), out_shape=(s_type,...]
    pallas_call x1, Pallas kernels: 4.94 us -> 4.41 us  [local(): pl.pallas_call(functools.partial(inner_kernel, depth), out_shape=u_type,...]
  transfers between devices with their start and end apart: 5 -> 5, of which waited for: 0 -> 0; matrix products, arithmetic and copies ran while one was open for 0% -> 0% of each run, Pallas kernels for 48% -> 46%
where the time goes in v4:
time: 29.8 us; the launch traced here: 29.3 us
  Pallas kernels  18.7 us (63%)
  starting transfers between devices  10.3 us (35%)
    pallas_call x1, Pallas kernels, local(): pl.pallas_call(functools.partial(sweep_kernel, depth), out_shape=sds(disp...  5.77 us
    ppermute x1, starting transfers between devices, local(): u_odd = lax.ppermute(odd_send, 'depth', odd_pairs)  5.1 us
    ppermute x1, starting transfers between devices, local(): odd_recv = lax.ppermute(odd_send, 'depth', odd_pairs)  4.43 us
    pallas_call x1, Pallas kernels, local(): pl.pallas_call(functools.partial(inner_kernel, depth), out_shape=u_type,...  4.41 us
    pallas_call x1, Pallas kernels, local(): pl.pallas_call(functools.partial(load_kernel, depth), out_shape=(s_type,...  3.35 us
    pallas_call x1, Pallas kernels, local(): pl.pallas_call(functools.partial(seam_kernel, depth), out_shape=sds(displ...  3.17 us
    pallas_call x1, Pallas kernels, local(): pl.pallas_call(functools.partial(edge_kernel, depth), out_shape=(s_type,...  2.02 us
  transfers between devices with their start and end apart: 5, of which 0 were waited for; matrix products, arithmetic and copies ran while one was open for 0% of the time, Pallas kernels for 46%

profile of v4, /device:TPU:12, one launch (start us, length us, event | category | flops | bytes accessed | tf_op | source)
XLA Modules:
  0.0 29.3 jit_solution(4934096336351485914)
XLA Ops:
  0.0 0.0 copy-start
  0.0 0.0 copy-start.1
  0.0 0.0 copy-start.2
  0.0 0.1 collective-permute-start.2
  0.1 3.4 %load.1 = (f32[4,32,80,128]{3,2,1,0:T(8,128)S(1)}, f32[3,32,80,128]{3,2,1,0:T(8,128)S(1)}, f32[4,4096]{1,0:T(4,128)S(1)}, f32[4,4096]{1,0:T(4,128)S(1)}) custom-call(f32[4,8,32,8,128]{4,3,2,1,0:T(8,128)} %bitcast.9, f32[3,8,32,8,128]{4,3,2,1,0:T(8,128)} %bitcast.10), custom_call_target="tpu_custom_call" | custom-call | tf_op jit(solution)/shard_map/load/pallas_call | solution.py:320
  3.4 0.6 %collective-permute-start = (f32[4,4096]{1,0:T(4,128)S(1)}, f32[4,4096]{1,0:T(4,128)S(1)}, u32[]{:S(2)}, u32[]{:S(2)}) collective-permute-start(f32[4,4096]{1,0:T(4,128)S(1)} %get-tuple-element.12), channel_id=1, source_target_pairs={{0,1},{1,0},{2,3},{3,2},{4,5},{5,4},{6,7},{7,6},{8,9},{9,8},{10,11... | collective-permute-start | bytes 196616 | tf_op jit(solution)/shard_map/ppermute | solution.py:330
  4.0 4.4 %collective-permute-start.1 = (f32[4,4096]{1,0:T(4,128)S(1)}, f32[4,4096]{1,0:T(4,128)S(1)}, u32[]{:S(2)}, u32[]{:S(2)}) collective-permute-start(f32[4,4096]{1,0:T(4,128)S(1)} %get-tuple-element.13), channel_id=1, source_target_pairs={{1,2},{2,1},{3,4},{4,3},{5,6},{6,5},{9,10},{10,9},{11,12},{12,11},... | collective-permute-start | bytes 196616 | tf_op jit(solution)/shard_map/ppermute | solution.py:331
  8.5 0.0 collective-permute-done.2.recv
  8.5 0.0 copy-done
  8.5 0.0 copy-done.1
  8.5 0.0 copy-done.2
  8.5 4.4 %inner_force.1.u_in = f32[3,32,80,128]{3,2,1,0:T(8,128)S(1)} custom-call(s32[1,4]{1,0:T(1,128)S(1)} %copy-done.1, s32[4]{0:T(128)S(1)} %copy-done.2, f32[4,32,80,128]{3,2,1,0:T(8,128)S(1)} %get-tuple-element.14.s_ref.s_in, f32[3,32,80,128]{3,2,1,0:T(8,128)S(1)} %get-tuple-element.15.u_in, ...), custom_call_target="tpu_custom_call", output_to_operand_aliasing={{}: (3, {})} | custom-call | flops 400000000 | bytes 10485760 | tf_op jit(solution)/shard_map/inner_force/pallas_call | solution.py:335
  12.9 0.0 collective-permute-done.even_recv
  12.9 0.0 collective-permute-done.1.odd_recv
  12.9 2.0 %edge_force.1 = (f32[4,32,80,128]{3,2,1,0:T(8,128)S(1)}, f32[3,32,80,128]{3,2,1,0:T(8,128)S(1)}, f32[3,4,4096]{2,1,0:T(4,128)S(1)}, f32[3,4,4096]{2,1,0:T(4,128)S(1)}) custom-call(s32[1,4]{1,0:T(1,128)S(1)} %copy-done.1, s32[4]{0:T(128)S(1)} %copy-done.2, ...), custom_call_target="tpu_custom_call", output_to_operand_aliasing={{0}: (6, {}), {1}: (7, {})} | custom-call | flops 100000000 | bytes 8388608 | tf_op jit(solution)/shard_map/edge_force/pallas_call | solution.py:347
  15.0 0.1 collective-permute-start.3
  15.1 5.1 %collective-permute-start.4 = (f32[3,4,4096]{2,1,0:T(4,128)S(1)}, f32[3,4,4096]{2,1,0:T(4,128)S(1)}, u32[]{:S(2)}, u32[]{:S(2)}) collective-permute-start(f32[3,4,4096]{2,1,0:T(4,128)S(1)} %get-tuple-element.18), channel_id=1, source_target_pairs={{1,2},{2,1},{3,4},{4,3},{5,6},{6,5},{9,10},{10,9},{11,12},{12,11},... | collective-permute-start | bytes 589832 | tf_op jit(solution)/shard_map/ppermute | solution.py:360
  20.2 5.8 %sweeps.1.before = f32[1,3,64,4096]{3,2,1,0:T(8,128)} custom-call(f32[3,32,80,128]{3,2,1,0:T(8,128)S(1)} %get-tuple-element.16.u_ref), custom_call_target="tpu_custom_call" | custom-call | flops 1000000000 | bytes 41943040 | tf_op jit(solution)/shard_map/sweeps/pallas_call | solution.py:362
  25.9 0.0 collective-permute-done.3.even_recv
  25.9 0.0 collective-permute-done.4.odd_recv
  26.0 3.2 %seam_sweeps.1 = f32[1,3,64,4096]{3,2,1,0:T(8,128)} custom-call(f32[3,32,80,128]{3,2,1,0:T(8,128)S(1)} %get-tuple-element.16.u_ref, f32[3,4,4096]{2,1,0:T(4,128)S(1)} %collective-permute-done.3.even_recv, f32[3,4,4096]{2,1,0:T(4,128)S(1)} %collective-permute-done.4.odd_recv, f32[1,3,64,4096]{3,2,1,0:T(8,128)} %sweeps.1.before), custom_call_target="tpu_custom_call", output_to_operand_aliasing={{}: (3, {})} | custom-call | tf_op jit(solution)/shard_map/seam_sweeps/pallas_call | solution.py:379
Async XLA Ops:
  0.0 8.5 %copy-start = (bf16[1,4,64,4096]{3,2,1,0:T(8,128)(2,1)S(1)}, bf16[1,4,64,4096]{3,2,1,0:T(8,128)(2,1)}, u32[]{:S(2)}) copy-start(bf16[1,4,64,4096]{3,2,1,0:T(8,128)(2,1)} %param.5) | copy-start | bytes 6291460
  0.0 8.5 %copy-start.1 = (s32[1,4]{1,0:T(1,128)S(1)}, s32[1,4]{1,0:T(1,128)}, u32[]{:S(2)}) copy-start(s32[1,4]{1,0:T(1,128)} %order_hbm.3) | copy-start | bytes 52
  0.0 8.5 %copy-start.2 = (s32[4]{0:T(128)S(1)}, s32[4]{0:T(128)}, u32[]{:S(2)}) copy-start(s32[4]{0:T(128)} %owner_hbm.3) | copy-start | bytes 52
  0.0 8.5 %collective-permute-start.2 = (bf16[1,4,64,4096]{3,2,1,0:T(8,128)(2,1)}, bf16[1,4,64,4096]{3,2,1,0:T(8,128)(2,1)S(1)}, u32[]{:S(2)}, u32[]{:S(2)}) collective-permute-start(bf16[1,4,64,4096]{3,2,1,0:T(8,128)(2,1)} %param.5), channel_id=1, source_target_pairs={{0,8},{8,0},{1,9},{9,1},{2,10},{10,2},{3,11},{11,3},{4,12},{12,4},... | collective-permute-start | bytes 6291464 | tf_op jit(solution)/shard_map/ppermute | solution.py:302
  3.4 9.5 %collective-permute-start = (f32[4,4096]{1,0:T(4,128)S(1)}, f32[4,4096]{1,0:T(4,128)S(1)}, u32[]{:S(2)}, u32[]{:S(2)}) collective-permute-start(f32[4,4096]{1,0:T(4,128)S(1)} %get-tuple-element.12), channel_id=1, source_target_pairs={{0,1},{1,0},{2,3},{3,2},{4,5},{5,4},{6,7},{7,6},{8,9},{9,8},{10,11... | collective-permute-start | bytes 196616 | tf_op jit(solution)/shard_map/ppermute | solution.py:330
  4.0 8.9 %collective-permute-start.1 = (f32[4,4096]{1,0:T(4,128)S(1)}, f32[4,4096]{1,0:T(4,128)S(1)}, u32[]{:S(2)}, u32[]{:S(2)}) collective-permute-start(f32[4,4096]{1,0:T(4,128)S(1)} %get-tuple-element.13), channel_id=1, source_target_pairs={{1,2},{2,1},{3,4},{4,3},{5,6},{6,5},{9,10},{10,9},{11,12},{12,11},... | collective-permute-start | bytes 196616 | tf_op jit(solution)/shard_map/ppermute | solution.py:331
  15.0 11.0 %collective-permute-start.3 = (f32[3,4,4096]{2,1,0:T(4,128)S(1)}, f32[3,4,4096]{2,1,0:T(4,128)S(1)}, u32[]{:S(2)}, u32[]{:S(2)}) collective-permute-start(f32[3,4,4096]{2,1,0:T(4,128)S(1)} %get-tuple-element.17), channel_id=1, source_target_pairs={{0,1},{1,0},{2,3},{3,2},{4,5},{5,4},{6,7},{7,6},{8,9},{9,8},{10,11... | collective-permute-start | bytes 589832 | tf_op jit(solution)/shard_map/ppermute | solution.py:359
  15.1 10.9 %collective-permute-start.4 = (f32[3,4,4096]{2,1,0:T(4,128)S(1)}, f32[3,4,4096]{2,1,0:T(4,128)S(1)}, u32[]{:S(2)}, u32[]{:S(2)}) collective-permute-start(f32[3,4,4096]{2,1,0:T(4,128)S(1)} %get-tuple-element.18), channel_id=1, source_target_pairs={{1,2},{2,1},{3,4},{4,3},{5,6},{6,5},{9,10},{10,9},{11,12},{12,11},... | collective-permute-start | bytes 589832 | tf_op jit(solution)/shard_map/ppermute | solution.py:360

commit v5 on v4

--- a/solution.py
+++ b/solution.py
@@ -13,8 +13,8 @@
 RATE = 0.15
 F32 = jnp.float32
 BF16 = jnp.bfloat16
-LIMIT = 48
-LOAD = 46
+LIMIT = 32
+LOAD = 47
 
 ANY = pl.BlockSpec(memory_space=pl.ANY)
 HBM = pl.BlockSpec(memory_space=pltpu.HBM)
@@ -64,7 +64,7 @@
         done = stop
 
 
-def force_stain(s_ref, k, mine, regions, own, recv, u_ref, r_ref, y_ref, matrix):
+def force_stain(s_ref, k, mine, regions, own, recv, moved, u_ref, r_ref, y_ref, matrix):
     tiles = s_ref.shape[1]
     parts = [s_ref[k, :, s0 : s0 + n, :] for s0, _, _, n in regions]
     x = parts[0] if len(parts) == 1 else jnp.concatenate(parts, 1)
@@ -92,9 +92,13 @@
                 place = (k, slice(block, block + 16), slice(c * LANES, (c + 1) * LANES))
                 fixed = jnp.where(mine, own[place], recv[(0,) + place]).astype(F32)
                 fixed = fixed[skip : skip + count]
-                ux, uy, uz = u_ref[0, c, at, :], u_ref[1, c, at, :], u_ref[2, c, at, :]
-                moved = (gx * ux + gy * uy) + gz * uz
-                twice = (fixed - s_ref[k, c, s : s + count, :]) * 2.0 - moved
+                if moved is None:
+                    ux, uy, uz = (u_ref[q, c, at, :] for q in range(3))
+                else:
+                    from_plane = slice(f0 + z, f0 + z + count)
+                    ux, uy, uz = (moved[0, q, from_plane, c * LANES : (c + 1) * LANES] for q in range(3))
+                slope = (gx * ux + gy * uy) + gz * uz
+                twice = (fixed - s_ref[k, c, s : s + count, :]) * 2.0 - slope
                 denom = (gx * gx + gy * gy) + (gz * gz + (twice * twice + 2.0))
                 w = twice * inverse(denom)
                 u_ref[0, c, at, :] = ux + w * gx
@@ -130,7 +134,7 @@
         ref[tuple(at)] = jnp.zeros(shape, F32)
 
 
-def load_kernel(depth, subject, moved, s_ref, u_ref, even_send, odd_send, s_sem, u_sem):
+def load_kernel(depth, subject, s_ref, even_send, odd_send, s_sem):
     stains, tiles = s_ref.shape[:2]
     tall = depth // 8
     even = (lax.axis_index("depth") % 2) == 0
@@ -138,14 +142,9 @@
     def s_copy(t):
         return pltpu.make_async_copy(subject.at[:, t], s_ref.at[:, :, 8 + 8 * t : 16 + 8 * t, :], s_sem.at[t])
 
-    def u_copy(t):
-        return pltpu.make_async_copy(moved.at[:, t], u_ref.at[:, :, 8 + 8 * t : 16 + 8 * t, :], u_sem.at[t])
-
     order = (0, tall - 1) + tuple(range(1, tall - 1))
     for t in order:
         s_copy(t).start()
-    for t in range(tall):
-        u_copy(t).start()
     for t in order[:2]:
         s_copy(t).wait()
     for k in range(stains):
@@ -156,11 +155,9 @@
             odd_send[k : k + 1, at] = jnp.where(even, low, high)
     for t in order[2:]:
         s_copy(t).wait()
-    for t in range(tall):
-        u_copy(t).wait()
-
-
-def inner_kernel(depth, order_hbm, owner_hbm, s_ref, u_in, own, recv, u_ref, order, owner, r_ref, y_ref, o_sem):
+
+
+def inner_kernel(depth, order_hbm, owner_hbm, s_ref, moved, own, recv, u_ref, order, owner, r_ref, y_ref, o_sem):
     copies = [
         pltpu.make_async_copy(order_hbm, order, o_sem.at[0]),
         pltpu.make_async_copy(owner_hbm, owner, o_sem.at[1]),
@@ -174,10 +171,10 @@
     for j in range(s_ref.shape[0]):
         k = order[0, j]
         mine = owner[k] == lax.axis_index("subj")
-        force_stain(s_ref, k, mine, ((16, 8, 16, depth - 16),), own, recv, u_ref, r_ref, y_ref, matrix)
-
-
-def edge_kernel(depth, order_hbm, owner_hbm, even_recv, odd_recv, own, recv, s_in, u_in, s_ref, u_ref, even_send,
+        force_stain(s_ref, k, mine, ((16, 8, 16, depth - 16),), own, recv, moved if j == 0 else None, u_ref, r_ref, y_ref, matrix)
+
+
+def edge_kernel(depth, order_hbm, owner_hbm, even_recv, odd_recv, own, recv, moved, s_in, u_in, s_ref, u_ref, even_send,
                 odd_send, order, owner, r_ref, y_ref, o_sem):
     stains, tiles = s_ref.shape[:2]
     copies = [
@@ -202,7 +199,7 @@
         k = order[0, j]
         mine = owner[k] == lax.axis_index("subj")
         regions = ((8, 0, 8, 8), (depth, depth - 8, depth, 8))
-        force_stain(s_ref, k, mine, regions, own, recv, u_ref, r_ref, y_ref, matrix)
+        force_stain(s_ref, k, mine, regions, own, recv, moved if j == 0 else None, u_ref, r_ref, y_ref, matrix)
     n = SWEEPS
     for q in range(3):
         for c in range(tiles):
@@ -212,7 +209,7 @@
             odd_send[q, :, at] = jnp.where(even, low, high)
 
 
-def sweep_kernel(depth, u_ref, out, a_ref, b_ref, r_ref, o_ref, o_sem):
+def sweep_kernel(depth, u_ref, o_ref, a_ref, b_ref, r_ref):
     clear_rim(r_ref, 1)
     matrix = lateral_matrix(False)
     src, dst = u_ref, a_ref
@@ -227,11 +224,7 @@
                     dst[q, c, 8 : 8 + depth, :] = value
 
             sweep(src, store, q, 8, depth, r_ref, matrix)
-            if final:
-                pltpu.make_async_copy(o_ref.at[q], out.at[0, q], o_sem.at[q]).start()
         src, dst = dst, (b_ref if dst is a_ref else a_ref)
-    for q in range(3):
-        pltpu.make_async_copy(o_ref.at[q], out.at[0, q], o_sem.at[q]).wait()
 
 
 def seam_kernel(depth, u_ref, even_recv, odd_recv, before, out, a_ref, b_ref, r_ref, o_ref, sem):
@@ -241,15 +234,14 @@
     has_low = at_depth > 0
     has_high = at_depth < lax.axis_size("depth") - 1
     ends = (0, depth - 8)
-    ins = [
-        pltpu.make_async_copy(before.at[0, :, z : z + 8, :], o_ref.at[i], sem.at[i]) for i, z in enumerate(ends)
-    ]
+    inner = pl.ds(8, depth - 16)
+    inside = [pltpu.make_async_copy(before.at[q, inner, :], out.at[0, q, inner, :], sem.at[6 + q]) for q in range(3)]
     outs = [
-        pltpu.make_async_copy(o_ref.at[i, q], out.at[0, q, z : z + 8, :], sem.at[2 + 2 * q + i])
+        pltpu.make_async_copy(o_ref.at[i, q], out.at[0, q, z : z + 8, :], sem.at[2 * q + i])
         for q in range(3)
         for i, z in enumerate(ends)
     ]
-    for copy in ins:
+    for copy in inside:
         copy.start()
     clear_rim(r_ref, 1)
     n = SWEEPS
@@ -268,17 +260,14 @@
     src, dst = a_ref, b_ref
     for i in range(SWEEPS):
         final = i == SWEEPS - 1
-        if final:
-            for copy in ins:
-                copy.wait()
         for q in range(3):
 
             def store(c, value, q=q, dst=dst, final=final):
                 at = slice(c * LANES, (c + 1) * LANES)
                 if final:
                     value = value * RATE**SWEEPS
-                    o_ref[0, q, :, at] = jnp.where(top, value[16:24], o_ref[0, q, :, at])
-                    o_ref[1, q, :, at] = jnp.where(top, o_ref[1, q, :, at], value[0:8])
+                    o_ref[0, q, :, at] = jnp.where(top, value[16:24], before[q, 0:8, at])
+                    o_ref[1, q, :, at] = jnp.where(top, before[q, depth - 8 : depth, at], value[0:8])
                 else:
                     dst[q, c, 8:16, :] = value[0:8]
                     dst[q, c, 16:24, :] = value[8:16] * keep
@@ -289,7 +278,7 @@
                 for copy in outs[2 * q : 2 * q + 2]:
                     copy.start()
         src, dst = dst, src
-    for copy in outs:
+    for copy in outs + inside:
         copy.wait()
 
 
@@ -304,7 +293,7 @@
     def tiled(a):
         return a.reshape(a.shape[1], depth // 8, 8, tiles, LANES).transpose(0, 1, 3, 2, 4)
 
-    subject5, moved5 = tiled(subject), tiled(displacement)
+    subject5 = tiled(subject)
     sds = jax.ShapeDtypeStruct
     dma = pltpu.SemaphoreType.DMA
 
@@ -317,15 +306,16 @@
         return [pltpu.VMEM((tiles + 2, planes, LANES), F32), pltpu.VMEM((tiles, planes, LANES), F32)]
 
     plane_type = pltpu.VMEM((stains, cells), F32)
-    s, u, even_send, odd_send = pl.pallas_call(
+    s, even_send, odd_send = pl.pallas_call(
         functools.partial(load_kernel, depth),
-        out_shape=(s_type, u_type, plane_type, plane_type),
-        in_specs=[HBM, HBM],
-        out_specs=(VMEM,) * 4,
-        scratch_shapes=[dma((tall,)), dma((tall,))],
+        out_shape=(s_type, plane_type, plane_type),
+        in_specs=[HBM],
+        out_specs=(VMEM,) * 3,
+        scratch_shapes=[dma((tall,))],
         compiler_params=params(LOAD),
+        cost_estimate=pl.CostEstimate(flops=4 * 10**9, bytes_accessed=24 << 20, transcendentals=0),
         name="load",
-    )(subject5, moved5)
+    )(subject5)
 
     even_recv = lax.ppermute(even_send, "depth", even_pairs)
     odd_recv = lax.ppermute(odd_send, "depth", odd_pairs)
@@ -338,38 +328,35 @@
         in_specs=[HBM, HBM, VMEM, VMEM, VMEM, VMEM],
         out_specs=VMEM,
         scratch_shapes=scalars + force_scratch(depth - 16) + [dma((2,))],
-        input_output_aliases={3: 0},
         compiler_params=params(20),
         cost_estimate=pl.CostEstimate(flops=4 * 10**8, bytes_accessed=10 << 20, transcendentals=0),
         name="inner_force",
-    )(order, owner, s, u, own, recv)
+    )(order, owner, s, displacement, own, recv)
 
     s, u, even_send, odd_send = pl.pallas_call(
         functools.partial(edge_kernel, depth),
         out_shape=(s_type, u_type, send_type, send_type),
-        in_specs=[HBM, HBM] + [VMEM] * 6,
+        in_specs=[HBM, HBM] + [VMEM] * 7,
         out_specs=(VMEM, VMEM, VMEM, VMEM),
         scratch_shapes=scalars + force_scratch(16) + [dma((2,))],
-        input_output_aliases={6: 0, 7: 1},
+        input_output_aliases={7: 0, 8: 1},
         compiler_params=params(20),
         cost_estimate=pl.CostEstimate(flops=10**8, bytes_accessed=8 << 20, transcendentals=0),
         name="edge_force",
-    )(order, owner, even_recv, odd_recv, own, recv, s, u)
+    )(order, owner, even_recv, odd_recv, own, recv, displacement, s, u)
 
     u_even = lax.ppermute(even_send, "depth", even_pairs)
     u_odd = lax.ppermute(odd_send, "depth", odd_pairs)
 
     inside = pl.pallas_call(
         functools.partial(sweep_kernel, depth),
-        out_shape=sds(displacement.shape, F32),
+        out_shape=pltpu.VMEM((3, depth, cells), F32),
         in_specs=[VMEM],
-        out_specs=ANY,
+        out_specs=VMEM,
         scratch_shapes=[
             pltpu.VMEM((3, tiles, depth + 16, LANES), F32),
             pltpu.VMEM((3, tiles, depth + 16, LANES), F32),
             pltpu.VMEM((3, tiles + 2, depth, LANES), F32),
-            pltpu.VMEM((3, depth, cells), F32),
-            dma((3,)),
         ],
         compiler_params=params(LIMIT),
         cost_estimate=pl.CostEstimate(flops=10**9, bytes_accessed=40 << 20, transcendentals=0),
@@ -379,16 +366,15 @@
     return pl.pallas_call(
         functools.partial(seam_kernel, depth),
         out_shape=sds(displacement.shape, F32),
-        in_specs=[VMEM, VMEM, VMEM, ANY],
+        in_specs=[VMEM, VMEM, VMEM, VMEM],
         out_specs=ANY,
         scratch_shapes=[
             pltpu.VMEM((3, tiles, 40, LANES), F32),
             pltpu.VMEM((3, tiles, 40, LANES), F32),
             pltpu.VMEM((3, tiles + 2, 24, LANES), F32),
             pltpu.VMEM((2, 3, 8, cells), F32),
-            dma((8,)),
+            dma((9,)),
         ],
-        input_output_aliases={3: 0},
         compiler_params=params(LIMIT),
         name="seam_sweeps",
     )(u, u_even, u_odd, inside)

time: 29.8 us -> 28.4 us (0.953)
  the two profiles are of different devices: /device:TPU:12 before, /device:TPU:0 now
where the time goes in v5:
time: 28.4 us; the launch traced here: 28.3 us
  Pallas kernels  15.9 us (56%)
  starting transfers between devices  8.88 us (31%)
  waiting for transfers between devices  3.17 us (11%)
    pallas_call x1, Pallas kernels, local(): pl.pallas_call(functools.partial(sweep_kernel, depth), out_shape=pltpu.VM...  4.46 us
    pallas_call x1, Pallas kernels, local(): pl.pallas_call(functools.partial(inner_kernel, depth), out_shape=u_type,...  4.41 us
    ppermute x1, starting transfers between devices, local(): u_even = lax.ppermute(even_send, 'depth', even_pairs)  4.34 us
    ppermute x1, waiting for transfers between devices, local(): u_even = lax.ppermute(even_send, 'depth', even_pairs)  3.16 us
    pallas_call x1, Pallas kernels, local(): pl.pallas_call(functools.partial(seam_kernel, depth), out_shape=sds(displ...  2.65 us
    ppermute x1, starting transfers between devices, local(): even_recv = lax.ppermute(even_send, 'depth', even_pairs)  2.6 us
    pallas_call x1, Pallas kernels, local(): pl.pallas_call(functools.partial(load_kernel, depth), out_shape=(s_type,...  2.38 us
    pallas_call x1, Pallas kernels, local(): pl.pallas_call(functools.partial(edge_kernel, depth), out_shape=(s_type,...  2.03 us
  transfers between devices with their start and end apart: 5, of which 1 were waited for; matrix products, arithmetic and copies ran while one was open for 0% of the time, Pallas kernels for 40%

profile of v5, /device:TPU:0, one launch (start us, length us, event | category | flops | bytes accessed | tf_op | source)
XLA Modules:
  0.0 28.3 jit_solution(8306572171701326952)
XLA Ops:
  0.0 0.5 %collective-permute-start.2 = (bf16[1,4,64,4096]{3,2,1,0:T(8,128)(2,1)}, bf16[1,4,64,4096]{3,2,1,0:T(8,128)(2,1)S(1)}, u32[]{:S(2)}, u32[]{:S(2)}) collective-permute-start(bf16[1,4,64,4096]{3,2,1,0:T(8,128)(2,1)} %param.5), channel_id=1, source_target_pairs={{0,8},{8,0},{1,9},{9,1},{2,10},{10,2},{3,11},{11,3},{4,12},{12,4},... | collective-permute-start | bytes 6291464 | tf_op jit(solution)/shard_map/ppermute | solution.py:291
  0.5 0.0 copy-start
  0.5 0.0 copy-start.1
  0.5 0.0 copy-start.2
  0.5 0.0 copy-start.3
  0.5 2.4 %load.1 = (f32[4,32,80,128]{3,2,1,0:T(8,128)S(1)}, f32[4,4096]{1,0:T(4,128)S(1)}, f32[4,4096]{1,0:T(4,128)S(1)}) custom-call(f32[4,8,32,8,128]{4,3,2,1,0:T(8,128)} %bitcast.6), custom_call_target="tpu_custom_call" | custom-call | flops 4000000000 | bytes 25165824 | tf_op jit(solution)/shard_map/load/pallas_call | solution.py:309
  2.9 2.6 %collective-permute-start = (f32[4,4096]{1,0:T(4,128)S(1)}, f32[4,4096]{1,0:T(4,128)S(1)}, u32[]{:S(2)}, u32[]{:S(2)}) collective-permute-start(f32[4,4096]{1,0:T(4,128)S(1)} %get-tuple-element.11), channel_id=1, source_target_pairs={{0,1},{1,0},{2,3},{3,2},{4,5},{5,4},{6,7},{7,6},{8,9},{9,8},{10,11... | collective-permute-start | bytes 196616 | tf_op jit(solution)/shard_map/ppermute | solution.py:320
  5.5 0.7 %collective-permute-start.1 = (f32[4,4096]{1,0:T(4,128)S(1)}, f32[4,4096]{1,0:T(4,128)S(1)}, u32[]{:S(2)}, u32[]{:S(2)}) collective-permute-start(f32[4,4096]{1,0:T(4,128)S(1)} %get-tuple-element.12), channel_id=1, source_target_pairs={{1,2},{2,1},{3,4},{4,3},{5,6},{6,5},{9,10},{10,9},{11,12},{12,11},... | collective-permute-start | bytes 196616 | tf_op jit(solution)/shard_map/ppermute | solution.py:321
  6.1 0.0 collective-permute-done.2.recv
  6.1 0.0 copy-done
  6.1 0.0 copy-done.1
  6.1 0.0 copy-done.2
  6.2 0.0 copy-done.3
  6.2 4.4 %inner_force.1.u_in = f32[3,32,80,128]{3,2,1,0:T(8,128)S(1)} custom-call(s32[1,4]{1,0:T(1,128)S(1)} %copy-done.2, s32[4]{0:T(128)S(1)} %copy-done.3, f32[4,32,80,128]{3,2,1,0:T(8,128)S(1)} %get-tuple-element.13.s_ref.s_in, f32[1,3,64,4096]{3,2,1,0:T(8,128)S(1)} %copy-done, bf16[4,64,4096]{2,1,0:T(8,128)(2,1)S(1)} %bitcast.4, ...), custom_call_target="tpu_custom_call" | custom-call | flops 400000000 | bytes 10485760 | tf_op jit(solution)/shard_map/inner_force/pallas_call | solution.py:325
  10.6 0.0 collective-permute-done.even_recv
  10.6 0.0 collective-permute-done.1.odd_recv
  10.6 2.0 %edge_force.1 = (f32[4,32,80,128]{3,2,1,0:T(8,128)S(1)}, f32[3,32,80,128]{3,2,1,0:T(8,128)S(1)}, f32[3,4,4096]{2,1,0:T(4,128)S(1)}, f32[3,4,4096]{2,1,0:T(4,128)S(1)}) custom-call(s32[1,4]{1,0:T(1,128)S(1)} %copy-done.2, s32[4]{0:T(128)S(1)} %copy-done.3, ...), custom_call_target="tpu_custom_call", output_to_operand_aliasing={{0}: (7, {}), {1}: (8, {})} | custom-call | flops 100000000 | bytes 8388608 | tf_op jit(solution)/shard_map/edge_force/pallas_call | solution.py:336
  12.6 4.3 %collective-permute-start.3 = (f32[3,4,4096]{2,1,0:T(4,128)S(1)}, f32[3,4,4096]{2,1,0:T(4,128)S(1)}, u32[]{:S(2)}, u32[]{:S(2)}) collective-permute-start(f32[3,4,4096]{2,1,0:T(4,128)S(1)} %get-tuple-element.15), channel_id=1, source_target_pairs={{0,1},{1,0},{2,3},{3,2},{4,5},{5,4},{6,7},{7,6},{8,9},{9,8},{10,11... | collective-permute-start | bytes 589832 | tf_op jit(solution)/shard_map/ppermute | solution.py:348
  17.0 0.8 %collective-permute-start.4 = (f32[3,4,4096]{2,1,0:T(4,128)S(1)}, f32[3,4,4096]{2,1,0:T(4,128)S(1)}, u32[]{:S(2)}, u32[]{:S(2)}) collective-permute-start(f32[3,4,4096]{2,1,0:T(4,128)S(1)} %get-tuple-element.16), channel_id=1, source_target_pairs={{1,2},{2,1},{3,4},{4,3},{5,6},{6,5},{9,10},{10,9},{11,12},{12,11},... | collective-permute-start | bytes 589832 | tf_op jit(solution)/shard_map/ppermute | solution.py:349
  17.8 4.5 %sweeps.1.before = f32[3,64,4096]{2,1,0:T(8,128)S(1)} custom-call(f32[3,32,80,128]{3,2,1,0:T(8,128)S(1)} %get-tuple-element.14.u_ref), custom_call_target="tpu_custom_call" | custom-call | flops 1000000000 | bytes 41943040 | tf_op jit(solution)/shard_map/sweeps/pallas_call | solution.py:351
  22.3 3.2 %collective-permute-done.3.even_recv = f32[3,4,4096]{2,1,0:T(4,128)S(1)} collective-permute-done((f32[3,4,4096]{2,1,0:T(4,128)S(1)}, f32[3,4,4096]{2,1,0:T(4,128)S(1)}, u32[]{:S(2)}, u32[]{:S(2)}) %collective-permute-start.3) | collective-permute-done | bytes 196640 | tf_op jit(solution)/shard_map/ppermute | solution.py:348
  25.4 0.0 collective-permute-done.4.odd_recv
  25.5 2.6 %seam_sweeps.1 = f32[1,3,64,4096]{3,2,1,0:T(8,128)} custom-call(f32[3,32,80,128]{3,2,1,0:T(8,128)S(1)} %get-tuple-element.14.u_ref, f32[3,4,4096]{2,1,0:T(4,128)S(1)} %collective-permute-done.3.even_recv, f32[3,4,4096]{2,1,0:T(4,128)S(1)} %collective-permute-done.4.odd_recv, f32[3,64,4096]{2,1,0:T(8,128)S(1)} %sweeps.1.before), custom_call_target="tpu_custom_call" | custom-call | tf_op jit(solution)/shard_map/seam_sweeps/pallas_call | solution.py:366
Async XLA Ops:
  0.0 6.1 %collective-permute-start.2 = (bf16[1,4,64,4096]{3,2,1,0:T(8,128)(2,1)}, bf16[1,4,64,4096]{3,2,1,0:T(8,128)(2,1)S(1)}, u32[]{:S(2)}, u32[]{:S(2)}) collective-permute-start(bf16[1,4,64,4096]{3,2,1,0:T(8,128)(2,1)} %param.5), channel_id=1, source_target_pairs={{0,8},{8,0},{1,9},{9,1},{2,10},{10,2},{3,11},{11,3},{4,12},{12,4},... | collective-permute-start | bytes 6291464 | tf_op jit(solution)/shard_map/ppermute | solution.py:291
  0.5 5.7 %copy-start = (f32[1,3,64,4096]{3,2,1,0:T(8,128)S(1)}, f32[1,3,64,4096]{3,2,1,0:T(8,128)}, u32[]{:S(2)}) copy-start(f32[1,3,64,4096]{3,2,1,0:T(8,128)} %moved.3) | copy-start | bytes 9437188
  0.5 5.7 %copy-start.1 = (bf16[1,4,64,4096]{3,2,1,0:T(8,128)(2,1)S(1)}, bf16[1,4,64,4096]{3,2,1,0:T(8,128)(2,1)}, u32[]{:S(2)}) copy-start(bf16[1,4,64,4096]{3,2,1,0:T(8,128)(2,1)} %param.5) | copy-start | bytes 6291460
  0.5 5.7 %copy-start.2 = (s32[1,4]{1,0:T(1,128)S(1)}, s32[1,4]{1,0:T(1,128)}, u32[]{:S(2)}) copy-start(s32[1,4]{1,0:T(1,128)} %order_hbm.3) | copy-start | bytes 52
  0.5 5.7 %copy-start.3 = (s32[4]{0:T(128)S(1)}, s32[4]{0:T(128)}, u32[]{:S(2)}) copy-start(s32[4]{0:T(128)} %owner_hbm.3) | copy-start | bytes 52
  2.9 7.7 %collective-permute-start = (f32[4,4096]{1,0:T(4,128)S(1)}, f32[4,4096]{1,0:T(4,128)S(1)}, u32[]{:S(2)}, u32[]{:S(2)}) collective-permute-start(f32[4,4096]{1,0:T(4,128)S(1)} %get-tuple-element.11), channel_id=1, source_target_pairs={{0,1},{1,0},{2,3},{3,2},{4,5},{5,4},{6,7},{7,6},{8,9},{9,8},{10,11... | collective-permute-start | bytes 196616 | tf_op jit(solution)/shard_map/ppermute | solution.py:320
  5.5 5.1 %collective-permute-start.1 = (f32[4,4096]{1,0:T(4,128)S(1)}, f32[4,4096]{1,0:T(4,128)S(1)}, u32[]{:S(2)}, u32[]{:S(2)}) collective-permute-start(f32[4,4096]{1,0:T(4,128)S(1)} %get-tuple-element.12), channel_id=1, source_target_pairs={{1,2},{2,1},{3,4},{4,3},{5,6},{6,5},{9,10},{10,9},{11,12},{12,11},... | collective-permute-start | bytes 196616 | tf_op jit(solution)/shard_map/ppermute | solution.py:321
  12.6 12.8 %collective-permute-start.3 = (f32[3,4,4096]{2,1,0:T(4,128)S(1)}, f32[3,4,4096]{2,1,0:T(4,128)S(1)}, u32[]{:S(2)}, u32[]{:S(2)}) collective-permute-start(f32[3,4,4096]{2,1,0:T(4,128)S(1)} %get-tuple-element.15), channel_id=1, source_target_pairs={{0,1},{1,0},{2,3},{3,2},{4,5},{5,4},{6,7},{7,6},{8,9},{9,8},{10,11... | collective-permute-start | bytes 589832 | tf_op jit(solution)/shard_map/ppermute | solution.py:348
  17.0 8.5 %collective-permute-start.4 = (f32[3,4,4096]{2,1,0:T(4,128)S(1)}, f32[3,4,4096]{2,1,0:T(4,128)S(1)}, u32[]{:S(2)}, u32[]{:S(2)}) collective-permute-start(f32[3,4,4096]{2,1,0:T(4,128)S(1)} %get-tuple-element.16), channel_id=1, source_target_pairs={{1,2},{2,1},{3,4},{4,3},{5,6},{6,5},{9,10},{10,9},{11,12},{12,11},... | collective-permute-start | bytes 589832 | tf_op jit(solution)/shard_map/ppermute | solution.py:349

commit v6 on v5

--- a/solution.py
+++ b/solution.py
@@ -175,7 +175,7 @@
 
 
 def edge_kernel(depth, order_hbm, owner_hbm, even_recv, odd_recv, own, recv, moved, s_in, u_in, s_ref, u_ref, even_send,
-                odd_send, order, owner, r_ref, y_ref, o_sem):
+                odd_send, order, owner, r_ref, y_ref, o_sem, t_ref):
     stains, tiles = s_ref.shape[:2]
     copies = [
         pltpu.make_async_copy(order_hbm, order, o_sem.at[0]),
@@ -185,6 +185,7 @@
         copy.start()
     even = (lax.axis_index("depth") % 2) == 0
     clear_rim(r_ref, 0)
+    t_ref[...] = jnp.zeros(t_ref.shape, F32)
     matrix = lateral_matrix(True)
     for c in range(tiles):
         at = slice(c * LANES, (c + 1) * LANES)
@@ -201,12 +202,15 @@
         regions = ((8, 0, 8, 8), (depth, depth - 8, depth, 8))
         force_stain(s_ref, k, mine, regions, own, recv, moved if j == 0 else None, u_ref, r_ref, y_ref, matrix)
     n = SWEEPS
-    for q in range(3):
+    for send, up in ((even_send, even), (odd_send, jnp.logical_not(even))):
         for c in range(tiles):
             at = slice(c * LANES, (c + 1) * LANES)
-            low, high = u_ref[q, c, 8 : 8 + n, :], u_ref[q, c, 8 + depth - n : 8 + depth, :]
-            even_send[q, :, at] = jnp.where(even, high, low)
-            odd_send[q, :, at] = jnp.where(even, low, high)
+            for q in range(3):
+                low, high = u_ref[q, c, 8 : 8 + n, :], u_ref[q, c, 8 + depth - n : 8 + depth, :]
+                t_ref[n * q : n * q + n, at] = jnp.where(up, high, low)
+                near = jnp.where(up, u_ref[q, c, 7 + depth : 8 + depth, :], u_ref[q, c, 8:9, :])
+                t_ref[3 * n + q : 3 * n + q + 1, at] = near - near.astype(BF16).astype(F32)
+            send[:, at] = t_ref[:, at].astype(BF16)
 
 
 def sweep_kernel(depth, u_ref, o_ref, a_ref, b_ref, r_ref):
@@ -227,7 +231,7 @@
         src, dst = dst, (b_ref if dst is a_ref else a_ref)
 
 
-def seam_kernel(depth, u_ref, even_recv, odd_recv, before, out, a_ref, b_ref, r_ref, o_ref, sem):
+def seam_kernel(depth, u_ref, even_recv, odd_recv, before, out, a_ref, b_ref, r_ref, o_ref, sem, h_ref):
     tiles = u_ref.shape[1]
     at_depth = lax.axis_index("depth")
     even = (at_depth % 2) == 0
@@ -248,11 +252,17 @@
     for q in range(3):
         a_ref[q, :, 8:16, :] = u_ref[q, :, depth : depth + 8, :]
         a_ref[q, :, 24:32, :] = u_ref[q, :, 8:16, :]
-        for c in range(tiles):
-            at = slice(c * LANES, (c + 1) * LANES)
-            x, y = even_recv[q, :, at], odd_recv[q, :, at]
-            a_ref[q, c, 16 : 16 + n, :] = jnp.where(even, x, y)
-            a_ref[q, c, 20 : 20 + n, :] = jnp.where(even, y, x)
+    for c in range(tiles):
+        at = slice(c * LANES, (c + 1) * LANES)
+        x, y = even_recv[:, at].astype(F32), odd_recv[:, at].astype(F32)
+        h_ref[0, :, at] = jnp.where(even, x, y)
+        h_ref[1, :, at] = jnp.where(even, y, x)
+        for q in range(3):
+            rest = slice(3 * n + q, 3 * n + q + 1)
+            a_ref[q, c, 16 : 16 + n, :] = h_ref[0, n * q : n * q + n, at]
+            a_ref[q, c, 20 : 20 + n, :] = h_ref[1, n * q : n * q + n, at]
+            a_ref[q, c, 16:17, :] = h_ref[0, n * q : n * q + 1, at] + h_ref[0, rest, at]
+            a_ref[q, c, 23:24, :] = h_ref[1, n * q + n - 1 : n * q + n, at] + h_ref[1, rest, at]
     row = lax.broadcasted_iota(jnp.int32, (8, LANES), 0)
     keep = jnp.where(row < n, jnp.where(has_high, 1.0, 0.0), jnp.where(has_low, 1.0, 0.0))
     top = lax.broadcasted_iota(jnp.int32, (8, LANES), 0) < 4
@@ -300,7 +310,7 @@
     tall = depth // 8
     s_type = pltpu.VMEM((stains, tiles, depth + 16, LANES), F32)
     u_type = pltpu.VMEM((3, tiles, depth + 16, LANES), F32)
-    send_type = pltpu.VMEM((3, SWEEPS, cells), F32)
+    send_type = pltpu.VMEM((16, cells), BF16)
 
     def force_scratch(planes):
         return [pltpu.VMEM((tiles + 2, planes, LANES), F32), pltpu.VMEM((tiles, planes, LANES), F32)]
@@ -338,7 +348,7 @@
         out_shape=(s_type, u_type, send_type, send_type),
         in_specs=[HBM, HBM] + [VMEM] * 7,
         out_specs=(VMEM, VMEM, VMEM, VMEM),
-        scratch_shapes=scalars + force_scratch(16) + [dma((2,))],
+        scratch_shapes=scalars + force_scratch(16) + [dma((2,)), pltpu.VMEM((16, cells), F32)],
         input_output_aliases={7: 0, 8: 1},
         compiler_params=params(20),
         cost_estimate=pl.CostEstimate(flops=10**8, bytes_accessed=8 << 20, transcendentals=0),
@@ -374,6 +384,7 @@
             pltpu.VMEM((3, tiles + 2, 24, LANES), F32),
             pltpu.VMEM((2, 3, 8, cells), F32),
             dma((9,)),
+            pltpu.VMEM((2, 16, cells), F32),
         ],
         compiler_params=params(LIMIT),
         name="seam_sweeps",

time: 28.4 us -> 27 us (0.951)
  the two profiles are of different devices: /device:TPU:0 before, /device:TPU:12 now
where the time goes in v6:
time: 27 us; the launch traced here: 26.8 us
  Pallas kernels  16.3 us (60%)
  starting transfers between devices  10.2 us (38%)
  between operations  0.31 us (1%)
    ppermute x1, starting transfers between devices, local(): u_odd = lax.ppermute(odd_send, 'depth', odd_pairs)  5.1 us
    pallas_call x1, Pallas kernels, local(): pl.pallas_call(functools.partial(sweep_kernel, depth), out_shape=pltpu.VM...  4.45 us
    ppermute x1, starting transfers between devices, local(): odd_recv = lax.ppermute(odd_send, 'depth', odd_pairs)  4.43 us
    pallas_call x1, Pallas kernels, local(): pl.pallas_call(functools.partial(inner_kernel, depth), out_shape=u_type,...  4.41 us
    pallas_call x1, Pallas kernels, local(): pl.pallas_call(functools.partial(seam_kernel, depth), out_shape=sds(displ...  2.77 us
    pallas_call x1, Pallas kernels, local(): pl.pallas_call(functools.partial(load_kernel, depth), out_shape=(s_type,...  2.38 us
    pallas_call x1, Pallas kernels, local(): pl.pallas_call(functools.partial(edge_kernel, depth), out_shape=(s_type,...  2.31 us
    ppermute x1, starting transfers between devices, local(): even_recv = lax.ppermute(even_send, 'depth', even_pairs)  0.57 us
  transfers between devices with their start and end apart: 5, of which 0 were waited for; matrix products, arithmetic and copies ran while one was open for 0% of the time, Pallas kernels for 42%

profile of v6, /device:TPU:12, one launch (start us, length us, event | category | flops | bytes accessed | tf_op | source)
XLA Modules:
  0.0 26.8 jit_solution(3594557809930712189)
XLA Ops:
  0.0 0.0 collective-permute-start.2
  0.0 0.0 copy-start
  0.0 0.0 copy-start.1
  0.0 0.0 copy-start.2
  0.0 0.0 copy-start.3
  0.0 2.4 %load.1 = (f32[4,32,80,128]{3,2,1,0:T(8,128)S(1)}, f32[4,4096]{1,0:T(4,128)S(1)}, f32[4,4096]{1,0:T(4,128)S(1)}) custom-call(f32[4,8,32,8,128]{4,3,2,1,0:T(8,128)} %bitcast.6), custom_call_target="tpu_custom_call" | custom-call | flops 4000000000 | bytes 25165824 | tf_op jit(solution)/shard_map/load/pallas_call | solution.py:319
  2.4 0.6 %collective-permute-start = (f32[4,4096]{1,0:T(4,128)S(1)}, f32[4,4096]{1,0:T(4,128)S(1)}, u32[]{:S(2)}, u32[]{:S(2)}) collective-permute-start(f32[4,4096]{1,0:T(4,128)S(1)} %get-tuple-element.11), channel_id=1, source_target_pairs={{0,1},{1,0},{2,3},{3,2},{4,5},{5,4},{6,7},{7,6},{8,9},{9,8},{10,11... | collective-permute-start | bytes 196616 | tf_op jit(solution)/shard_map/ppermute | solution.py:330
  3.0 4.4 %collective-permute-start.1 = (f32[4,4096]{1,0:T(4,128)S(1)}, f32[4,4096]{1,0:T(4,128)S(1)}, u32[]{:S(2)}, u32[]{:S(2)}) collective-permute-start(f32[4,4096]{1,0:T(4,128)S(1)} %get-tuple-element.12), channel_id=1, source_target_pairs={{1,2},{2,1},{3,4},{4,3},{5,6},{6,5},{9,10},{10,9},{11,12},{12,11},... | collective-permute-start | bytes 196616 | tf_op jit(solution)/shard_map/ppermute | solution.py:331
  7.4 0.0 collective-permute-done.2.recv
  7.4 0.0 copy-done
  7.4 0.0 copy-done.1
  7.5 0.0 copy-done.2
  7.5 0.0 copy-done.3
  7.5 4.4 %inner_force.1.u_in = f32[3,32,80,128]{3,2,1,0:T(8,128)S(1)} custom-call(s32[1,4]{1,0:T(1,128)S(1)} %copy-done.2, s32[4]{0:T(128)S(1)} %copy-done.3, f32[4,32,80,128]{3,2,1,0:T(8,128)S(1)} %get-tuple-element.13.s_ref.s_in, f32[1,3,64,4096]{3,2,1,0:T(8,128)S(1)} %copy-done, bf16[4,64,4096]{2,1,0:T(8,128)(2,1)S(1)} %bitcast.4, ...), custom_call_target="tpu_custom_call" | custom-call | flops 400000000 | bytes 10485760 | tf_op jit(solution)/shard_map/inner_force/pallas_call | solution.py:335
  11.9 0.0 collective-permute-done.even_recv
  11.9 0.0 collective-permute-done.1.odd_recv
  11.9 2.3 %edge_force.1 = (f32[4,32,80,128]{3,2,1,0:T(8,128)S(1)}, f32[3,32,80,128]{3,2,1,0:T(8,128)S(1)}, bf16[16,4096]{1,0:T(8,128)(2,1)S(1)}, bf16[16,4096]{1,0:T(8,128)(2,1)S(1)}) custom-call(s32[1,4]{1,0:T(1,128)S(1)} %copy-done.2, s32[4]{0:T(128)S(1)} %copy-done.3, ...), custom_call_target="tpu_custom_call", output_to_operand_aliasing={{0}: (7, {}), {1}: (8, {})} | custom-call | flops 100000000 | bytes 8388608 | tf_op jit(solution)/shard_map/edge_force/pallas_call | solution.py:346
  14.2 0.1 collective-permute-start.3
  14.3 5.1 %collective-permute-start.4 = (bf16[16,4096]{1,0:T(8,128)(2,1)S(1)}, bf16[16,4096]{1,0:T(8,128)(2,1)S(1)}, u32[]{:S(2)}, u32[]{:S(2)}) collective-permute-start(bf16[16,4096]{1,0:T(8,128)(2,1)S(1)} %get-tuple-element.16), channel_id=1, source_target_pairs={{1,2},{2,1},{3,4},{4,3},{5,6},{6,5},{9,10},{10,9},{11,12},{12,11},... | collective-permute-start | bytes 393224 | tf_op jit(solution)/shard_map/ppermute | solution.py:359
  19.4 4.5 %sweeps.1.before = f32[3,64,4096]{2,1,0:T(8,128)S(1)} custom-call(f32[3,32,80,128]{3,2,1,0:T(8,128)S(1)} %get-tuple-element.14.u_ref), custom_call_target="tpu_custom_call" | custom-call | flops 1000000000 | bytes 41943040 | tf_op jit(solution)/shard_map/sweeps/pallas_call | solution.py:361
  23.9 0.0 collective-permute-done.3.even_recv
  23.9 0.0 collective-permute-done.4.odd_recv
  23.9 2.8 %seam_sweeps.1 = f32[1,3,64,4096]{3,2,1,0:T(8,128)} custom-call(f32[3,32,80,128]{3,2,1,0:T(8,128)S(1)} %get-tuple-element.14.u_ref, bf16[16,4096]{1,0:T(8,128)(2,1)S(1)} %collective-permute-done.3.even_recv, bf16[16,4096]{1,0:T(8,128)(2,1)S(1)} %collective-permute-done.4.odd_recv, f32[3,64,4096]{2,1,0:T(8,128)S(1)} %sweeps.1.before), custom_call_target="tpu_custom_call" | custom-call | tf_op jit(solution)/shard_map/seam_sweeps/pallas_call | solution.py:376
Async XLA Ops:
  0.0 7.4 %collective-permute-start.2 = (bf16[1,4,64,4096]{3,2,1,0:T(8,128)(2,1)}, bf16[1,4,64,4096]{3,2,1,0:T(8,128)(2,1)S(1)}, u32[]{:S(2)}, u32[]{:S(2)}) collective-permute-start(bf16[1,4,64,4096]{3,2,1,0:T(8,128)(2,1)} %param.5), channel_id=1, source_target_pairs={{0,8},{8,0},{1,9},{9,1},{2,10},{10,2},{3,11},{11,3},{4,12},{12,4},... | collective-permute-start | bytes 6291464 | tf_op jit(solution)/shard_map/ppermute | solution.py:301
  0.0 7.4 %copy-start = (f32[1,3,64,4096]{3,2,1,0:T(8,128)S(1)}, f32[1,3,64,4096]{3,2,1,0:T(8,128)}, u32[]{:S(2)}) copy-start(f32[1,3,64,4096]{3,2,1,0:T(8,128)} %moved.3) | copy-start | bytes 9437188
  0.0 7.4 %copy-start.1 = (bf16[1,4,64,4096]{3,2,1,0:T(8,128)(2,1)S(1)}, bf16[1,4,64,4096]{3,2,1,0:T(8,128)(2,1)}, u32[]{:S(2)}) copy-start(bf16[1,4,64,4096]{3,2,1,0:T(8,128)(2,1)} %param.5) | copy-start | bytes 6291460
  0.0 7.4 %copy-start.2 = (s32[1,4]{1,0:T(1,128)S(1)}, s32[1,4]{1,0:T(1,128)}, u32[]{:S(2)}) copy-start(s32[1,4]{1,0:T(1,128)} %order_hbm.3) | copy-start | bytes 52
  0.0 7.4 %copy-start.3 = (s32[4]{0:T(128)S(1)}, s32[4]{0:T(128)}, u32[]{:S(2)}) copy-start(s32[4]{0:T(128)} %owner_hbm.3) | copy-start | bytes 52
  2.4 9.5 %collective-permute-start = (f32[4,4096]{1,0:T(4,128)S(1)}, f32[4,4096]{1,0:T(4,128)S(1)}, u32[]{:S(2)}, u32[]{:S(2)}) collective-permute-start(f32[4,4096]{1,0:T(4,128)S(1)} %get-tuple-element.11), channel_id=1, source_target_pairs={{0,1},{1,0},{2,3},{3,2},{4,5},{5,4},{6,7},{7,6},{8,9},{9,8},{10,11... | collective-permute-start | bytes 196616 | tf_op jit(solution)/shard_map/ppermute | solution.py:330
  3.0 8.9 %collective-permute-start.1 = (f32[4,4096]{1,0:T(4,128)S(1)}, f32[4,4096]{1,0:T(4,128)S(1)}, u32[]{:S(2)}, u32[]{:S(2)}) collective-permute-start(f32[4,4096]{1,0:T(4,128)S(1)} %get-tuple-element.12), channel_id=1, source_target_pairs={{1,2},{2,1},{3,4},{4,3},{5,6},{6,5},{9,10},{10,9},{11,12},{12,11},... | collective-permute-start | bytes 196616 | tf_op jit(solution)/shard_map/ppermute | solution.py:331
  14.2 9.7 %collective-permute-start.3 = (bf16[16,4096]{1,0:T(8,128)(2,1)S(1)}, bf16[16,4096]{1,0:T(8,128)(2,1)S(1)}, u32[]{:S(2)}, u32[]{:S(2)}) collective-permute-start(bf16[16,4096]{1,0:T(8,128)(2,1)S(1)} %get-tuple-element.15), channel_id=1, source_target_pairs={{0,1},{1,0},{2,3},{3,2},{4,5},{5,4},{6,7},{7,6},{8,9},{9,8},{10,11... | collective-permute-start | bytes 393224 | tf_op jit(solution)/shard_map/ppermute | solution.py:358
  14.3 9.6 %collective-permute-start.4 = (bf16[16,4096]{1,0:T(8,128)(2,1)S(1)}, bf16[16,4096]{1,0:T(8,128)(2,1)S(1)}, u32[]{:S(2)}, u32[]{:S(2)}) collective-permute-start(bf16[16,4096]{1,0:T(8,128)(2,1)S(1)} %get-tuple-element.16), channel_id=1, source_target_pairs={{1,2},{2,1},{3,4},{4,3},{5,6},{6,5},{9,10},{10,9},{11,12},{12,11},... | collective-permute-start | bytes 393224 | tf_op jit(solution)/shard_map/ppermute | solution.py:359
